TPU v7x, 32 devices: a whole 2x2x4 slice. The times are simulated.
32 devices in a mesh: slab: 8 (over y, x, core), brick: 4 (over z).
Axes of the slice: x: 2, y: 2, z: 4, core: 2. Of those that a mesh axis runs over, the one named last changes fastest.
Arguments:
- velocity: float32 [3, 16, 32, 257], P(None, 'slab', 'brick'), may hold values from -6 to 6
- energy: float32 [8, 8, 16, 128], P(None, 'slab', 'brick'), may hold values from 0.5 to 2
- density: float32 [8, 8, 16, 128], P(None, 'slab', 'brick'), may hold values from 0.5 to 18, as said below
- material: int32 [8, 16, 128], P('slab', 'brick'), may hold values from 0 to 1
- geometry: bfloat16 [81, 8, 8, 16, 128], P(None, None, 'slab', 'brick'), may hold values from -2 to 2
- mass_weight: float32 [27, 8, 16, 128], P(None, 'slab', 'brick'), may hold values from 2 to 8
- energy_mass: float32 [8, 8, 16, 128], P(None, 'slab', 'brick'), may hold values from 0.5 to 2
Outputs:
- velocity_half: float32 [3, 16, 32, 257], P(None, 'slab', 'brick')
- energy_half: float32 [8, 8, 16, 128], P(None, 'slab', 'brick')
Inputs may be any that keep to these rules, and one draw needn't show every extreme that they name: `density`: densities at the thermodynamic degrees of freedom, positive.
All inputs are finite; a program needn't handle non-finite values.
Results may differ from a plain program's by a relative error of at most 0.005.
Values may be sent and summed in bfloat16 or wider, within the bound.
No kernel may reach another device: no remote copies, remote signals or barrier semaphores. Data moves between devices by JAX's collectives and lax.ppermute only.
A program may use at most 64 MiB of HBM per device.

v0:
```python
import jax
import jax.numpy as jnp
import numpy as np
from jax import lax
from jax.experimental import pallas as pl
from jax.experimental.pallas import tpu as pltpu
from jax.sharding import PartitionSpec as P

HALF_STEP = 0.25
GRAVITY = 1.0
F32 = jnp.float32
BF16 = jnp.bfloat16

OFFSET = float(np.sqrt(0.6) / 2.0)
SIDE = 0.3
MIDDLE = 0.4
LINE_WEIGHTS = (5.0 / 18.0, 8.0 / 18.0, 5.0 / 18.0)
POINT_WEIGHT = [a * b * c for a in LINE_WEIGHTS for b in LINE_WEIGHTS for c in LINE_WEIGHTS]
OWN = 4
HALO = 2


def lines(direction):
    stride = (9, 3, 1)[direction]
    return [(n, n + stride, n + 2 * stride) for n in range(27) if (n // stride) % 3 == 0]


def to_points(values):
    values = list(values)
    for direction in range(3):
        for i, j, k in lines(direction):
            even = SIDE * (values[i] + values[k]) + MIDDLE * values[j]
            odd = OFFSET * (values[i] - values[k])
            values[i], values[k] = even + odd, even - odd
    return values


def from_points(values):
    values = list(values)
    for direction in range(3):
        for i, j, k in lines(direction):
            total = values[i] + values[k]
            odd = OFFSET * (values[i] - values[k])
            even = SIDE * total
            values[i], values[k] = even + odd, even - odd
            values[j] = values[j] + MIDDLE * total
    return values


def lane_of(shape):
    return lax.broadcasted_iota(jnp.int32, shape, len(shape) - 1)


def assemble_z(values, wall):
    values = list(values)
    lane = lane_of(values[0].shape)
    first, last = lane == 0, lane == 127
    for i, _, k in lines(2):
        total = values[i] + jnp.where(first, 0.0, pltpu.roll(values[k], 1, 1))
        top = values[k]
        if wall:
            total = jnp.where(first, 0.0, total)
            top = jnp.zeros_like(top)
        values[i] = total
        values[k] = jnp.where(last, top, pltpu.roll(total, 127, 1))
    return values


def assemble_y(values):
    values = list(values)
    for i, _, k in lines(1):
        values[i] = values[i] + pltpu.roll(values[k], 1, 0)
        values[k] = pltpu.roll(values[i], 7, 0)
    return values


def force_kernel(geometry, density, energy, material, mass_weight, field, to_left, to_right):
    gamma = jnp.where(material[...] == 0, 2.0 / 3.0, 0.4).astype(F32)
    pressure = (gamma[None] * density[...] * energy[...]).astype(BF16).astype(F32)
    gravity = from_points([mass_weight[q] * POINT_WEIGHT[q] for q in range(27)])
    for comp in range(3):
        for n in range(27):
            r = 27 * comp + n
            block = geometry[pl.ds(8 * r, 8)].astype(F32)
            value = -jnp.sum(block * pressure, axis=0)
            if comp == 2:
                value = value - GRAVITY * gravity[n]
            field[r] = value
            if n // 9 == 0:
                to_left[9 * comp + n] = value
            if n // 9 == 2:
                to_right[9 * comp + n - 18] = value


def spread_kernel(velocity, out):
    rows = velocity[...].astype(BF16).reshape(48, velocity.shape[3])
    low = rows[:, :256]
    high = rows[:, 256:257].astype(F32)
    node = lax.broadcasted_iota(jnp.int32, (256, 384), 0)
    lane = lax.broadcasted_iota(jnp.int32, (256, 384), 1)
    pick = (node == 2 * (lane % 128) + lane // 128).astype(F32).astype(BF16)
    spread = jnp.dot(low, pick, preferred_element_type=F32)
    top = jnp.where(lane_of((48, 128)) == 127, high, 0.0)
    spread = jnp.concatenate([spread[:, :256], spread[:, 256:] + top], axis=1)
    row = lax.broadcasted_iota(jnp.int32, (96, 48), 0)
    source = lax.broadcasted_iota(jnp.int32, (96, 48), 1)
    wanted = (row // 16) * 8 + 2 * (row % 8) + (row // 8) % 2
    move = ((source == wanted) & (row % 8 < OWN)).astype(F32).astype(BF16)
    moved = jnp.dot(move, spread.astype(BF16), preferred_element_type=F32)
    for group in range(12):
        for c in range(3):
            out[3 * group + c] = moved[8 * group : 8 * group + 8, 128 * c : 128 * c + 128]


def rim_kernel(field, from_left, from_right, mass_weight, spread, out, to_low, to_high):
    for comp in range(3):
        for n in range(27):
            r = 27 * comp + n
            value = field[r]
            if n // 9 == 0:
                value = value + from_left[9 * comp + n]
            if n // 9 == 2:
                value = value + from_right[9 * comp + n - 18]
            out[r] = value
            to_low[r] = value[:HALO]
            to_high[r] = value[OWN - HALO :]
    for q in range(27):
        to_low[81 + q] = mass_weight[q, :HALO]
        to_high[81 + q] = mass_weight[q, OWN - HALO :]
    for comp in range(3):
        for a in range(2):
            for c in range(3):
                to_low[108 + 6 * comp + 3 * a + c] = spread[12 * comp + 6 * a + c, :HALO]


def send_planes(values, comp, to_left, to_right):
    slot = 0
    for b in range(2):
        for c in range(3):
            to_left[6 * comp + slot] = values[3 * b + c]
            to_right[6 * comp + slot] = values[18 + 3 * b + c]
            slot += 1


def apply_mass(values, weight, wall):
    points = to_points(values)
    points = [points[q] * weight[q] for q in range(27)]
    return assemble_y(assemble_z(from_points(points), wall))


def first_kernel(
    own, from_low, from_high, mass_weight, spread, field, weight, image, to_left, to_right, speeds, rows
):
    for q in range(27):
        rows[q, :HALO] = from_low[81 + q]
        rows[q, HALO : HALO + OWN] = mass_weight[q]
        rows[q, HALO + OWN :] = from_high[81 + q]
    for q in range(27):
        weight[q] = rows[q] * POINT_WEIGHT[q]
    for r in range(81):
        rows[r, :HALO] = from_low[r]
        rows[r, HALO : HALO + OWN] = own[r]
        rows[r, HALO + OWN :] = from_high[r]
    for comp in range(3):
        values = [rows[27 * comp + n] for n in range(27)]
        values = assemble_y(assemble_z(values, comp == 2))
        for n in range(27):
            field[27 * comp + n] = values[n]
        values = apply_mass(values, weight, comp == 2)
        for n in range(27):
            image[27 * comp + n] = values[n]
        send_planes(values, comp, to_left, to_right)
    row = lax.broadcasted_iota(jnp.int32, (8, 128), 0)
    for comp in range(3):
        for a in range(2):
            for c in range(3):
                for b in range(2):
                    value = spread[12 * comp + 6 * a + 3 * b + c]
                    speeds[18 * comp + 9 * a + 3 * b + c] = value
                    if a == 0:
                        to_left[18 + 9 * comp + 3 * b + c] = value
                beyond = from_high[108 + 6 * comp + 3 * a + c, 0:1]
                value = spread[12 * comp + 6 * a + c]
                value = jnp.where(row == OWN - 1, beyond, pltpu.roll(value, 7, 0))
                speeds[18 * comp + 9 * a + 6 + c] = value
                if a == 0:
                    to_left[18 + 9 * comp + 6 + c] = value


def take_planes(image, from_left, from_right, comp):
    values = [image[27 * comp + n] for n in range(27)]
    slot = 0
    for b in range(2):
        for c in range(3):
            values[3 * b + c] = values[3 * b + c] + from_left[6 * comp + slot]
            values[18 + 3 * b + c] = values[18 + 3 * b + c] + from_right[6 * comp + slot]
            slot += 1
    for a in (0, 18):
        for c in range(3):
            values[a + 6 + c] = pltpu.roll(values[a + c], 7, 0)
    return values


def second_kernel(image, from_left, from_right, weight, field, image_out, to_left, to_right):
    for comp in range(3):
        values = take_planes(image, from_left, from_right, comp)
        for n in range(27):
            field[27 * comp + n] = values[n]
        values = apply_mass(values, weight, comp == 2)
        for n in range(27):
            image_out[27 * comp + n] = values[n]
        send_planes(values, comp, to_left, to_right)


def work_kernel(geometry, density, energy, material, energy_mass, speeds, from_right, out):
    gamma = jnp.where(material[...] == 0, 2.0 / 3.0, 0.4).astype(F32)
    pressure = (gamma[None] * density[...] * energy[...]).astype(BF16).astype(F32)
    work = jnp.zeros_like(pressure)
    for comp in range(3):
        for n in range(27):
            if n < 18:
                speed = speeds[18 * comp + n, :OWN]
            else:
                speed = from_right[18 + 9 * comp + n - 18, :OWN]
            work = work + geometry[pl.ds(8 * (27 * comp + n), 8)].astype(F32) * speed[None]
    out[...] = energy[...] + HALF_STEP * pressure * work / energy_mass[...]


def dot_owned(first, second, comp, total):
    last = lane_of((8, 128)) == 127
    for a in range(2):
        for b in range(2):
            n = 27 * comp + 9 * a + 3 * b
            total = total + first[n] * second[n] + first[n + 1] * second[n + 1]
            total = total + jnp.where(last, first[n + 2] * second[n + 2], 0.0)
    return total


def moment_kernel(image, from_left, from_right, weight, zeroth, first, second, moments):
    zero = jnp.zeros((8, 128), F32)
    energy_norm = zero
    for comp in range(3):
        values = take_planes(image, from_left, from_right, comp)
        for n in range(27):
            second[27 * comp + n] = values[n]
        points = to_points(values)
        for q in range(27):
            energy_norm = energy_norm + points[q] * points[q] * weight[q]
    pairs = [(zeroth, zeroth), (zeroth, first), (first, first), (first, second), (second, second)]
    totals = []
    for one, other in pairs:
        total = zero
        for comp in range(3):
            total = dot_owned(one, other, comp, total)
        totals.append(total)
    totals.append(energy_norm)
    row = lax.broadcasted_iota(jnp.int32, (8, 128), 0)
    lane = lane_of((1, 128))
    mine = (row >= HALO) & (row < HALO + OWN)
    line = jnp.zeros((1, 128), F32)
    for k, total in enumerate(totals):
        total = jnp.sum(jnp.where(mine, total, 0.0), axis=0, keepdims=True)
        line = jnp.where(lane == k, jnp.sum(total, axis=1, keepdims=True), line)
    moments[...] = jnp.broadcast_to(line, moments.shape)


def solve(moments):
    def ratio(top, pivot, scale):
        good = pivot > 1e-7 * scale
        return jnp.where(good, top / jnp.where(good, pivot, 1.0), 0.0)

    m = moments
    l10 = ratio(m[2], m[1], 0.0)
    l20 = ratio(m[3], m[1], 0.0)
    d1 = m[3] - l10 * m[2]
    e1 = m[4] - l20 * m[2]
    l21 = ratio(e1, d1, m[3])
    d2 = m[5] - l20 * m[3] - l21 * e1
    y1 = m[1] - l10 * m[0]
    y2 = m[2] - l20 * m[0] - l21 * y1
    c2 = ratio(y2, d2, m[5])
    c1 = ratio(y1, d1, m[3]) - l21 * c2
    c0 = ratio(m[0], m[1], 0.0) - l10 * c1 - l20 * c2
    return c0, c1, c2


def halves(x):
    high = x.astype(BF16)
    return high, (x - high.astype(F32)).astype(BF16)


def last_kernel(moments, zeroth, first, second, velocity, out):
    line = jnp.sum(moments[...], axis=0, keepdims=True)
    lane = lane_of((1, 128))
    mu = [jnp.sum(jnp.where(lane == k, line, 0.0), axis=1, keepdims=True) for k in range(6)]
    c0, c1, c2 = [HALF_STEP * c for c in solve(mu)]
    blocks = []
    for c in range(3):
        column = []
        for comp in range(3):
            for a in range(2):
                for b in range(2):
                    n = 27 * comp + 9 * a + 3 * b + c
                    column.append(c0 * zeroth[n] + c1 * first[n] + c2 * second[n])
        blocks.append(jnp.concatenate(column, axis=0))
    joined = jnp.concatenate(blocks, axis=1)
    row = lax.broadcasted_iota(jnp.int32, (48, 96), 0)
    source = lax.broadcasted_iota(jnp.int32, (48, 96), 1)
    wanted = (row // 8) * 16 + (row % 2) * 8 + HALO + (row % 8) // 2
    move = (source == wanted).astype(F32).astype(BF16)
    high, low = halves(joined)
    moved = jnp.dot(move, high, preferred_element_type=F32) + jnp.dot(move, low, preferred_element_type=F32)
    source = lax.broadcasted_iota(jnp.int32, (384, 384), 0)
    node = lax.broadcasted_iota(jnp.int32, (384, 384), 1)
    wanted = jnp.where(node < 256, (node % 2) * 128 + node // 2, 383)
    place = ((source == wanted) & (node <= 256)).astype(F32).astype(BF16)
    high, low = halves(moved)
    placed = jnp.dot(high, place, preferred_element_type=F32) + jnp.dot(low, place, preferred_element_type=F32)
    for comp in range(3):
        for x in range(2):
            start = 16 * comp + 8 * x
            out[comp, x] = velocity[comp, x] + placed[start : start + 8, : velocity.shape[3]]


VMEM = pl.BlockSpec(memory_space=pltpu.VMEM)


def call(kernel, outs, *args, scratch=(), flops=100000):
    shapes = [jax.ShapeDtypeStruct(shape, F32) for shape in outs]
    moved = sum(a.size * a.dtype.itemsize for a in args) + sum(4 * int(np.prod(s)) for s in outs)
    return pl.pallas_call(
        kernel,
        out_shape=shapes,
        in_specs=[VMEM] * len(args),
        out_specs=[VMEM] * len(outs),
        scratch_shapes=list(scratch),
        compiler_params=pltpu.CompilerParams(vmem_limit_bytes=32 * 1024 * 1024),
        cost_estimate=pl.CostEstimate(flops=flops, bytes_accessed=moved, transcendentals=0),
        name=kernel.__name__,
    )(*args)


def shift(x, axis, by):
    count = lax.axis_size(axis)
    return lax.ppermute(x, axis, [(i, (i + by) % count) for i in range(count)])


def local(velocity, energy, density, material, geometry, mass_weight, energy_mass):
    tile = (4, 128)
    geometry = geometry.reshape((648,) + tile)
    density = density.reshape((8,) + tile)
    energy = energy.reshape((8,) + tile)
    energy_mass = energy_mass.reshape((8,) + tile)
    mass_weight = mass_weight.reshape((27,) + tile)
    material = material.reshape(tile)
    full = (8, 128)
    pair = (2, 128)
    devices = lax.axis_size("slab") * lax.axis_size("brick")

    force, to_left, to_right = call(
        force_kernel, [(81,) + tile, (27,) + tile, (27,) + tile], geometry, density, energy, material, mass_weight
    )
    (spread,) = call(spread_kernel, [(36,) + full], velocity)
    from_right = shift(to_left, "slab", -1)
    from_left = shift(to_right, "slab", 1)
    own, to_low, to_high = call(
        rim_kernel,
        [(81,) + tile, (126,) + pair, (108,) + pair],
        force, from_left, from_right, mass_weight, spread,
    )
    from_high = shift(to_low, "brick", -1)
    from_low = shift(to_high, "brick", 1)
    zeroth, weight, image, to_left, to_right, speeds = call(
        first_kernel,
        [(81,) + full, (27,) + full, (81,) + full, (45,) + full, (18,) + full, (54,) + full],
        own, from_low, from_high, mass_weight, spread,
        scratch=[pltpu.VMEM((81,) + full, F32)],
    )
    from_right = shift(to_left, "slab", -1)
    from_left = shift(to_right, "slab", 1)
    first, image, to_left, to_right = call(
        second_kernel,
        [(81,) + full, (81,) + full, (18,) + full, (18,) + full],
        image, from_left, from_right, weight,
    )
    (energy_half,) = call(
        work_kernel, [(8,) + tile], geometry, density, energy, material, energy_mass, speeds, from_right
    )
    from_right = shift(to_left, "slab", -1)
    from_left = shift(to_right, "slab", 1)
    second, moments = call(
        moment_kernel, [(81,) + full, (devices, 128)], image, from_left, from_right, weight, zeroth, first
    )
    moments = lax.all_to_all(moments, ("slab", "brick"), 0, 0, tiled=True)
    (velocity_half,) = call(last_kernel, [velocity.shape], moments, zeroth, first, second, velocity)
    return (velocity_half, energy_half.reshape(8, 1, 4, 128))


def solution(mesh):
    nodes = P(None, "slab", "brick", None)
    return jax.shard_map(
        local,
        mesh=mesh,
        in_specs=(
            nodes,
            nodes,
            nodes,
            P("slab", "brick", None),
            P(None, None, "slab", "brick", None),
            nodes,
            nodes,
        ),
        out_specs=(nodes, nodes),
        check_vma=False,
    )
```

profile of v0, /device:TPU:0, one launch (start us, length us, event | category | flops | bytes accessed | tf_op | source)
XLA Modules:
  0.0 47.3 jit_solution(17656705693897455905)
XLA Ops:
  0.6 0.7 %copy-done.10 = s32[1,4,128]{2,1,0:T(4,128)S(1)} copy-done((s32[1,4,128]{2,1,0:T(4,128)S(1)}, s32[1,4,128]{2,1,0:T(4,128)}, u32[]{:S(2)}) %copy-start.10) | copy-done | bytes 2072
  1.3 1.1 %copy-done = bf16[81,8,1,4,128]{4,3,2,1,0:T(4,128)(2,1)S(1)} copy-done((bf16[81,8,1,4,128]{4,3,2,1,0:T(4,128)(2,1)S(1)}, bf16[81,8,1,4,128]{4,3,2,1,0:T(4,128)(2,1)}, u32[]{:S(2)}) %copy-start) | copy-done | bytes 663576
  2.4 0.8 %copy-done.2 = f32[27,1,4,128]{3,2,1,0:T(4,128)S(1)} copy-done((f32[27,1,4,128]{3,2,1,0:T(4,128)S(1)}, f32[27,1,4,128]{3,2,1,0:T(4,128)}, u32[]{:S(2)}) %copy-start.2) | copy-done | bytes 55320
  3.2 0.7 %copy-done.5 = f32[8,1,4,128]{3,2,1,0:T(4,128)S(1)} copy-done((f32[8,1,4,128]{3,2,1,0:T(4,128)S(1)}, f32[8,1,4,128]{3,2,1,0:T(4,128)}, u32[]{:S(2)}) %copy-start.5) | copy-done | bytes 16408
  3.9 0.7 %copy-done.7 = f32[8,1,4,128]{3,2,1,0:T(4,128)S(1)} copy-done((f32[8,1,4,128]{3,2,1,0:T(4,128)S(1)}, f32[8,1,4,128]{3,2,1,0:T(4,128)}, u32[]{:S(2)}) %copy-start.7) | copy-done | bytes 16408
  4.7 0.4 force_kernel.1
  5.0 0.5 %collective-permute-start = (f32[27,4,128]{2,1,0:T(4,128)S(1)}, f32[27,4,128]{2,1,0:T(4,128)S(1)}, u32[]{:S(2)}, u32[]{:S(2)}) collective-permute-start(f32[27,4,128]{2,1,0:T(4,128)S(1)} %get-tuple-element.21), channel_id=1, source_target_pairs={{0,4},{4,8},{8,12},{12,16},{16,20},{20,24},{24,28},{28,0},{1,5},{5... | collective-permute-start | bytes 165896 | tf_op jit(solution)/shard_map/ppermute | solution.py:345
  5.6 3.0 %collective-permute-start.1 = (f32[27,4,128]{2,1,0:T(4,128)S(1)}, f32[27,4,128]{2,1,0:T(4,128)S(1)}, u32[]{:S(2)}, u32[]{:S(2)}) collective-permute-start(f32[27,4,128]{2,1,0:T(4,128)S(1)} %get-tuple-element.22), channel_id=1, source_target_pairs={{0,28},{4,0},{8,4},{12,8},{16,12},{20,16},{24,20},{28,24},{1,29},{... | collective-permute-start | bytes 165896 | tf_op jit(solution)/shard_map/ppermute | solution.py:345
  8.5 0.3 spread_kernel.1.spread
  8.8 1.5 %collective-permute-done.from_left = f32[27,4,128]{2,1,0:T(4,128)S(1)} collective-permute-done((f32[27,4,128]{2,1,0:T(4,128)S(1)}, f32[27,4,128]{2,1,0:T(4,128)S(1)}, u32[]{:S(2)}, u32[]{:S(2)}) %collective-permute-start) | collective-permute-done | bytes 55328 | tf_op jit(solution)/shard_map/ppermute | solution.py:345
  10.3 0.0 collective-permute-done.1.from_right
  10.3 0.1 rim_kernel.1
  10.4 4.4 %collective-permute-start.3 = (f32[126,2,128]{2,1,0:T(2,128)S(1)}, f32[126,2,128]{2,1,0:T(2,128)S(1)}, u32[]{:S(2)}, u32[]{:S(2)}) collective-permute-start(f32[126,2,128]{2,1,0:T(2,128)S(1)} %get-tuple-element.25), channel_id=1, source_target_pairs={{0,3},{1,0},{2,1},{3,2},{4,7},{5,4},{6,5},{7,6},{8,11},{9,8},{10,9... | collective-permute-start | bytes 387080 | tf_op jit(solution)/shard_map/ppermute | solution.py:345
  14.8 0.0 collective-permute-start.2
  14.8 7.2 %collective-permute-done.2.from_low = f32[108,2,128]{2,1,0:T(2,128)S(1)} collective-permute-done((f32[108,2,128]{2,1,0:T(2,128)S(1)}, f32[108,2,128]{2,1,0:T(2,128)S(1)}, u32[]{:S(2)}, u32[]{:S(2)}) %collective-permute-start.2) | collective-permute-done | bytes 110624 | tf_op jit(solution)/shard_map/ppermute | solution.py:345
  22.0 0.0 collective-permute-done.3.from_high
  22.0 0.5 %first_kernel.1 = (f32[81,8,128]{2,1,0:T(8,128)S(1)}, f32[27,8,128]{2,1,0:T(8,128)S(1)}, f32[81,8,128]{2,1,0:T(8,128)S(1)}, f32[45,8,128]{2,1,0:T(8,128)S(1)}, f...) custom-call(f32[81,4,128]{2,1,0:T(4,128)S(1)} %get-tuple-element.23.own, ...), custom_call_target="tpu_custom_call" | custom-call | flops 100000 | bytes 1861632 | tf_op jit(solution)/shard_map/first_kernel/pallas_call | solution.py:331
  22.5 1.6 %collective-permute-start.5 = (f32[45,8,128]{2,1,0:T(8,128)S(1)}, f32[45,8,128]{2,1,0:T(8,128)S(1)}, u32[]{:S(2)}, u32[]{:S(2)}) collective-permute-start(f32[45,8,128]{2,1,0:T(8,128)S(1)} %get-tuple-element.28), channel_id=1, source_target_pairs={{0,28},{4,0},{8,4},{12,8},{16,12},{20,16},{24,20},{28,24},{1,29},{... | collective-permute-start | bytes 552968 | tf_op jit(solution)/shard_map/ppermute | solution.py:345
  24.2 0.0 collective-permute-start.4
  24.2 5.0 %collective-permute-done.4.from_left = f32[18,8,128]{2,1,0:T(8,128)S(1)} collective-permute-done((f32[18,8,128]{2,1,0:T(8,128)S(1)}, f32[18,8,128]{2,1,0:T(8,128)S(1)}, u32[]{:S(2)}, u32[]{:S(2)}) %collective-permute-start.4) | collective-permute-done | bytes 73760 | tf_op jit(solution)/shard_map/ppermute | solution.py:345
  29.1 0.0 collective-permute-done.5.from_right
  29.1 0.4 second_kernel.1
  29.5 0.0 copy-start.1
  29.5 0.1 collective-permute-start.6
  29.6 2.6 %collective-permute-start.7 = (f32[18,8,128]{2,1,0:T(8,128)S(1)}, f32[18,8,128]{2,1,0:T(8,128)S(1)}, u32[]{:S(2)}, u32[]{:S(2)}) collective-permute-start(f32[18,8,128]{2,1,0:T(8,128)S(1)} %get-tuple-element.32), channel_id=1, source_target_pairs={{0,28},{4,0},{8,4},{12,8},{16,12},{20,16},{24,20},{28,24},{1,29},{... | collective-permute-start | bytes 221192 | tf_op jit(solution)/shard_map/ppermute | solution.py:345
  32.2 2.5 %collective-permute-done.6.from_left = f32[18,8,128]{2,1,0:T(8,128)S(1)} collective-permute-done((f32[18,8,128]{2,1,0:T(8,128)S(1)}, f32[18,8,128]{2,1,0:T(8,128)S(1)}, u32[]{:S(2)}, u32[]{:S(2)}) %collective-permute-start.6) | collective-permute-done | bytes 73760 | tf_op jit(solution)/shard_map/ppermute | solution.py:345
  34.7 0.0 collective-permute-done.7.from_right
  34.7 0.9 %moment_kernel.1 = (f32[81,8,128]{2,1,0:T(8,128)S(1)}, f32[32,128]{1,0:T(8,128)}) custom-call(f32[81,8,128]{2,1,0:T(8,128)S(1)} %get-tuple-element.30.image, f32[18,8,128]{2,1,0:T(8,128)S(1)} %collective-permute-done.6.from_left, f32[18,8,128]{2,1,0:T(8,128)S(1)} %collective-permute-done.7.from_right, f32[27,8,128]{2,1,0:T(8,128)S(1)} %get-tuple-element.29.weight, ...), custom_call_target="tpu_custom_call" | custom-call | flops 100000 | bytes 1601536 | tf_op jit(solution)/shard_map/moment_kernel/pallas_call | solution.py:331
  35.6 3.5 %all-to-all-start = ((f32[32,1,128]{2,1,0:T(1,128)}), f32[32,1,128]{2,1,0:T(1,128)S(1)}, u32[]{:S(2)}, u32[]{:S(2)}) async-start(f32[32,1,128]{2,1,0:T(1,128)} %bitcast.6), calls=%async_computation | async-start | bytes 32768 | tf_op jit(solution)/shard_map/all_to_all | solution.py:394
  39.1 0.9 %work_kernel.1 = f32[8,4,128]{2,1,0:T(4,128)} custom-call(bf16[648,4,128]{2,1,0:T(4,128)(2,1)S(1)} %bitcast.14, f32[8,4,128]{2,1,0:T(4,128)S(1)} %bitcast.19, f32[8,4,128]{2,1,0:T(4,128)S(1)} %bitcast.21, s32[4,128]{1,0:T(4,128)S(1)} %bitcast.25, f32[8,4,128]{2,1,0:T(4,128)S(1)} %bitcast.23, f32[54,8,128]{2,1,0:T(8,128)S(1)} %get-tuple-element.37.speeds, ...), custom_call_target="tpu_custom_call" | custom-call | flops 100000 | bytes 1136640 | tf_op jit(solution)/shard_map/work_kernel/pallas_call | solution.py:331
  40.1 6.1 %all-to-all-done = f32[32,1,128]{2,1,0:T(1,128)S(1)} async-done(((f32[32,1,128]{2,1,0:T(1,128)}), f32[32,1,128]{2,1,0:T(1,128)S(1)}, u32[]{:S(2)}, u32[]{:S(2)}) %all-to-all-start) | async-done | bytes 16416 | tf_op jit(solution)/shard_map/all_to_all | solution.py:394
  46.2 1.2 %last_kernel.1 = f32[3,2,8,257]{3,2,1,0:T(8,128)} custom-call(f32[32,128]{1,0:T(8,128)S(1)} %bitcast.22, f32[81,8,128]{2,1,0:T(8,128)S(1)} %get-tuple-element.33.zeroth, f32[81,8,128]{2,1,0:T(8,128)S(1)} %get-tuple-element.34.first, f32[81,8,128]{2,1,0:T(8,128)S(1)} %get-tuple-element.36.second, f32[3,2,8,257]{3,2,1,0:T(8,128)S(1)} %copy-done.4), custom_call_target="tpu_custom_call" | custom-call | flops 100000 | bytes 1110400 | tf_op jit(solution)/shard_map/last_kernel/pallas_call | solution.py:331
  (16 shorter events, 0.0 us)
Async XLA Ops:
  0.6 0.7 %copy-start.10 = (s32[1,4,128]{2,1,0:T(4,128)S(1)}, s32[1,4,128]{2,1,0:T(4,128)}, u32[]{:S(2)}) copy-start(s32[1,4,128]{2,1,0:T(4,128)} %param.10) | copy-start | bytes 6148
  1.3 1.1 %copy-start = (bf16[81,8,1,4,128]{4,3,2,1,0:T(4,128)(2,1)S(1)}, bf16[81,8,1,4,128]{4,3,2,1,0:T(4,128)(2,1)}, u32[]{:S(2)}) copy-start(bf16[81,8,1,4,128]{4,3,2,1,0:T(4,128)(2,1)} %param.11) | copy-start | bytes 1990660
  2.4 0.8 %copy-start.2 = (f32[27,1,4,128]{3,2,1,0:T(4,128)S(1)}, f32[27,1,4,128]{3,2,1,0:T(4,128)}, u32[]{:S(2)}) copy-start(f32[27,1,4,128]{3,2,1,0:T(4,128)} %param.12) | copy-start | bytes 165892
  3.2 0.7 %copy-start.5 = (f32[8,1,4,128]{3,2,1,0:T(4,128)S(1)}, f32[8,1,4,128]{3,2,1,0:T(4,128)}, u32[]{:S(2)}) copy-start(f32[8,1,4,128]{3,2,1,0:T(4,128)} %param.9) | copy-start | bytes 49156
  3.9 0.7 %copy-start.7 = (f32[8,1,4,128]{3,2,1,0:T(4,128)S(1)}, f32[8,1,4,128]{3,2,1,0:T(4,128)}, u32[]{:S(2)}) copy-start(f32[8,1,4,128]{3,2,1,0:T(4,128)} %param.8) | copy-start | bytes 49156
  4.7 3.9 %copy-start.4 = (f32[3,2,8,257]{3,2,1,0:T(8,128)S(1)}, f32[3,2,8,257]{3,2,1,0:T(8,128)}, u32[]{:S(2)}) copy-start(f32[3,2,8,257]{3,2,1,0:T(8,128)} %velocity.3) | copy-start | bytes 148036
  5.0 5.2 %collective-permute-start = (f32[27,4,128]{2,1,0:T(4,128)S(1)}, f32[27,4,128]{2,1,0:T(4,128)S(1)}, u32[]{:S(2)}, u32[]{:S(2)}) collective-permute-start(f32[27,4,128]{2,1,0:T(4,128)S(1)} %get-tuple-element.21), channel_id=1, source_target_pairs={{0,4},{4,8},{8,12},{12,16},{16,20},{20,24},{24,28},{28,0},{1,5},{5... | collective-permute-start | bytes 165896 | tf_op jit(solution)/shard_map/ppermute | solution.py:345
  5.6 4.8 %copy-start.3 = (f32[27,1,4,128]{3,2,1,0:T(4,128)S(1)}, f32[27,1,4,128]{3,2,1,0:T(4,128)}, u32[]{:S(2)}) copy-start(f32[27,1,4,128]{3,2,1,0:T(4,128)} %param.12) | copy-start | bytes 165892
  5.6 4.8 %collective-permute-start.1 = (f32[27,4,128]{2,1,0:T(4,128)S(1)}, f32[27,4,128]{2,1,0:T(4,128)S(1)}, u32[]{:S(2)}, u32[]{:S(2)}) collective-permute-start(f32[27,4,128]{2,1,0:T(4,128)S(1)} %get-tuple-element.22), channel_id=1, source_target_pairs={{0,28},{4,0},{8,4},{12,8},{16,12},{20,16},{24,20},{28,24},{1,29},{... | collective-permute-start | bytes 165896 | tf_op jit(solution)/shard_map/ppermute | solution.py:345
  10.4 11.6 %collective-permute-start.3 = (f32[126,2,128]{2,1,0:T(2,128)S(1)}, f32[126,2,128]{2,1,0:T(2,128)S(1)}, u32[]{:S(2)}, u32[]{:S(2)}) collective-permute-start(f32[126,2,128]{2,1,0:T(2,128)S(1)} %get-tuple-element.25), channel_id=1, source_target_pairs={{0,3},{1,0},{2,1},{3,2},{4,7},{5,4},{6,5},{7,6},{8,11},{9,8},{10,9... | collective-permute-start | bytes 387080 | tf_op jit(solution)/shard_map/ppermute | solution.py:345
  14.8 7.2 %collective-permute-start.2 = (f32[108,2,128]{2,1,0:T(2,128)S(1)}, f32[108,2,128]{2,1,0:T(2,128)S(1)}, u32[]{:S(2)}, u32[]{:S(2)}) collective-permute-start(f32[108,2,128]{2,1,0:T(2,128)S(1)} %get-tuple-element.24), channel_id=1, source_target_pairs={{0,1},{1,2},{2,3},{3,0},{4,5},{5,6},{6,7},{7,4},{8,9},{9,10},{10,1... | collective-permute-start | bytes 331784 | tf_op jit(solution)/shard_map/ppermute | solution.py:345
  22.5 6.6 %collective-permute-start.5 = (f32[45,8,128]{2,1,0:T(8,128)S(1)}, f32[45,8,128]{2,1,0:T(8,128)S(1)}, u32[]{:S(2)}, u32[]{:S(2)}) collective-permute-start(f32[45,8,128]{2,1,0:T(8,128)S(1)} %get-tuple-element.28), channel_id=1, source_target_pairs={{0,28},{4,0},{8,4},{12,8},{16,12},{20,16},{24,20},{28,24},{1,29},{... | collective-permute-start | bytes 552968 | tf_op jit(solution)/shard_map/ppermute | solution.py:345
  24.2 5.0 %collective-permute-start.4 = (f32[18,8,128]{2,1,0:T(8,128)S(1)}, f32[18,8,128]{2,1,0:T(8,128)S(1)}, u32[]{:S(2)}, u32[]{:S(2)}) collective-permute-start(f32[18,8,128]{2,1,0:T(8,128)S(1)} %get-tuple-element.27), channel_id=1, source_target_pairs={{0,4},{4,8},{8,12},{12,16},{16,20},{20,24},{24,28},{28,0},{1,5},{5... | collective-permute-start | bytes 221192 | tf_op jit(solution)/shard_map/ppermute | solution.py:345
  29.5 9.6 %copy-start.1 = (bf16[81,8,1,4,128]{4,3,2,1,0:T(4,128)(2,1)S(1)}, bf16[81,8,1,4,128]{4,3,2,1,0:T(4,128)(2,1)}, u32[]{:S(2)}) copy-start(bf16[81,8,1,4,128]{4,3,2,1,0:T(4,128)(2,1)} %param.11) | copy-start | bytes 1990660
  29.5 5.2 %collective-permute-start.6 = (f32[18,8,128]{2,1,0:T(8,128)S(1)}, f32[18,8,128]{2,1,0:T(8,128)S(1)}, u32[]{:S(2)}, u32[]{:S(2)}) collective-permute-start(f32[18,8,128]{2,1,0:T(8,128)S(1)} %get-tuple-element.31), channel_id=1, source_target_pairs={{0,4},{4,8},{8,12},{12,16},{16,20},{20,24},{24,28},{28,0},{1,5},{5... | collective-permute-start | bytes 221192 | tf_op jit(solution)/shard_map/ppermute | solution.py:345
  29.6 5.1 %collective-permute-start.7 = (f32[18,8,128]{2,1,0:T(8,128)S(1)}, f32[18,8,128]{2,1,0:T(8,128)S(1)}, u32[]{:S(2)}, u32[]{:S(2)}) collective-permute-start(f32[18,8,128]{2,1,0:T(8,128)S(1)} %get-tuple-element.32), channel_id=1, source_target_pairs={{0,28},{4,0},{8,4},{12,8},{16,12},{20,16},{24,20},{28,24},{1,29},{... | collective-permute-start | bytes 221192 | tf_op jit(solution)/shard_map/ppermute | solution.py:345
  34.7 4.4 %copy-start.9 = (f32[8,1,4,128]{3,2,1,0:T(4,128)S(1)}, f32[8,1,4,128]{3,2,1,0:T(4,128)}, u32[]{:S(2)}) copy-start(f32[8,1,4,128]{3,2,1,0:T(4,128)} %param.13) | copy-start | bytes 49156
  35.6 3.5 %copy-start.6 = (f32[8,1,4,128]{3,2,1,0:T(4,128)S(1)}, f32[8,1,4,128]{3,2,1,0:T(4,128)}, u32[]{:S(2)}) copy-start(f32[8,1,4,128]{3,2,1,0:T(4,128)} %param.9) | copy-start | bytes 49156
  35.6 3.5 %copy-start.8 = (f32[8,1,4,128]{3,2,1,0:T(4,128)S(1)}, f32[8,1,4,128]{3,2,1,0:T(4,128)}, u32[]{:S(2)}) copy-start(f32[8,1,4,128]{3,2,1,0:T(4,128)} %param.8) | copy-start | bytes 49156
  35.6 10.6 %all-to-all-start = ((f32[32,1,128]{2,1,0:T(1,128)}), f32[32,1,128]{2,1,0:T(1,128)S(1)}, u32[]{:S(2)}, u32[]{:S(2)}) async-start(f32[32,1,128]{2,1,0:T(1,128)} %bitcast.6), calls=%async_computation | async-start | bytes 32768 | tf_op jit(solution)/shard_map/all_to_all | solution.py:394
where the time goes:
time: 47.8 us; the launch traced here: 47.3 us
  waiting for transfers between devices  22.3 us (47%)
  starting transfers between devices  15.6 us (33%)
  Pallas kernels  4.69 us (10%)
  local copies, waits for them, and re-layouts  4.04 us (8%)
  between operations  0.73 us (2%)
    ppermute x8, waiting for transfers between devices, shift(): return lax.ppermute(x, axis, [(i, (i + by) % count) for i in range(count)])  16.2 us
    ppermute x8, starting transfers between devices, shift(): return lax.ppermute(x, axis, [(i, (i + by) % count) for i in range(count)])  12.1 us
    all_to_all x1, waiting for transfers between devices, local(): moments = lax.all_to_all(moments, ('slab', 'brick'), 0, 0, tiled=True)  6.13 us
    pallas_call x8, Pallas kernels, call(): pl.pallas_call(kernel, out_shape=shapes, in_specs=[VMEM] * len(args), out...  4.69 us
    unnamed x22, local copies, waits for them, and re-layouts  4.04 us
    all_to_all x1, starting transfers between devices, local(): moments = lax.all_to_all(moments, ('slab', 'brick'), 0, 0, tiled=True)  3.46 us
  transfers between devices with their start and end apart: 9, of which 5 were waited for; matrix products, arithmetic and copies ran while one was open for 0% of the time, Pallas kernels for 3%

commit v1 on v0

--- a/solution.py
+++ b/solution.py
@@ -74,11 +74,32 @@
     return values
 
 
-def force_kernel(geometry, density, energy, material, mass_weight, field, to_left, to_right):
+def force_kernel(
+    geometry_in, density_in, energy_in, material_in, mass_weight_in,
+    field, to_left, to_right,
+    geometry, density, energy, material, mass_weight, sems,
+):
+    small = [
+        pltpu.make_async_copy(source, target, sems.at[3 + i])
+        for i, (source, target) in enumerate(
+            [(density_in, density), (energy_in, energy), (material_in, material), (mass_weight_in, mass_weight)]
+        )
+    ]
+    parts = [
+        pltpu.make_async_copy(
+            geometry_in.at[pl.ds(216 * comp, 216)], geometry.at[pl.ds(216 * comp, 216)], sems.at[comp]
+        )
+        for comp in range(3)
+    ]
+    for copy in small + parts:
+        copy.start()
+    for copy in small:
+        copy.wait()
     gamma = jnp.where(material[...] == 0, 2.0 / 3.0, 0.4).astype(F32)
     pressure = (gamma[None] * density[...] * energy[...]).astype(BF16).astype(F32)
     gravity = from_points([mass_weight[q] * POINT_WEIGHT[q] for q in range(27)])
     for comp in range(3):
+        parts[comp].wait()
         for n in range(27):
             r = 27 * comp + n
             block = geometry[pl.ds(8 * r, 8)].astype(F32)
@@ -122,15 +143,15 @@
             if n // 9 == 2:
                 value = value + from_right[9 * comp + n - 18]
             out[r] = value
-            to_low[r] = value[:HALO]
-            to_high[r] = value[OWN - HALO :]
+            to_low[r] = value[:HALO].astype(BF16)
+            to_high[r] = value[OWN - HALO :].astype(BF16)
     for q in range(27):
-        to_low[81 + q] = mass_weight[q, :HALO]
-        to_high[81 + q] = mass_weight[q, OWN - HALO :]
+        to_low[81 + q] = mass_weight[q, :HALO].astype(BF16)
+        to_high[81 + q] = mass_weight[q, OWN - HALO :].astype(BF16)
     for comp in range(3):
         for a in range(2):
             for c in range(3):
-                to_low[108 + 6 * comp + 3 * a + c] = spread[12 * comp + 6 * a + c, :HALO]
+                to_low[108 + 6 * comp + 3 * a + c] = spread[12 * comp + 6 * a + c, :HALO].astype(BF16)
 
 
 def send_planes(values, comp, to_left, to_right):
@@ -152,15 +173,15 @@
     own, from_low, from_high, mass_weight, spread, field, weight, image, to_left, to_right, speeds, rows
 ):
     for q in range(27):
-        rows[q, :HALO] = from_low[81 + q]
+        rows[q, :HALO] = from_low[81 + q].astype(F32)
         rows[q, HALO : HALO + OWN] = mass_weight[q]
-        rows[q, HALO + OWN :] = from_high[81 + q]
+        rows[q, HALO + OWN :] = from_high[81 + q].astype(F32)
     for q in range(27):
         weight[q] = rows[q] * POINT_WEIGHT[q]
     for r in range(81):
-        rows[r, :HALO] = from_low[r]
+        rows[r, :HALO] = from_low[r].astype(F32)
         rows[r, HALO : HALO + OWN] = own[r]
-        rows[r, HALO + OWN :] = from_high[r]
+        rows[r, HALO + OWN :] = from_high[r].astype(F32)
     for comp in range(3):
         values = [rows[27 * comp + n] for n in range(27)]
         values = assemble_y(assemble_z(values, comp == 2))
@@ -171,20 +192,20 @@
             image[27 * comp + n] = values[n]
         send_planes(values, comp, to_left, to_right)
     row = lax.broadcasted_iota(jnp.int32, (8, 128), 0)
+    plane = []
     for comp in range(3):
         for a in range(2):
+            speed = [spread[12 * comp + 6 * a + n] for n in range(6)]
             for c in range(3):
-                for b in range(2):
-                    value = spread[12 * comp + 6 * a + 3 * b + c]
-                    speeds[18 * comp + 9 * a + 3 * b + c] = value
-                    if a == 0:
-                        to_left[18 + 9 * comp + 3 * b + c] = value
-                beyond = from_high[108 + 6 * comp + 3 * a + c, 0:1]
-                value = spread[12 * comp + 6 * a + c]
-                value = jnp.where(row == OWN - 1, beyond, pltpu.roll(value, 7, 0))
-                speeds[18 * comp + 9 * a + 6 + c] = value
-                if a == 0:
-                    to_left[18 + 9 * comp + 6 + c] = value
+                beyond = from_high[108 + 6 * comp + 3 * a + c].astype(F32)[0:1]
+                speed.append(jnp.where(row == OWN - 1, beyond, pltpu.roll(speed[c], 7, 0)))
+            for n in range(9):
+                speeds[18 * comp + 9 * a + n] = speed[n]
+            if a == 0:
+                plane += speed
+    for n in range(0, 27, 2):
+        upper = plane[n] if n == 26 else pltpu.roll(plane[n + 1], 4, 0)
+        to_left[18 + n // 2] = jnp.where(row < OWN, plane[n], upper)
 
 
 def take_planes(image, from_left, from_right, comp):
@@ -221,7 +242,8 @@
             if n < 18:
                 speed = speeds[18 * comp + n, :OWN]
             else:
-                speed = from_right[18 + 9 * comp + n - 18, :OWN]
+                k = 9 * comp + n - 18
+                speed = from_right[18 + k // 2, OWN * (k % 2) : OWN * (k % 2) + OWN]
             work = work + geometry[pl.ds(8 * (27 * comp + n), 8)].astype(F32) * speed[None]
     out[...] = energy[...] + HALF_STEP * pressure * work / energy_mass[...]
 
@@ -236,29 +258,32 @@
     return total
 
 
-def moment_kernel(image, from_left, from_right, weight, zeroth, first, second, moments):
+def product_kernel(zeroth, first, products):
+    for k, (one, other) in enumerate([(zeroth, zeroth), (zeroth, first), (first, first)]):
+        total = jnp.zeros((8, 128), F32)
+        for comp in range(3):
+            total = dot_owned(one, other, comp, total)
+        products[k] = total
+
+
+def moment_kernel(image, from_left, from_right, weight, first, products, second, moments):
     zero = jnp.zeros((8, 128), F32)
-    energy_norm = zero
+    cross, norm, quadratic = zero, zero, zero
     for comp in range(3):
         values = take_planes(image, from_left, from_right, comp)
         for n in range(27):
             second[27 * comp + n] = values[n]
+        values_at = {27 * comp + n: values[n] for n in range(27)}
+        cross = dot_owned(first, values_at, comp, cross)
+        norm = dot_owned(values_at, values_at, comp, norm)
         points = to_points(values)
         for q in range(27):
-            energy_norm = energy_norm + points[q] * points[q] * weight[q]
-    pairs = [(zeroth, zeroth), (zeroth, first), (first, first), (first, second), (second, second)]
-    totals = []
-    for one, other in pairs:
-        total = zero
-        for comp in range(3):
-            total = dot_owned(one, other, comp, total)
-        totals.append(total)
-    totals.append(energy_norm)
+            quadratic = quadratic + points[q] * points[q] * weight[q]
     row = lax.broadcasted_iota(jnp.int32, (8, 128), 0)
     lane = lane_of((1, 128))
     mine = (row >= HALO) & (row < HALO + OWN)
     line = jnp.zeros((1, 128), F32)
-    for k, total in enumerate(totals):
+    for k, total in enumerate([products[0], products[1], products[2], cross, norm, quadratic]):
         total = jnp.sum(jnp.where(mine, total, 0.0), axis=0, keepdims=True)
         line = jnp.where(lane == k, jnp.sum(total, axis=1, keepdims=True), line)
     moments[...] = jnp.broadcast_to(line, moments.shape)
@@ -289,49 +314,52 @@
     return high, (x - high.astype(F32)).astype(BF16)
 
 
-def last_kernel(moments, zeroth, first, second, velocity, out):
+def nodal_kernel(zeroth, first, second, out):
+    row = lax.broadcasted_iota(jnp.int32, (48, 96), 0)
+    source = lax.broadcasted_iota(jnp.int32, (48, 96), 1)
+    wanted = (row // 8) * 16 + (row % 2) * 8 + HALO + (row % 8) // 2
+    move = (source == wanted).astype(F32).astype(BF16)
+    source = lax.broadcasted_iota(jnp.int32, (384, 384), 0)
+    node = lax.broadcasted_iota(jnp.int32, (384, 384), 1)
+    wanted = jnp.where(node < 256, (node % 2) * 128 + node // 2, 383)
+    place = ((source == wanted) & (node <= 256)).astype(F32).astype(BF16)
+    for k, field in enumerate((zeroth, first, second)):
+        blocks = []
+        for c in range(3):
+            column = []
+            for comp in range(3):
+                for a in range(2):
+                    for b in range(2):
+                        column.append(field[27 * comp + 9 * a + 3 * b + c])
+            blocks.append(jnp.concatenate(column, axis=0))
+        high, low = halves(jnp.concatenate(blocks, axis=1))
+        moved = jnp.dot(move, high, preferred_element_type=F32) + jnp.dot(move, low, preferred_element_type=F32)
+        high, low = halves(moved)
+        out[k] = jnp.dot(high, place, preferred_element_type=F32) + jnp.dot(low, place, preferred_element_type=F32)
+
+
+def last_kernel(moments, nodal, velocity, out):
     line = jnp.sum(moments[...], axis=0, keepdims=True)
     lane = lane_of((1, 128))
     mu = [jnp.sum(jnp.where(lane == k, line, 0.0), axis=1, keepdims=True) for k in range(6)]
     c0, c1, c2 = [HALF_STEP * c for c in solve(mu)]
-    blocks = []
-    for c in range(3):
-        column = []
-        for comp in range(3):
-            for a in range(2):
-                for b in range(2):
-                    n = 27 * comp + 9 * a + 3 * b + c
-                    column.append(c0 * zeroth[n] + c1 * first[n] + c2 * second[n])
-        blocks.append(jnp.concatenate(column, axis=0))
-    joined = jnp.concatenate(blocks, axis=1)
-    row = lax.broadcasted_iota(jnp.int32, (48, 96), 0)
-    source = lax.broadcasted_iota(jnp.int32, (48, 96), 1)
-    wanted = (row // 8) * 16 + (row % 2) * 8 + HALO + (row % 8) // 2
-    move = (source == wanted).astype(F32).astype(BF16)
-    high, low = halves(joined)
-    moved = jnp.dot(move, high, preferred_element_type=F32) + jnp.dot(move, low, preferred_element_type=F32)
-    source = lax.broadcasted_iota(jnp.int32, (384, 384), 0)
-    node = lax.broadcasted_iota(jnp.int32, (384, 384), 1)
-    wanted = jnp.where(node < 256, (node % 2) * 128 + node // 2, 383)
-    place = ((source == wanted) & (node <= 256)).astype(F32).astype(BF16)
-    high, low = halves(moved)
-    placed = jnp.dot(high, place, preferred_element_type=F32) + jnp.dot(low, place, preferred_element_type=F32)
     for comp in range(3):
         for x in range(2):
             start = 16 * comp + 8 * x
-            out[comp, x] = velocity[comp, x] + placed[start : start + 8, : velocity.shape[3]]
+            part = [nodal[k, pl.ds(start, 8), : velocity.shape[3]] for k in range(3)]
+            out[comp, x] = velocity[comp, x] + (c0 * part[0] + c1 * part[1] + c2 * part[2])
 
 
 VMEM = pl.BlockSpec(memory_space=pltpu.VMEM)
 
 
-def call(kernel, outs, *args, scratch=(), flops=100000):
-    shapes = [jax.ShapeDtypeStruct(shape, F32) for shape in outs]
+def call(kernel, outs, *args, scratch=(), flops=100000, place=VMEM, dtypes=None):
+    shapes = [jax.ShapeDtypeStruct(shape, dtype) for shape, dtype in zip(outs, dtypes or [F32] * len(outs))]
     moved = sum(a.size * a.dtype.itemsize for a in args) + sum(4 * int(np.prod(s)) for s in outs)
     return pl.pallas_call(
         kernel,
         out_shape=shapes,
-        in_specs=[VMEM] * len(args),
+        in_specs=[place] * len(args),
         out_specs=[VMEM] * len(outs),
         scratch_shapes=list(scratch),
         compiler_params=pltpu.CompilerParams(vmem_limit_bytes=32 * 1024 * 1024),
@@ -358,7 +386,18 @@
     devices = lax.axis_size("slab") * lax.axis_size("brick")
 
     force, to_left, to_right = call(
-        force_kernel, [(81,) + tile, (27,) + tile, (27,) + tile], geometry, density, energy, material, mass_weight
+        force_kernel,
+        [(81,) + tile, (27,) + tile, (27,) + tile],
+        *[pltpu.with_memory_space_constraint(x, pltpu.HBM) for x in (geometry, density, energy, material, mass_weight)],
+        scratch=[
+            pltpu.VMEM((648,) + tile, BF16),
+            pltpu.VMEM((8,) + tile, F32),
+            pltpu.VMEM((8,) + tile, F32),
+            pltpu.VMEM(tile, jnp.int32),
+            pltpu.VMEM((27,) + tile, F32),
+            pltpu.SemaphoreType.DMA((7,)),
+        ],
+        place=pl.BlockSpec(memory_space=pltpu.HBM),
     )
     (spread,) = call(spread_kernel, [(36,) + full], velocity)
     from_right = shift(to_left, "slab", -1)
@@ -367,12 +406,13 @@
         rim_kernel,
         [(81,) + tile, (126,) + pair, (108,) + pair],
         force, from_left, from_right, mass_weight, spread,
+        dtypes=[F32, BF16, BF16],
     )
     from_high = shift(to_low, "brick", -1)
     from_low = shift(to_high, "brick", 1)
     zeroth, weight, image, to_left, to_right, speeds = call(
         first_kernel,
-        [(81,) + full, (27,) + full, (81,) + full, (45,) + full, (18,) + full, (54,) + full],
+        [(81,) + full, (27,) + full, (81,) + full, (32,) + full, (18,) + full, (54,) + full],
         own, from_low, from_high, mass_weight, spread,
         scratch=[pltpu.VMEM((81,) + full, F32)],
     )
@@ -388,11 +428,13 @@
     )
     from_right = shift(to_left, "slab", -1)
     from_left = shift(to_right, "slab", 1)
+    (products,) = call(product_kernel, [(3,) + full], zeroth, first)
     second, moments = call(
-        moment_kernel, [(81,) + full, (devices, 128)], image, from_left, from_right, weight, zeroth, first
+        moment_kernel, [(81,) + full, (devices, 128)], image, from_left, from_right, weight, first, products
     )
     moments = lax.all_to_all(moments, ("slab", "brick"), 0, 0, tiled=True)
-    (velocity_half,) = call(last_kernel, [velocity.shape], moments, zeroth, first, second, velocity)
+    (nodal,) = call(nodal_kernel, [(3, 48, 384)], zeroth, first, second)
+    (velocity_half,) = call(last_kernel, [velocity.shape], moments, nodal, velocity)
     return (velocity_half, energy_half.reshape(8, 1, 4, 128))
 
 

time: 47.8 us -> 41.9 us (0.88)
  local copies, waits for them, and re-layouts: 4.04 us -> 0.66 us
  waiting for transfers between devices: 22.3 us -> 19.2 us
  Pallas kernels: 4.69 us -> 6.27 us
  starting transfers between devices: 15.6 us -> 14.8 us
    unnamed x22 -> x14, local copies, waits for them, and re-layouts: 4.04 us -> 0.66 us
    ppermute x8, waiting for transfers between devices: 16.2 us -> 14.6 us  [shift(): return lax.ppermute(x, axis, [(i, (i + by) % count) for i in range(count)])]
    pallas_call x8 -> x10, Pallas kernels: 4.69 us -> 6.27 us  [call(): pl.pallas_call(kernel, out_shape=shapes, in_specs=[place] * len(args), ou...]
    all_to_all x1, waiting for transfers between devices: 6.13 us -> 4.62 us  [local(): moments = lax.all_to_all(moments, ('slab', 'brick'), 0, 0, tiled=True)]
    all_to_all x1, starting transfers between devices: 3.46 us -> 2.68 us  [local(): moments = lax.all_to_all(moments, ('slab', 'brick'), 0, 0, tiled=True)]
  transfers between devices with their start and end apart: 9 -> 9, of which waited for: 5 -> 5; matrix products, arithmetic and copies ran while one was open for 0% -> 0% of each run, Pallas kernels for 3% -> 5%
where the time goes in v1:
time: 41.9 us; the launch traced here: 41.6 us
  waiting for transfers between devices  19.2 us (46%)
  starting transfers between devices  14.8 us (35%)
  Pallas kernels  6.27 us (15%)
  between operations  0.74 us (2%)
  local copies, waits for them, and re-layouts  0.66 us (2%)
    ppermute x8, waiting for transfers between devices, shift(): return lax.ppermute(x, axis, [(i, (i + by) % count) for i in range(count)])  14.6 us
    ppermute x8, starting transfers between devices, shift(): return lax.ppermute(x, axis, [(i, (i + by) % count) for i in range(count)])  12.1 us
    pallas_call x10, Pallas kernels, call(): pl.pallas_call(kernel, out_shape=shapes, in_specs=[place] * len(args), ou...  6.27 us
    all_to_all x1, waiting for transfers between devices, local(): moments = lax.all_to_all(moments, ('slab', 'brick'), 0, 0, tiled=True)  4.62 us
    all_to_all x1, starting transfers between devices, local(): moments = lax.all_to_all(moments, ('slab', 'brick'), 0, 0, tiled=True)  2.68 us
  transfers between devices with their start and end apart: 9, of which 5 were waited for; matrix products, arithmetic and copies ran while one was open for 0% of the time, Pallas kernels for 5%

profile of v1, /device:TPU:0, one launch (start us, length us, event | category | flops | bytes accessed | tf_op | source)
XLA Modules:
  0.0 41.6 jit_solution(10759492842251510215)
XLA Ops:
  0.6 0.0 copy-start.2
  0.6 1.5 %force_kernel.1 = (f32[81,4,128]{2,1,0:T(4,128)S(1)}, f32[27,4,128]{2,1,0:T(4,128)S(1)}, f32[27,4,128]{2,1,0:T(4,128)S(1)}) custom-call(bf16[648,4,128]{2,1,0:T(4,128)(2,1)} %bitcast.13, f32[8,4,128]{2,1,0:T(4,128)} %bitcast.18, f32[8,4,128]{2,1,0:T(4,128)} %bitcast.20, s32[4,128]{1,0:T(4,128)} %bitcast.24, f32[27,4,128]{2,1,0:T(4,128)} %bitcast.15), custom_call_target="tpu_custom_call" | custom-call | flops 100000 | bytes 1030144 | tf_op jit(solution)/shard_map/force_kernel/pallas_call | solution.py:359
  2.1 0.5 %collective-permute-start = (f32[27,4,128]{2,1,0:T(4,128)S(1)}, f32[27,4,128]{2,1,0:T(4,128)S(1)}, u32[]{:S(2)}, u32[]{:S(2)}) collective-permute-start(f32[27,4,128]{2,1,0:T(4,128)S(1)} %get-tuple-element.21), channel_id=1, source_target_pairs={{0,4},{4,8},{8,12},{12,16},{16,20},{20,24},{24,28},{28,0},{1,5},{5... | collective-permute-start | bytes 165896 | tf_op jit(solution)/shard_map/ppermute | solution.py:373
  2.6 3.0 %collective-permute-start.1 = (f32[27,4,128]{2,1,0:T(4,128)S(1)}, f32[27,4,128]{2,1,0:T(4,128)S(1)}, u32[]{:S(2)}, u32[]{:S(2)}) collective-permute-start(f32[27,4,128]{2,1,0:T(4,128)S(1)} %get-tuple-element.22), channel_id=1, source_target_pairs={{0,28},{4,0},{8,4},{12,8},{16,12},{20,16},{24,20},{28,24},{1,29},{... | collective-permute-start | bytes 165896 | tf_op jit(solution)/shard_map/ppermute | solution.py:373
  5.6 0.0 copy-done.2
  5.6 0.3 spread_kernel.1.spread
  5.9 1.5 %collective-permute-done.from_left = f32[27,4,128]{2,1,0:T(4,128)S(1)} collective-permute-done((f32[27,4,128]{2,1,0:T(4,128)S(1)}, f32[27,4,128]{2,1,0:T(4,128)S(1)}, u32[]{:S(2)}, u32[]{:S(2)}) %collective-permute-start) | collective-permute-done | bytes 55328 | tf_op jit(solution)/shard_map/ppermute | solution.py:373
  7.4 0.0 collective-permute-done.1.from_right
  7.4 0.1 rim_kernel.1
  7.5 4.4 %collective-permute-start.3 = (bf16[126,2,128]{2,1,0:T(2,128)(2,1)S(1)}, bf16[126,2,128]{2,1,0:T(2,128)(2,1)S(1)}, u32[]{:S(2)}, u32[]{:S(2)}) collective-permute-start(bf16[126,2,128]{2,1,0:T(2,128)(2,1)S(1)} %get-tuple-element.25), channel_id=1, source_target_pairs={{0,3},{1,0},{2,1},{3,2},{4,7},{5,4},{6,5},{7,6},{8,11},{9,8},{10,9... | collective-permute-start | bytes 193544 | tf_op jit(solution)/shard_map/ppermute | solution.py:373
  11.9 0.0 collective-permute-start.2
  11.9 6.0 %collective-permute-done.2.from_low = bf16[108,2,128]{2,1,0:T(2,128)(2,1)S(1)} collective-permute-done((bf16[108,2,128]{2,1,0:T(2,128)(2,1)S(1)}, bf16[108,2,128]{2,1,0:T(2,128)(2,1)S(1)}, u32[]{:S(2)}, u32[]{:S(2)}) %collective-permute-start.2) | collective-permute-done | bytes 55328 | tf_op jit(solution)/shard_map/ppermute | solution.py:373
  17.9 0.0 collective-permute-done.3.from_high
  17.9 0.6 %first_kernel.1 = (f32[81,8,128]{2,1,0:T(8,128)S(1)}, f32[27,8,128]{2,1,0:T(8,128)S(1)}, f32[81,8,128]{2,1,0:T(8,128)S(1)}, f32[32,8,128]{2,1,0:T(8,128)S(1)}, f...) custom-call(f32[81,4,128]{2,1,0:T(4,128)S(1)} %get-tuple-element.23.own, ...), custom_call_target="tpu_custom_call" | custom-call | flops 100000 | bytes 1688576 | tf_op jit(solution)/shard_map/first_kernel/pallas_call | solution.py:359
  18.5 1.6 %collective-permute-start.5 = (f32[32,8,128]{2,1,0:T(8,128)S(1)}, f32[32,8,128]{2,1,0:T(8,128)S(1)}, u32[]{:S(2)}, u32[]{:S(2)}) collective-permute-start(f32[32,8,128]{2,1,0:T(8,128)S(1)} %get-tuple-element.28), channel_id=1, source_target_pairs={{0,28},{4,0},{8,4},{12,8},{16,12},{20,16},{24,20},{28,24},{1,29},{... | collective-permute-start | bytes 393224 | tf_op jit(solution)/shard_map/ppermute | solution.py:373
  20.1 0.0 collective-permute-start.4
  20.1 4.7 %collective-permute-done.4.from_left = f32[18,8,128]{2,1,0:T(8,128)S(1)} collective-permute-done((f32[18,8,128]{2,1,0:T(8,128)S(1)}, f32[18,8,128]{2,1,0:T(8,128)S(1)}, u32[]{:S(2)}, u32[]{:S(2)}) %collective-permute-start.4) | collective-permute-done | bytes 73760 | tf_op jit(solution)/shard_map/ppermute | solution.py:373
  24.7 0.0 collective-permute-done.5.from_right
  24.7 0.4 second_kernel.1
  25.1 0.1 collective-permute-start.6
  25.2 2.6 %collective-permute-start.7 = (f32[18,8,128]{2,1,0:T(8,128)S(1)}, f32[18,8,128]{2,1,0:T(8,128)S(1)}, u32[]{:S(2)}, u32[]{:S(2)}) collective-permute-start(f32[18,8,128]{2,1,0:T(8,128)S(1)} %get-tuple-element.32), channel_id=1, source_target_pairs={{0,28},{4,0},{8,4},{12,8},{16,12},{20,16},{24,20},{28,24},{1,29},{... | collective-permute-start | bytes 221192 | tf_op jit(solution)/shard_map/ppermute | solution.py:373
  27.8 0.1 product_kernel.1.products
  27.9 2.4 %collective-permute-done.6.from_left = f32[18,8,128]{2,1,0:T(8,128)S(1)} collective-permute-done((f32[18,8,128]{2,1,0:T(8,128)S(1)}, f32[18,8,128]{2,1,0:T(8,128)S(1)}, u32[]{:S(2)}, u32[]{:S(2)}) %collective-permute-start.6) | collective-permute-done | bytes 73760 | tf_op jit(solution)/shard_map/ppermute | solution.py:373
  30.2 0.0 collective-permute-done.7.from_right
  30.2 0.9 %moment_kernel.1 = (f32[81,8,128]{2,1,0:T(8,128)S(1)}, f32[32,128]{1,0:T(8,128)}) custom-call(f32[81,8,128]{2,1,0:T(8,128)S(1)} %get-tuple-element.30.image, f32[18,8,128]{2,1,0:T(8,128)S(1)} %collective-permute-done.6.from_left, f32[18,8,128]{2,1,0:T(8,128)S(1)} %collective-permute-done.7.from_right, f32[27,8,128]{2,1,0:T(8,128)S(1)} %get-tuple-element.29.weight, ...), custom_call_target="tpu_custom_call" | custom-call | flops 100000 | bytes 1282048 | tf_op jit(solution)/shard_map/moment_kernel/pallas_call | solution.py:359
  31.1 2.7 %all-to-all-start = ((f32[32,1,128]{2,1,0:T(1,128)}), f32[32,1,128]{2,1,0:T(1,128)S(1)}, u32[]{:S(2)}, u32[]{:S(2)}) async-start(f32[32,1,128]{2,1,0:T(1,128)} %bitcast.6), calls=%async_computation | async-start | bytes 32768 | tf_op jit(solution)/shard_map/all_to_all | solution.py:435
  33.8 0.0 copy-start.6
  33.8 0.6 %copy-done.6 = s32[1,4,128]{2,1,0:T(4,128)S(1)} copy-done((s32[1,4,128]{2,1,0:T(4,128)S(1)}, s32[1,4,128]{2,1,0:T(4,128)}, u32[]{:S(2)}) %copy-start.6) | copy-done | bytes 2072
  34.5 1.0 %work_kernel.1 = f32[8,4,128]{2,1,0:T(4,128)} custom-call(bf16[648,4,128]{2,1,0:T(4,128)(2,1)S(1)} %bitcast.14, f32[8,4,128]{2,1,0:T(4,128)S(1)} %bitcast.19, f32[8,4,128]{2,1,0:T(4,128)S(1)} %bitcast.21, s32[4,128]{1,0:T(4,128)S(1)} %bitcast.25, f32[8,4,128]{2,1,0:T(4,128)S(1)} %bitcast.23, f32[54,8,128]{2,1,0:T(8,128)S(1)} %get-tuple-element.37.speeds, ...), custom_call_target="tpu_custom_call" | custom-call | flops 100000 | bytes 1083392 | tf_op jit(solution)/shard_map/work_kernel/pallas_call | solution.py:359
  35.4 0.8 %nodal_kernel.1.nodal = f32[3,48,384]{2,1,0:T(8,128)S(1)} custom-call(f32[81,8,128]{2,1,0:T(8,128)S(1)} %get-tuple-element.34.zeroth, f32[81,8,128]{2,1,0:T(8,128)S(1)} %get-tuple-element.33.first, f32[81,8,128]{2,1,0:T(8,128)S(1)} %get-tuple-element.36.second), custom_call_target="tpu_custom_call" | custom-call | flops 100000 | bytes 1216512 | tf_op jit(solution)/shard_map/nodal_kernel/pallas_call | solution.py:359
  36.3 4.6 %all-to-all-done = f32[32,1,128]{2,1,0:T(1,128)S(1)} async-done(((f32[32,1,128]{2,1,0:T(1,128)}), f32[32,1,128]{2,1,0:T(1,128)S(1)}, u32[]{:S(2)}, u32[]{:S(2)}) %all-to-all-start) | async-done | bytes 16416 | tf_op jit(solution)/shard_map/all_to_all | solution.py:435
  40.9 0.8 %last_kernel.1 = f32[3,2,8,257]{3,2,1,0:T(8,128)} custom-call(f32[32,128]{1,0:T(8,128)S(1)} %bitcast.22, f32[3,48,384]{2,1,0:T(8,128)S(1)} %nodal_kernel.1.nodal, f32[3,2,8,257]{3,2,1,0:T(8,128)S(1)} %copy-done.2), custom_call_target="tpu_custom_call" | custom-call | flops 100000 | bytes 336256 | tf_op jit(solution)/shard_map/last_kernel/pallas_call | solution.py:359
  (10 shorter events, 0.0 us)
Async XLA Ops:
  0.6 5.0 %copy-start.2 = (f32[3,2,8,257]{3,2,1,0:T(8,128)S(1)}, f32[3,2,8,257]{3,2,1,0:T(8,128)}, u32[]{:S(2)}) copy-start(f32[3,2,8,257]{3,2,1,0:T(8,128)} %velocity.3) | copy-start | bytes 148036
  2.1 5.2 %collective-permute-start = (f32[27,4,128]{2,1,0:T(4,128)S(1)}, f32[27,4,128]{2,1,0:T(4,128)S(1)}, u32[]{:S(2)}, u32[]{:S(2)}) collective-permute-start(f32[27,4,128]{2,1,0:T(4,128)S(1)} %get-tuple-element.21), channel_id=1, source_target_pairs={{0,4},{4,8},{8,12},{12,16},{16,20},{20,24},{24,28},{28,0},{1,5},{5... | collective-permute-start | bytes 165896 | tf_op jit(solution)/shard_map/ppermute | solution.py:373
  2.6 4.8 %copy-start.1 = (f32[27,1,4,128]{3,2,1,0:T(4,128)S(1)}, f32[27,1,4,128]{3,2,1,0:T(4,128)}, u32[]{:S(2)}) copy-start(f32[27,1,4,128]{3,2,1,0:T(4,128)} %param.12) | copy-start | bytes 165892
  2.6 4.8 %collective-permute-start.1 = (f32[27,4,128]{2,1,0:T(4,128)S(1)}, f32[27,4,128]{2,1,0:T(4,128)S(1)}, u32[]{:S(2)}, u32[]{:S(2)}) collective-permute-start(f32[27,4,128]{2,1,0:T(4,128)S(1)} %get-tuple-element.22), channel_id=1, source_target_pairs={{0,28},{4,0},{8,4},{12,8},{16,12},{20,16},{24,20},{28,24},{1,29},{... | collective-permute-start | bytes 165896 | tf_op jit(solution)/shard_map/ppermute | solution.py:373
  7.5 10.4 %collective-permute-start.3 = (bf16[126,2,128]{2,1,0:T(2,128)(2,1)S(1)}, bf16[126,2,128]{2,1,0:T(2,128)(2,1)S(1)}, u32[]{:S(2)}, u32[]{:S(2)}) collective-permute-start(bf16[126,2,128]{2,1,0:T(2,128)(2,1)S(1)} %get-tuple-element.25), channel_id=1, source_target_pairs={{0,3},{1,0},{2,1},{3,2},{4,7},{5,4},{6,5},{7,6},{8,11},{9,8},{10,9... | collective-permute-start | bytes 193544 | tf_op jit(solution)/shard_map/ppermute | solution.py:373
  11.9 6.0 %collective-permute-start.2 = (bf16[108,2,128]{2,1,0:T(2,128)(2,1)S(1)}, bf16[108,2,128]{2,1,0:T(2,128)(2,1)S(1)}, u32[]{:S(2)}, u32[]{:S(2)}) collective-permute-start(bf16[108,2,128]{2,1,0:T(2,128)(2,1)S(1)} %get-tuple-element.24), channel_id=1, source_target_pairs={{0,1},{1,2},{2,3},{3,0},{4,5},{5,6},{6,7},{7,4},{8,9},{9,10},{10,1... | collective-permute-start | bytes 165896 | tf_op jit(solution)/shard_map/ppermute | solution.py:373
  18.5 6.3 %collective-permute-start.5 = (f32[32,8,128]{2,1,0:T(8,128)S(1)}, f32[32,8,128]{2,1,0:T(8,128)S(1)}, u32[]{:S(2)}, u32[]{:S(2)}) collective-permute-start(f32[32,8,128]{2,1,0:T(8,128)S(1)} %get-tuple-element.28), channel_id=1, source_target_pairs={{0,28},{4,0},{8,4},{12,8},{16,12},{20,16},{24,20},{28,24},{1,29},{... | collective-permute-start | bytes 393224 | tf_op jit(solution)/shard_map/ppermute | solution.py:373
  20.1 4.7 %collective-permute-start.4 = (f32[18,8,128]{2,1,0:T(8,128)S(1)}, f32[18,8,128]{2,1,0:T(8,128)S(1)}, u32[]{:S(2)}, u32[]{:S(2)}) collective-permute-start(f32[18,8,128]{2,1,0:T(8,128)S(1)} %get-tuple-element.27), channel_id=1, source_target_pairs={{0,4},{4,8},{8,12},{12,16},{16,20},{20,24},{24,28},{28,0},{1,5},{5... | collective-permute-start | bytes 221192 | tf_op jit(solution)/shard_map/ppermute | solution.py:373
  25.1 5.1 %collective-permute-start.6 = (f32[18,8,128]{2,1,0:T(8,128)S(1)}, f32[18,8,128]{2,1,0:T(8,128)S(1)}, u32[]{:S(2)}, u32[]{:S(2)}) collective-permute-start(f32[18,8,128]{2,1,0:T(8,128)S(1)} %get-tuple-element.31), channel_id=1, source_target_pairs={{0,4},{4,8},{8,12},{12,16},{16,20},{20,24},{24,28},{28,0},{1,5},{5... | collective-permute-start | bytes 221192 | tf_op jit(solution)/shard_map/ppermute | solution.py:373
  25.2 5.1 %collective-permute-start.7 = (f32[18,8,128]{2,1,0:T(8,128)S(1)}, f32[18,8,128]{2,1,0:T(8,128)S(1)}, u32[]{:S(2)}, u32[]{:S(2)}) collective-permute-start(f32[18,8,128]{2,1,0:T(8,128)S(1)} %get-tuple-element.32), channel_id=1, source_target_pairs={{0,28},{4,0},{8,4},{12,8},{16,12},{20,16},{24,20},{28,24},{1,29},{... | collective-permute-start | bytes 221192 | tf_op jit(solution)/shard_map/ppermute | solution.py:373
  27.8 6.0 %copy-start = (bf16[81,8,1,4,128]{4,3,2,1,0:T(4,128)(2,1)S(1)}, bf16[81,8,1,4,128]{4,3,2,1,0:T(4,128)(2,1)}, u32[]{:S(2)}) copy-start(bf16[81,8,1,4,128]{4,3,2,1,0:T(4,128)(2,1)} %param.11) | copy-start | bytes 1990660
  30.2 3.6 %copy-start.5 = (f32[8,1,4,128]{3,2,1,0:T(4,128)S(1)}, f32[8,1,4,128]{3,2,1,0:T(4,128)}, u32[]{:S(2)}) copy-start(f32[8,1,4,128]{3,2,1,0:T(4,128)} %param.13) | copy-start | bytes 49156
  31.1 2.7 %copy-start.3 = (f32[8,1,4,128]{3,2,1,0:T(4,128)S(1)}, f32[8,1,4,128]{3,2,1,0:T(4,128)}, u32[]{:S(2)}) copy-start(f32[8,1,4,128]{3,2,1,0:T(4,128)} %param.9) | copy-start | bytes 49156
  31.1 2.7 %copy-start.4 = (f32[8,1,4,128]{3,2,1,0:T(4,128)S(1)}, f32[8,1,4,128]{3,2,1,0:T(4,128)}, u32[]{:S(2)}) copy-start(f32[8,1,4,128]{3,2,1,0:T(4,128)} %param.8) | copy-start | bytes 49156
  31.1 9.8 %all-to-all-start = ((f32[32,1,128]{2,1,0:T(1,128)}), f32[32,1,128]{2,1,0:T(1,128)S(1)}, u32[]{:S(2)}, u32[]{:S(2)}) async-start(f32[32,1,128]{2,1,0:T(1,128)} %bitcast.6), calls=%async_computation | async-start | bytes 32768 | tf_op jit(solution)/shard_map/all_to_all | solution.py:435
  33.8 0.7 %copy-start.6 = (s32[1,4,128]{2,1,0:T(4,128)S(1)}, s32[1,4,128]{2,1,0:T(4,128)}, u32[]{:S(2)}) copy-start(s32[1,4,128]{2,1,0:T(4,128)} %param.10) | copy-start | bytes 6148

commit v2 on v1

--- a/solution.py
+++ b/solution.py
@@ -108,9 +108,9 @@
                 value = value - GRAVITY * gravity[n]
             field[r] = value
             if n // 9 == 0:
-                to_left[9 * comp + n] = value
+                to_left[9 * comp + n] = value.astype(BF16)
             if n // 9 == 2:
-                to_right[9 * comp + n - 18] = value
+                to_right[9 * comp + n - 18] = value.astype(BF16)
 
 
 def spread_kernel(velocity, out):
@@ -139,9 +139,9 @@
             r = 27 * comp + n
             value = field[r]
             if n // 9 == 0:
-                value = value + from_left[9 * comp + n]
+                value = value + from_left[9 * comp + n].astype(F32)
             if n // 9 == 2:
-                value = value + from_right[9 * comp + n - 18]
+                value = value + from_right[9 * comp + n - 18].astype(F32)
             out[r] = value
             to_low[r] = value[:HALO].astype(BF16)
             to_high[r] = value[OWN - HALO :].astype(BF16)
@@ -158,8 +158,8 @@
     slot = 0
     for b in range(2):
         for c in range(3):
-            to_left[6 * comp + slot] = values[3 * b + c]
-            to_right[6 * comp + slot] = values[18 + 3 * b + c]
+            to_left[6 * comp + slot] = values[3 * b + c].astype(BF16)
+            to_right[6 * comp + slot] = values[18 + 3 * b + c].astype(BF16)
             slot += 1
 
 
@@ -205,7 +205,7 @@
                 plane += speed
     for n in range(0, 27, 2):
         upper = plane[n] if n == 26 else pltpu.roll(plane[n + 1], 4, 0)
-        to_left[18 + n // 2] = jnp.where(row < OWN, plane[n], upper)
+        to_left[18 + n // 2] = jnp.where(row < OWN, plane[n], upper).astype(BF16)
 
 
 def take_planes(image, from_left, from_right, comp):
@@ -213,8 +213,8 @@
     slot = 0
     for b in range(2):
         for c in range(3):
-            values[3 * b + c] = values[3 * b + c] + from_left[6 * comp + slot]
-            values[18 + 3 * b + c] = values[18 + 3 * b + c] + from_right[6 * comp + slot]
+            values[3 * b + c] = values[3 * b + c] + from_left[6 * comp + slot].astype(F32)
+            values[18 + 3 * b + c] = values[18 + 3 * b + c] + from_right[6 * comp + slot].astype(F32)
             slot += 1
     for a in (0, 18):
         for c in range(3):
@@ -243,7 +243,7 @@
                 speed = speeds[18 * comp + n, :OWN]
             else:
                 k = 9 * comp + n - 18
-                speed = from_right[18 + k // 2, OWN * (k % 2) : OWN * (k % 2) + OWN]
+                speed = from_right[18 + k // 2].astype(F32)[OWN * (k % 2) : OWN * (k % 2) + OWN]
             work = work + geometry[pl.ds(8 * (27 * comp + n), 8)].astype(F32) * speed[None]
     out[...] = energy[...] + HALF_STEP * pressure * work / energy_mass[...]
 
@@ -280,12 +280,13 @@
         for q in range(27):
             quadratic = quadratic + points[q] * points[q] * weight[q]
     row = lax.broadcasted_iota(jnp.int32, (8, 128), 0)
-    lane = lane_of((1, 128))
     mine = (row >= HALO) & (row < HALO + OWN)
-    line = jnp.zeros((1, 128), F32)
+    sums = jnp.zeros((8, 128), F32)
     for k, total in enumerate([products[0], products[1], products[2], cross, norm, quadratic]):
         total = jnp.sum(jnp.where(mine, total, 0.0), axis=0, keepdims=True)
-        line = jnp.where(lane == k, jnp.sum(total, axis=1, keepdims=True), line)
+        sums = jnp.where(row == k, total, sums)
+    sums = jnp.sum(sums, axis=1, keepdims=True)
+    line = jnp.sum(jnp.where(lane_of((8, 128)) == row, sums, 0.0), axis=0, keepdims=True)
     moments[...] = jnp.broadcast_to(line, moments.shape)
 
 
@@ -398,6 +399,7 @@
             pltpu.SemaphoreType.DMA((7,)),
         ],
         place=pl.BlockSpec(memory_space=pltpu.HBM),
+        dtypes=[F32, BF16, BF16],
     )
     (spread,) = call(spread_kernel, [(36,) + full], velocity)
     from_right = shift(to_left, "slab", -1)
@@ -415,6 +417,7 @@
         [(81,) + full, (27,) + full, (81,) + full, (32,) + full, (18,) + full, (54,) + full],
         own, from_low, from_high, mass_weight, spread,
         scratch=[pltpu.VMEM((81,) + full, F32)],
+        dtypes=[F32, F32, F32, BF16, BF16, F32],
     )
     from_right = shift(to_left, "slab", -1)
     from_left = shift(to_right, "slab", 1)
@@ -422,6 +425,7 @@
         second_kernel,
         [(81,) + full, (81,) + full, (18,) + full, (18,) + full],
         image, from_left, from_right, weight,
+        dtypes=[F32, F32, BF16, BF16],
     )
     (energy_half,) = call(
         work_kernel, [(8,) + tile], geometry, density, energy, material, energy_mass, speeds, from_right
@@ -432,6 +436,7 @@
     second, moments = call(
         moment_kernel, [(81,) + full, (devices, 128)], image, from_left, from_right, weight, first, products
     )
+    moments = pltpu.with_memory_space_constraint(moments, pltpu.VMEM)
     moments = lax.all_to_all(moments, ("slab", "brick"), 0, 0, tiled=True)
     (nodal,) = call(nodal_kernel, [(3, 48, 384)], zeroth, first, second)
     (velocity_half,) = call(last_kernel, [velocity.shape], moments, nodal, velocity)

time: 41.9 us -> 40.7 us (0.971)
  waiting for transfers between devices: 19.2 us -> 17.7 us
    ppermute x8, waiting for transfers between devices: 14.6 us -> 13.1 us  [shift(): return lax.ppermute(x, axis, [(i, (i + by) % count) for i in range(count)])]
  transfers between devices with their start and end apart: 9 -> 9, of which waited for: 5 -> 6; matrix products, arithmetic and copies ran while one was open for 0% -> 0% of each run, Pallas kernels for 5% -> 5%
where the time goes in v2:
time: 40.7 us; the launch traced here: 40.5 us
  waiting for transfers between devices  17.7 us (43%)
  starting transfers between devices  15.1 us (37%)
  Pallas kernels  6.21 us (15%)
  between operations  0.73 us (2%)
  local copies, waits for them, and re-layouts  0.66 us (2%)
    ppermute x8, waiting for transfers between devices, shift(): return lax.ppermute(x, axis, [(i, (i + by) % count) for i in range(count)])  13.1 us
    ppermute x8, starting transfers between devices, shift(): return lax.ppermute(x, axis, [(i, (i + by) % count) for i in range(count)])  12.1 us
    pallas_call x10, Pallas kernels, call(): pl.pallas_call(kernel, out_shape=shapes, in_specs=[place] * len(args), ou...  6.21 us
    all_to_all x1, waiting for transfers between devices, local(): moments = lax.all_to_all(moments, ('slab', 'brick'), 0, 0, tiled=True)  4.62 us
    all_to_all x1, starting transfers between devices, local(): moments = lax.all_to_all(moments, ('slab', 'brick'), 0, 0, tiled=True)  3.02 us
  transfers between devices with their start and end apart: 9, of which 6 were waited for; matrix products, arithmetic and copies ran while one was open for 0% of the time, Pallas kernels for 5%

profile of v2, /device:TPU:0, one launch (start us, length us, event | category | flops | bytes accessed | tf_op | source)
XLA Modules:
  0.0 40.5 jit_solution(237562531464900084)
XLA Ops:
  0.6 0.0 copy-start.2
  0.6 1.5 %force_kernel.1 = (f32[81,4,128]{2,1,0:T(4,128)S(1)}, bf16[27,4,128]{2,1,0:T(4,128)(2,1)S(1)}, bf16[27,4,128]{2,1,0:T(4,128)(2,1)S(1)}) custom-call(bf16[648,4,128]{2,1,0:T(4,128)(2,1)} %bitcast.13, f32[8,4,128]{2,1,0:T(4,128)} %bitcast.18, f32[8,4,128]{2,1,0:T(4,128)} %bitcast.20, s32[4,128]{1,0:T(4,128)} %bitcast.24, f32[27,4,128]{2,1,0:T(4,128)} %bitcast.15), custom_call_target="tpu_custom_call" | custom-call | flops 100000 | bytes 1030144 | tf_op jit(solution)/shard_map/force_kernel/pallas_call | solution.py:360
  2.1 0.5 %collective-permute-start = (bf16[27,4,128]{2,1,0:T(4,128)(2,1)S(1)}, bf16[27,4,128]{2,1,0:T(4,128)(2,1)S(1)}, u32[]{:S(2)}, u32[]{:S(2)}) collective-permute-start(bf16[27,4,128]{2,1,0:T(4,128)(2,1)S(1)} %get-tuple-element.21), channel_id=1, source_target_pairs={{0,4},{4,8},{8,12},{12,16},{16,20},{20,24},{24,28},{28,0},{1,5},{5... | collective-permute-start | bytes 82952 | tf_op jit(solution)/shard_map/ppermute | solution.py:374
  2.6 3.0 %collective-permute-start.1 = (bf16[27,4,128]{2,1,0:T(4,128)(2,1)S(1)}, bf16[27,4,128]{2,1,0:T(4,128)(2,1)S(1)}, u32[]{:S(2)}, u32[]{:S(2)}) collective-permute-start(bf16[27,4,128]{2,1,0:T(4,128)(2,1)S(1)} %get-tuple-element.22), channel_id=1, source_target_pairs={{0,28},{4,0},{8,4},{12,8},{16,12},{20,16},{24,20},{28,24},{1,29},{... | collective-permute-start | bytes 82952 | tf_op jit(solution)/shard_map/ppermute | solution.py:374
  5.6 0.0 copy-done.2
  5.6 0.3 spread_kernel.1.spread
  5.9 1.2 %collective-permute-done.from_left = bf16[27,4,128]{2,1,0:T(4,128)(2,1)S(1)} collective-permute-done((bf16[27,4,128]{2,1,0:T(4,128)(2,1)S(1)}, bf16[27,4,128]{2,1,0:T(4,128)(2,1)S(1)}, u32[]{:S(2)}, u32[]{:S(2)}) %collective-permute-start) | collective-permute-done | bytes 27680 | tf_op jit(solution)/shard_map/ppermute | solution.py:374
  7.1 0.1 collective-permute-done.1.from_right
  7.1 0.1 rim_kernel.1
  7.3 4.3 %collective-permute-start.3 = (bf16[126,2,128]{2,1,0:T(2,128)(2,1)S(1)}, bf16[126,2,128]{2,1,0:T(2,128)(2,1)S(1)}, u32[]{:S(2)}, u32[]{:S(2)}) collective-permute-start(bf16[126,2,128]{2,1,0:T(2,128)(2,1)S(1)} %get-tuple-element.25), channel_id=1, source_target_pairs={{0,3},{1,0},{2,1},{3,2},{4,7},{5,4},{6,5},{7,6},{8,11},{9,8},{10,9... | collective-permute-start | bytes 193544 | tf_op jit(solution)/shard_map/ppermute | solution.py:374
  11.6 0.0 collective-permute-start.2
  11.6 6.0 %collective-permute-done.2.from_low = bf16[108,2,128]{2,1,0:T(2,128)(2,1)S(1)} collective-permute-done((bf16[108,2,128]{2,1,0:T(2,128)(2,1)S(1)}, bf16[108,2,128]{2,1,0:T(2,128)(2,1)S(1)}, u32[]{:S(2)}, u32[]{:S(2)}) %collective-permute-start.2) | collective-permute-done | bytes 55328 | tf_op jit(solution)/shard_map/ppermute | solution.py:374
  17.6 0.0 collective-permute-done.3.from_high
  17.6 0.5 %first_kernel.1 = (f32[81,8,128]{2,1,0:T(8,128)S(1)}, f32[27,8,128]{2,1,0:T(8,128)S(1)}, f32[81,8,128]{2,1,0:T(8,128)S(1)}, bf16[32,8,128]{2,1,0:T(8,128)(2,1)S(...) custom-call(f32[81,4,128]{2,1,0:T(4,128)S(1)} %get-tuple-element.23.own, ...), custom_call_target="tpu_custom_call" | custom-call | flops 100000 | bytes 1688576 | tf_op jit(solution)/shard_map/first_kernel/pallas_call | solution.py:360
  18.1 1.6 %collective-permute-start.5 = (bf16[32,8,128]{2,1,0:T(8,128)(2,1)S(1)}, bf16[32,8,128]{2,1,0:T(8,128)(2,1)S(1)}, u32[]{:S(2)}, u32[]{:S(2)}) collective-permute-start(bf16[32,8,128]{2,1,0:T(8,128)(2,1)S(1)} %get-tuple-element.28), channel_id=1, source_target_pairs={{0,28},{4,0},{8,4},{12,8},{16,12},{20,16},{24,20},{28,24},{1,29},{... | collective-permute-start | bytes 196616 | tf_op jit(solution)/shard_map/ppermute | solution.py:374
  19.7 0.0 collective-permute-start.4
  19.7 4.3 %collective-permute-done.4.from_left = bf16[18,8,128]{2,1,0:T(8,128)(2,1)S(1)} collective-permute-done((bf16[18,8,128]{2,1,0:T(8,128)(2,1)S(1)}, bf16[18,8,128]{2,1,0:T(8,128)(2,1)S(1)}, u32[]{:S(2)}, u32[]{:S(2)}) %collective-permute-start.4) | collective-permute-done | bytes 36896 | tf_op jit(solution)/shard_map/ppermute | solution.py:374
  24.0 0.0 collective-permute-done.5.from_right
  24.0 0.3 second_kernel.1
  24.4 0.1 collective-permute-start.6
  24.4 2.6 %collective-permute-start.7 = (bf16[18,8,128]{2,1,0:T(8,128)(2,1)S(1)}, bf16[18,8,128]{2,1,0:T(8,128)(2,1)S(1)}, u32[]{:S(2)}, u32[]{:S(2)}) collective-permute-start(bf16[18,8,128]{2,1,0:T(8,128)(2,1)S(1)} %get-tuple-element.32), channel_id=1, source_target_pairs={{0,28},{4,0},{8,4},{12,8},{16,12},{20,16},{24,20},{28,24},{1,29},{... | collective-permute-start | bytes 110600 | tf_op jit(solution)/shard_map/ppermute | solution.py:374
  27.1 0.1 product_kernel.1.products
  27.1 1.6 %collective-permute-done.6.from_left = bf16[18,8,128]{2,1,0:T(8,128)(2,1)S(1)} collective-permute-done((bf16[18,8,128]{2,1,0:T(8,128)(2,1)S(1)}, bf16[18,8,128]{2,1,0:T(8,128)(2,1)S(1)}, u32[]{:S(2)}, u32[]{:S(2)}) %collective-permute-start.6) | collective-permute-done | bytes 36896 | tf_op jit(solution)/shard_map/ppermute | solution.py:374
  28.7 0.0 collective-permute-done.7.from_right
  28.7 0.9 %moment_kernel.1 = (f32[81,8,128]{2,1,0:T(8,128)S(1)}, f32[32,128]{1,0:T(8,128)}) custom-call(f32[81,8,128]{2,1,0:T(8,128)S(1)} %get-tuple-element.30.image, bf16[18,8,128]{2,1,0:T(8,128)(2,1)S(1)} %collective-permute-done.6.from_left, bf16[18,8,128]{2,1,0:T(8,128)(2,1)S(1)} %collective-permute-done.7.from_right, ...), custom_call_target="tpu_custom_call" | custom-call | flops 100000 | bytes 1208320 | tf_op jit(solution)/shard_map/moment_kernel/pallas_call | solution.py:360
  29.6 3.0 %all-to-all-start = ((f32[32,1,128]{2,1,0:T(1,128)}), f32[32,1,128]{2,1,0:T(1,128)S(1)}, u32[]{:S(2)}, u32[]{:S(2)}) async-start(f32[32,1,128]{2,1,0:T(1,128)} %bitcast.6), calls=%async_computation | async-start | bytes 32768 | tf_op jit(solution)/shard_map/all_to_all | solution.py:440
  32.6 0.0 copy-start.6
  32.7 0.6 %copy-done.6 = s32[1,4,128]{2,1,0:T(4,128)S(1)} copy-done((s32[1,4,128]{2,1,0:T(4,128)S(1)}, s32[1,4,128]{2,1,0:T(4,128)}, u32[]{:S(2)}) %copy-start.6) | copy-done | bytes 2072
  33.3 1.0 %work_kernel.1 = f32[8,4,128]{2,1,0:T(4,128)} custom-call(bf16[648,4,128]{2,1,0:T(4,128)(2,1)S(1)} %bitcast.14, f32[8,4,128]{2,1,0:T(4,128)S(1)} %bitcast.19, f32[8,4,128]{2,1,0:T(4,128)S(1)} %bitcast.21, s32[4,128]{1,0:T(4,128)S(1)} %bitcast.25, f32[8,4,128]{2,1,0:T(4,128)S(1)} %bitcast.23, f32[54,8,128]{2,1,0:T(8,128)S(1)} %get-tuple-element.37.speeds, ...), custom_call_target="tpu_custom_call" | custom-call | flops 100000 | bytes 1017856 | tf_op jit(solution)/shard_map/work_kernel/pallas_call | solution.py:360
  34.3 0.8 %nodal_kernel.1.nodal = f32[3,48,384]{2,1,0:T(8,128)S(1)} custom-call(f32[81,8,128]{2,1,0:T(8,128)S(1)} %get-tuple-element.34.zeroth, f32[81,8,128]{2,1,0:T(8,128)S(1)} %get-tuple-element.33.first, f32[81,8,128]{2,1,0:T(8,128)S(1)} %get-tuple-element.36.second), custom_call_target="tpu_custom_call" | custom-call | flops 100000 | bytes 1216512 | tf_op jit(solution)/shard_map/nodal_kernel/pallas_call | solution.py:360
  35.1 4.6 %all-to-all-done = f32[32,1,128]{2,1,0:T(1,128)S(1)} async-done(((f32[32,1,128]{2,1,0:T(1,128)}), f32[32,1,128]{2,1,0:T(1,128)S(1)}, u32[]{:S(2)}, u32[]{:S(2)}) %all-to-all-start) | async-done | bytes 16416 | tf_op jit(solution)/shard_map/all_to_all | solution.py:440
  39.7 0.8 %last_kernel.1 = f32[3,2,8,257]{3,2,1,0:T(8,128)} custom-call(f32[32,128]{1,0:T(8,128)S(1)} %bitcast.22, f32[3,48,384]{2,1,0:T(8,128)S(1)} %nodal_kernel.1.nodal, f32[3,2,8,257]{3,2,1,0:T(8,128)S(1)} %copy-done.2), custom_call_target="tpu_custom_call" | custom-call | flops 100000 | bytes 336256 | tf_op jit(solution)/shard_map/last_kernel/pallas_call | solution.py:360
  (10 shorter events, 0.0 us)
Async XLA Ops:
  0.6 5.0 %copy-start.2 = (f32[3,2,8,257]{3,2,1,0:T(8,128)S(1)}, f32[3,2,8,257]{3,2,1,0:T(8,128)}, u32[]{:S(2)}) copy-start(f32[3,2,8,257]{3,2,1,0:T(8,128)} %velocity.3) | copy-start | bytes 148036
  2.1 4.9 %collective-permute-start = (bf16[27,4,128]{2,1,0:T(4,128)(2,1)S(1)}, bf16[27,4,128]{2,1,0:T(4,128)(2,1)S(1)}, u32[]{:S(2)}, u32[]{:S(2)}) collective-permute-start(bf16[27,4,128]{2,1,0:T(4,128)(2,1)S(1)} %get-tuple-element.21), channel_id=1, source_target_pairs={{0,4},{4,8},{8,12},{12,16},{16,20},{20,24},{24,28},{28,0},{1,5},{5... | collective-permute-start | bytes 82952 | tf_op jit(solution)/shard_map/ppermute | solution.py:374
  2.6 4.5 %copy-start.1 = (f32[27,1,4,128]{3,2,1,0:T(4,128)S(1)}, f32[27,1,4,128]{3,2,1,0:T(4,128)}, u32[]{:S(2)}) copy-start(f32[27,1,4,128]{3,2,1,0:T(4,128)} %param.12) | copy-start | bytes 165892
  2.6 4.5 %collective-permute-start.1 = (bf16[27,4,128]{2,1,0:T(4,128)(2,1)S(1)}, bf16[27,4,128]{2,1,0:T(4,128)(2,1)S(1)}, u32[]{:S(2)}, u32[]{:S(2)}) collective-permute-start(bf16[27,4,128]{2,1,0:T(4,128)(2,1)S(1)} %get-tuple-element.22), channel_id=1, source_target_pairs={{0,28},{4,0},{8,4},{12,8},{16,12},{20,16},{24,20},{28,24},{1,29},{... | collective-permute-start | bytes 82952 | tf_op jit(solution)/shard_map/ppermute | solution.py:374
  7.3 10.3 %collective-permute-start.3 = (bf16[126,2,128]{2,1,0:T(2,128)(2,1)S(1)}, bf16[126,2,128]{2,1,0:T(2,128)(2,1)S(1)}, u32[]{:S(2)}, u32[]{:S(2)}) collective-permute-start(bf16[126,2,128]{2,1,0:T(2,128)(2,1)S(1)} %get-tuple-element.25), channel_id=1, source_target_pairs={{0,3},{1,0},{2,1},{3,2},{4,7},{5,4},{6,5},{7,6},{8,11},{9,8},{10,9... | collective-permute-start | bytes 193544 | tf_op jit(solution)/shard_map/ppermute | solution.py:374
  11.6 6.0 %collective-permute-start.2 = (bf16[108,2,128]{2,1,0:T(2,128)(2,1)S(1)}, bf16[108,2,128]{2,1,0:T(2,128)(2,1)S(1)}, u32[]{:S(2)}, u32[]{:S(2)}) collective-permute-start(bf16[108,2,128]{2,1,0:T(2,128)(2,1)S(1)} %get-tuple-element.24), channel_id=1, source_target_pairs={{0,1},{1,2},{2,3},{3,0},{4,5},{5,6},{6,7},{7,4},{8,9},{9,10},{10,1... | collective-permute-start | bytes 165896 | tf_op jit(solution)/shard_map/ppermute | solution.py:374
  18.1 5.9 %collective-permute-start.5 = (bf16[32,8,128]{2,1,0:T(8,128)(2,1)S(1)}, bf16[32,8,128]{2,1,0:T(8,128)(2,1)S(1)}, u32[]{:S(2)}, u32[]{:S(2)}) collective-permute-start(bf16[32,8,128]{2,1,0:T(8,128)(2,1)S(1)} %get-tuple-element.28), channel_id=1, source_target_pairs={{0,28},{4,0},{8,4},{12,8},{16,12},{20,16},{24,20},{28,24},{1,29},{... | collective-permute-start | bytes 196616 | tf_op jit(solution)/shard_map/ppermute | solution.py:374
  19.7 4.3 %collective-permute-start.4 = (bf16[18,8,128]{2,1,0:T(8,128)(2,1)S(1)}, bf16[18,8,128]{2,1,0:T(8,128)(2,1)S(1)}, u32[]{:S(2)}, u32[]{:S(2)}) collective-permute-start(bf16[18,8,128]{2,1,0:T(8,128)(2,1)S(1)} %get-tuple-element.27), channel_id=1, source_target_pairs={{0,4},{4,8},{8,12},{12,16},{16,20},{20,24},{24,28},{28,0},{1,5},{5... | collective-permute-start | bytes 110600 | tf_op jit(solution)/shard_map/ppermute | solution.py:374
  24.4 4.3 %collective-permute-start.6 = (bf16[18,8,128]{2,1,0:T(8,128)(2,1)S(1)}, bf16[18,8,128]{2,1,0:T(8,128)(2,1)S(1)}, u32[]{:S(2)}, u32[]{:S(2)}) collective-permute-start(bf16[18,8,128]{2,1,0:T(8,128)(2,1)S(1)} %get-tuple-element.31), channel_id=1, source_target_pairs={{0,4},{4,8},{8,12},{12,16},{16,20},{20,24},{24,28},{28,0},{1,5},{5... | collective-permute-start | bytes 110600 | tf_op jit(solution)/shard_map/ppermute | solution.py:374
  24.4 4.3 %collective-permute-start.7 = (bf16[18,8,128]{2,1,0:T(8,128)(2,1)S(1)}, bf16[18,8,128]{2,1,0:T(8,128)(2,1)S(1)}, u32[]{:S(2)}, u32[]{:S(2)}) collective-permute-start(bf16[18,8,128]{2,1,0:T(8,128)(2,1)S(1)} %get-tuple-element.32), channel_id=1, source_target_pairs={{0,28},{4,0},{8,4},{12,8},{16,12},{20,16},{24,20},{28,24},{1,29},{... | collective-permute-start | bytes 110600 | tf_op jit(solution)/shard_map/ppermute | solution.py:374
  27.1 5.6 %copy-start = (bf16[81,8,1,4,128]{4,3,2,1,0:T(4,128)(2,1)S(1)}, bf16[81,8,1,4,128]{4,3,2,1,0:T(4,128)(2,1)}, u32[]{:S(2)}) copy-start(bf16[81,8,1,4,128]{4,3,2,1,0:T(4,128)(2,1)} %param.11) | copy-start | bytes 1990660
  28.7 3.9 %copy-start.5 = (f32[8,1,4,128]{3,2,1,0:T(4,128)S(1)}, f32[8,1,4,128]{3,2,1,0:T(4,128)}, u32[]{:S(2)}) copy-start(f32[8,1,4,128]{3,2,1,0:T(4,128)} %param.13) | copy-start | bytes 49156
  29.6 3.1 %copy-start.3 = (f32[8,1,4,128]{3,2,1,0:T(4,128)S(1)}, f32[8,1,4,128]{3,2,1,0:T(4,128)}, u32[]{:S(2)}) copy-start(f32[8,1,4,128]{3,2,1,0:T(4,128)} %param.9) | copy-start | bytes 49156
  29.6 3.1 %copy-start.4 = (f32[8,1,4,128]{3,2,1,0:T(4,128)S(1)}, f32[8,1,4,128]{3,2,1,0:T(4,128)}, u32[]{:S(2)}) copy-start(f32[8,1,4,128]{3,2,1,0:T(4,128)} %param.8) | copy-start | bytes 49156
  29.6 10.1 %all-to-all-start = ((f32[32,1,128]{2,1,0:T(1,128)}), f32[32,1,128]{2,1,0:T(1,128)S(1)}, u32[]{:S(2)}, u32[]{:S(2)}) async-start(f32[32,1,128]{2,1,0:T(1,128)} %bitcast.6), calls=%async_computation | async-start | bytes 32768 | tf_op jit(solution)/shard_map/all_to_all | solution.py:440
  32.6 0.7 %copy-start.6 = (s32[1,4,128]{2,1,0:T(4,128)S(1)}, s32[1,4,128]{2,1,0:T(4,128)}, u32[]{:S(2)}) copy-start(s32[1,4,128]{2,1,0:T(4,128)} %param.10) | copy-start | bytes 6148

commit v3 on v2

--- a/solution.py
+++ b/solution.py
@@ -74,9 +74,23 @@
     return values
 
 
+def is_even():
+    return lax.axis_index("slab") % 2 == 0
+
+
+def put(near, far, slot, left, right, even):
+    near[slot] = jnp.where(even, right, left).astype(BF16)
+    far[slot] = jnp.where(even, left, right).astype(BF16)
+
+
+def get(near, far, slot, even):
+    one, other = near[slot].astype(F32), far[slot].astype(F32)
+    return jnp.where(even, other, one), jnp.where(even, one, other)
+
+
 def force_kernel(
     geometry_in, density_in, energy_in, material_in, mass_weight_in,
-    field, to_left, to_right,
+    field, near, far,
     geometry, density, energy, material, mass_weight, sems,
 ):
     small = [
@@ -98,8 +112,10 @@
     gamma = jnp.where(material[...] == 0, 2.0 / 3.0, 0.4).astype(F32)
     pressure = (gamma[None] * density[...] * energy[...]).astype(BF16).astype(F32)
     gravity = from_points([mass_weight[q] * POINT_WEIGHT[q] for q in range(27)])
+    even = is_even()
     for comp in range(3):
         parts[comp].wait()
+        values = []
         for n in range(27):
             r = 27 * comp + n
             block = geometry[pl.ds(8 * r, 8)].astype(F32)
@@ -107,10 +123,9 @@
             if comp == 2:
                 value = value - GRAVITY * gravity[n]
             field[r] = value
-            if n // 9 == 0:
-                to_left[9 * comp + n] = value.astype(BF16)
-            if n // 9 == 2:
-                to_right[9 * comp + n - 18] = value.astype(BF16)
+            values.append(value)
+        for n in range(9):
+            put(near, far, 9 * comp + n, values[n], values[18 + n], even)
 
 
 def spread_kernel(velocity, out):
@@ -133,18 +148,19 @@
             out[3 * group + c] = moved[8 * group : 8 * group + 8, 128 * c : 128 * c + 128]
 
 
-def rim_kernel(field, from_left, from_right, mass_weight, spread, out, to_low, to_high):
-    for comp in range(3):
+def rim_kernel(field, near, far, mass_weight, spread, out, to_low, to_high):
+    even = is_even()
+    for comp in range(3):
+        values = [field[27 * comp + n] for n in range(27)]
+        for n in range(9):
+            left, right = get(near, far, 9 * comp + n, even)
+            values[n] = values[n] + left
+            values[18 + n] = values[18 + n] + right
         for n in range(27):
             r = 27 * comp + n
-            value = field[r]
-            if n // 9 == 0:
-                value = value + from_left[9 * comp + n].astype(F32)
-            if n // 9 == 2:
-                value = value + from_right[9 * comp + n - 18].astype(F32)
-            out[r] = value
-            to_low[r] = value[:HALO].astype(BF16)
-            to_high[r] = value[OWN - HALO :].astype(BF16)
+            out[r] = values[n]
+            to_low[r] = values[n][:HALO].astype(BF16)
+            to_high[r] = values[n][OWN - HALO :].astype(BF16)
     for q in range(27):
         to_low[81 + q] = mass_weight[q, :HALO].astype(BF16)
         to_high[81 + q] = mass_weight[q, OWN - HALO :].astype(BF16)
@@ -154,13 +170,11 @@
                 to_low[108 + 6 * comp + 3 * a + c] = spread[12 * comp + 6 * a + c, :HALO].astype(BF16)
 
 
-def send_planes(values, comp, to_left, to_right):
-    slot = 0
+def send_planes(values, comp, near, far, even):
     for b in range(2):
         for c in range(3):
-            to_left[6 * comp + slot] = values[3 * b + c].astype(BF16)
-            to_right[6 * comp + slot] = values[18 + 3 * b + c].astype(BF16)
-            slot += 1
+            n = 3 * b + c
+            put(near, far, 6 * comp + n, values[n], values[18 + n], even)
 
 
 def apply_mass(values, weight, wall):
@@ -170,8 +184,9 @@
 
 
 def first_kernel(
-    own, from_low, from_high, mass_weight, spread, field, weight, image, to_left, to_right, speeds, rows
+    own, from_low, from_high, mass_weight, spread, field, weight, image, near, far, speeds, rows
 ):
+    even = is_even()
     for q in range(27):
         rows[q, :HALO] = from_low[81 + q].astype(F32)
         rows[q, HALO : HALO + OWN] = mass_weight[q]
@@ -190,7 +205,7 @@
         values = apply_mass(values, weight, comp == 2)
         for n in range(27):
             image[27 * comp + n] = values[n]
-        send_planes(values, comp, to_left, to_right)
+        send_planes(values, comp, near, far, even)
     row = lax.broadcasted_iota(jnp.int32, (8, 128), 0)
     plane = []
     for comp in range(3):
@@ -205,35 +220,39 @@
                 plane += speed
     for n in range(0, 27, 2):
         upper = plane[n] if n == 26 else pltpu.roll(plane[n + 1], 4, 0)
-        to_left[18 + n // 2] = jnp.where(row < OWN, plane[n], upper).astype(BF16)
-
-
-def take_planes(image, from_left, from_right, comp):
+        both = jnp.where(row < OWN, plane[n], upper).astype(BF16)
+        near[18 + n // 2] = both
+        far[18 + n // 2] = both
+
+
+def take_planes(image, near, far, comp, even):
     values = [image[27 * comp + n] for n in range(27)]
-    slot = 0
     for b in range(2):
         for c in range(3):
-            values[3 * b + c] = values[3 * b + c] + from_left[6 * comp + slot].astype(F32)
-            values[18 + 3 * b + c] = values[18 + 3 * b + c] + from_right[6 * comp + slot].astype(F32)
-            slot += 1
+            n = 3 * b + c
+            left, right = get(near, far, 6 * comp + n, even)
+            values[n] = values[n] + left
+            values[18 + n] = values[18 + n] + right
     for a in (0, 18):
         for c in range(3):
             values[a + 6 + c] = pltpu.roll(values[a + c], 7, 0)
     return values
 
 
-def second_kernel(image, from_left, from_right, weight, field, image_out, to_left, to_right):
-    for comp in range(3):
-        values = take_planes(image, from_left, from_right, comp)
+def second_kernel(image, near_in, far_in, weight, field, image_out, near, far):
+    even = is_even()
+    for comp in range(3):
+        values = take_planes(image, near_in, far_in, comp, even)
         for n in range(27):
             field[27 * comp + n] = values[n]
         values = apply_mass(values, weight, comp == 2)
         for n in range(27):
             image_out[27 * comp + n] = values[n]
-        send_planes(values, comp, to_left, to_right)
-
-
-def work_kernel(geometry, density, energy, material, energy_mass, speeds, from_right, out):
+        send_planes(values, comp, near, far, even)
+
+
+def work_kernel(geometry, density, energy, material, energy_mass, speeds, near, far, out):
+    even = is_even()
     gamma = jnp.where(material[...] == 0, 2.0 / 3.0, 0.4).astype(F32)
     pressure = (gamma[None] * density[...] * energy[...]).astype(BF16).astype(F32)
     work = jnp.zeros_like(pressure)
@@ -243,7 +262,8 @@
                 speed = speeds[18 * comp + n, :OWN]
             else:
                 k = 9 * comp + n - 18
-                speed = from_right[18 + k // 2].astype(F32)[OWN * (k % 2) : OWN * (k % 2) + OWN]
+                _, speed = get(near, far, 18 + k // 2, even)
+                speed = speed[OWN * (k % 2) : OWN * (k % 2) + OWN]
             work = work + geometry[pl.ds(8 * (27 * comp + n), 8)].astype(F32) * speed[None]
     out[...] = energy[...] + HALF_STEP * pressure * work / energy_mass[...]
 
@@ -266,11 +286,13 @@
         products[k] = total
 
 
-def moment_kernel(image, from_left, from_right, weight, first, products, second, moments):
+def moment_kernel(image, near, far, weight, first, products, second, moments):
     zero = jnp.zeros((8, 128), F32)
-    cross, norm, quadratic = zero, zero, zero
-    for comp in range(3):
-        values = take_planes(image, from_left, from_right, comp)
+    cross, norm = zero, zero
+    quadratic = [zero] * 3
+    even = is_even()
+    for comp in range(3):
+        values = take_planes(image, near, far, comp, even)
         for n in range(27):
             second[27 * comp + n] = values[n]
         values_at = {27 * comp + n: values[n] for n in range(27)}
@@ -278,7 +300,8 @@
         norm = dot_owned(values_at, values_at, comp, norm)
         points = to_points(values)
         for q in range(27):
-            quadratic = quadratic + points[q] * points[q] * weight[q]
+            quadratic[q % 3] = quadratic[q % 3] + points[q] * points[q] * weight[q]
+    quadratic = quadratic[0] + quadratic[1] + quadratic[2]
     row = lax.broadcasted_iota(jnp.int32, (8, 128), 0)
     mine = (row >= HALO) & (row < HALO + OWN)
     sums = jnp.zeros((8, 128), F32)
@@ -374,6 +397,13 @@
     return lax.ppermute(x, axis, [(i, (i + by) % count) for i in range(count)])
 
 
+def swap(near, far):
+    count = lax.axis_size("slab")
+    far = lax.ppermute(far, "slab", [(i, (i + (1 if i % 2 else -1)) % count) for i in range(count)])
+    near = lax.ppermute(near, "slab", [(i, i + (-1 if i % 2 else 1)) for i in range(count)])
+    return near, far
+
+
 def local(velocity, energy, density, material, geometry, mass_weight, energy_mass):
     tile = (4, 128)
     geometry = geometry.reshape((648,) + tile)
@@ -386,7 +416,7 @@
     pair = (2, 128)
     devices = lax.axis_size("slab") * lax.axis_size("brick")
 
-    force, to_left, to_right = call(
+    force, near, far = call(
         force_kernel,
         [(81,) + tile, (27,) + tile, (27,) + tile],
         *[pltpu.with_memory_space_constraint(x, pltpu.HBM) for x in (geometry, density, energy, material, mass_weight)],
@@ -402,39 +432,36 @@
         dtypes=[F32, BF16, BF16],
     )
     (spread,) = call(spread_kernel, [(36,) + full], velocity)
-    from_right = shift(to_left, "slab", -1)
-    from_left = shift(to_right, "slab", 1)
+    near, far = swap(near, far)
     own, to_low, to_high = call(
         rim_kernel,
         [(81,) + tile, (126,) + pair, (108,) + pair],
-        force, from_left, from_right, mass_weight, spread,
+        force, near, far, mass_weight, spread,
         dtypes=[F32, BF16, BF16],
     )
     from_high = shift(to_low, "brick", -1)
     from_low = shift(to_high, "brick", 1)
-    zeroth, weight, image, to_left, to_right, speeds = call(
+    zeroth, weight, image, near, far, speeds = call(
         first_kernel,
-        [(81,) + full, (27,) + full, (81,) + full, (32,) + full, (18,) + full, (54,) + full],
+        [(81,) + full, (27,) + full, (81,) + full, (32,) + full, (32,) + full, (54,) + full],
         own, from_low, from_high, mass_weight, spread,
         scratch=[pltpu.VMEM((81,) + full, F32)],
         dtypes=[F32, F32, F32, BF16, BF16, F32],
     )
-    from_right = shift(to_left, "slab", -1)
-    from_left = shift(to_right, "slab", 1)
-    first, image, to_left, to_right = call(
+    near, far = swap(near, far)
+    first, image, near_out, far_out = call(
         second_kernel,
         [(81,) + full, (81,) + full, (18,) + full, (18,) + full],
-        image, from_left, from_right, weight,
+        image, near, far, weight,
         dtypes=[F32, F32, BF16, BF16],
     )
     (energy_half,) = call(
-        work_kernel, [(8,) + tile], geometry, density, energy, material, energy_mass, speeds, from_right
-    )
-    from_right = shift(to_left, "slab", -1)
-    from_left = shift(to_right, "slab", 1)
+        work_kernel, [(8,) + tile], geometry, density, energy, material, energy_mass, speeds, near, far
+    )
+    near, far = swap(near_out, far_out)
     (products,) = call(product_kernel, [(3,) + full], zeroth, first)
     second, moments = call(
-        moment_kernel, [(81,) + full, (devices, 128)], image, from_left, from_right, weight, first, products
+        moment_kernel, [(81,) + full, (devices, 128)], image, near, far, weight, first, products
     )
     moments = pltpu.with_memory_space_constraint(moments, pltpu.VMEM)
     moments = lax.all_to_all(moments, ("slab", "brick"), 0, 0, tiled=True)

time: 40.7 us -> 39.5 us (0.971)
  waiting for transfers between devices: 17.7 us -> 16.6 us
    ppermute x0 -> x6, starting transfers between devices: none -> 8.48 us  [the longest x3 7.73 us: swap(): lax.ppermute(far, 'slab', [(i, (i + (1 if i % 2 else -1)) % count) for i...]
    ppermute x8 -> x2, starting transfers between devices: 12.1 us -> 3.82 us  [shift(): return lax.ppermute(x, axis, [(i, (i + by) % count) for i in range(count)])]
    ppermute x8 -> x2, waiting for transfers between devices: 13.1 us -> 5.95 us  [shift(): return lax.ppermute(x, axis, [(i, (i + by) % count) for i in range(count)])]
    ppermute x0 -> x6, waiting for transfers between devices: none -> 6.02 us  [the longest x3 6.01 us: swap(): lax.ppermute(far, 'slab', [(i, (i + (1 if i % 2 else -1)) % count) for i...]
  transfers between devices with their start and end apart: 9 -> 9, of which waited for: 6 -> 5; matrix products, arithmetic and copies ran while one was open for 0% -> 0% of each run, Pallas kernels for 5% -> 5%
where the time goes in v3:
time: 39.5 us; the launch traced here: 39.2 us
  waiting for transfers between devices  16.6 us (42%)
  starting transfers between devices  15 us (38%)
  Pallas kernels  6.29 us (16%)
  between operations  0.74 us (2%)
  local copies, waits for them, and re-layouts  0.66 us (2%)
    ppermute x3, starting transfers between devices, swap(): lax.ppermute(far, 'slab', [(i, (i + (1 if i % 2 else -1)) % count) for i...  7.73 us
    pallas_call x10, Pallas kernels, call(): pl.pallas_call(kernel, out_shape=shapes, in_specs=[place] * len(args), ou...  6.29 us
    ppermute x3, waiting for transfers between devices, swap(): lax.ppermute(far, 'slab', [(i, (i + (1 if i % 2 else -1)) % count) for i...  6.01 us
    ppermute x2, waiting for transfers between devices, shift(): return lax.ppermute(x, axis, [(i, (i + by) % count) for i in range(count)])  5.95 us
    all_to_all x1, waiting for transfers between devices, local(): moments = lax.all_to_all(moments, ('slab', 'brick'), 0, 0, tiled=True)  4.61 us
    ppermute x2, starting transfers between devices, shift(): return lax.ppermute(x, axis, [(i, (i + by) % count) for i in range(count)])  3.82 us
    all_to_all x1, starting transfers between devices, local(): moments = lax.all_to_all(moments, ('slab', 'brick'), 0, 0, tiled=True)  2.68 us
  transfers between devices with their start and end apart: 9, of which 5 were waited for; matrix products, arithmetic and copies ran while one was open for 0% of the time, Pallas kernels for 5%

profile of v3, /device:TPU:0, one launch (start us, length us, event | category | flops | bytes accessed | tf_op | source)
XLA Modules:
  0.0 39.2 jit_solution(9119777661334885632)
XLA Ops:
  0.6 0.0 copy-start.2
  0.6 1.5 %force_kernel.1 = (f32[81,4,128]{2,1,0:T(4,128)S(1)}, bf16[27,4,128]{2,1,0:T(4,128)(2,1)S(1)}, bf16[27,4,128]{2,1,0:T(4,128)(2,1)S(1)}) custom-call(bf16[648,4,128]{2,1,0:T(4,128)(2,1)} %bitcast.13, f32[8,4,128]{2,1,0:T(4,128)} %bitcast.18, f32[8,4,128]{2,1,0:T(4,128)} %bitcast.20, s32[4,128]{1,0:T(4,128)} %bitcast.24, f32[27,4,128]{2,1,0:T(4,128)} %bitcast.15), custom_call_target="tpu_custom_call" | custom-call | flops 100000 | bytes 1030144 | tf_op jit(solution)/shard_map/force_kernel/pallas_call | solution.py:383
  2.1 0.5 %collective-permute-start = (bf16[27,4,128]{2,1,0:T(4,128)(2,1)S(1)}, bf16[27,4,128]{2,1,0:T(4,128)(2,1)S(1)}, u32[]{:S(2)}, u32[]{:S(2)}) collective-permute-start(bf16[27,4,128]{2,1,0:T(4,128)(2,1)S(1)} %get-tuple-element.21), channel_id=1, source_target_pairs={{0,4},{4,0},{8,12},{12,8},{16,20},{20,16},{24,28},{28,24},{1,5},{5... | collective-permute-start | bytes 82952 | tf_op jit(solution)/shard_map/ppermute | solution.py:403
  2.7 3.6 %collective-permute-start.1 = (bf16[27,4,128]{2,1,0:T(4,128)(2,1)S(1)}, bf16[27,4,128]{2,1,0:T(4,128)(2,1)S(1)}, u32[]{:S(2)}, u32[]{:S(2)}) collective-permute-start(bf16[27,4,128]{2,1,0:T(4,128)(2,1)S(1)} %get-tuple-element.22), channel_id=1, source_target_pairs={{0,28},{4,8},{8,4},{12,16},{16,12},{20,24},{24,20},{28,0},{1,29},{... | collective-permute-start | bytes 82952 | tf_op jit(solution)/shard_map/ppermute | solution.py:402
  6.2 0.0 copy-done.2
  6.2 0.3 spread_kernel.1.spread
  6.5 0.0 collective-permute-done.near
  6.5 1.2 %collective-permute-done.1.far = bf16[27,4,128]{2,1,0:T(4,128)(2,1)S(1)} collective-permute-done((bf16[27,4,128]{2,1,0:T(4,128)(2,1)S(1)}, bf16[27,4,128]{2,1,0:T(4,128)(2,1)S(1)}, u32[]{:S(2)}, u32[]{:S(2)}) %collective-permute-start.1) | collective-permute-done | bytes 27680 | tf_op jit(solution)/shard_map/ppermute | solution.py:402
  7.8 0.1 rim_kernel.1
  7.9 3.8 %collective-permute-start.3 = (bf16[126,2,128]{2,1,0:T(2,128)(2,1)S(1)}, bf16[126,2,128]{2,1,0:T(2,128)(2,1)S(1)}, u32[]{:S(2)}, u32[]{:S(2)}) collective-permute-start(bf16[126,2,128]{2,1,0:T(2,128)(2,1)S(1)} %get-tuple-element.25), channel_id=1, source_target_pairs={{0,3},{1,0},{2,1},{3,2},{4,7},{5,4},{6,5},{7,6},{8,11},{9,8},{10,9... | collective-permute-start | bytes 193544 | tf_op jit(solution)/shard_map/ppermute | solution.py:397
  11.7 0.0 collective-permute-start.2
  11.7 6.0 %collective-permute-done.2.from_low = bf16[108,2,128]{2,1,0:T(2,128)(2,1)S(1)} collective-permute-done((bf16[108,2,128]{2,1,0:T(2,128)(2,1)S(1)}, bf16[108,2,128]{2,1,0:T(2,128)(2,1)S(1)}, u32[]{:S(2)}, u32[]{:S(2)}) %collective-permute-start.2) | collective-permute-done | bytes 55328 | tf_op jit(solution)/shard_map/ppermute | solution.py:397
  17.6 0.0 collective-permute-done.3.from_high
  17.7 0.5 %first_kernel.1 = (f32[81,8,128]{2,1,0:T(8,128)S(1)}, f32[27,8,128]{2,1,0:T(8,128)S(1)}, f32[81,8,128]{2,1,0:T(8,128)S(1)}, bf16[32,8,128]{2,1,0:T(8,128)(2,1)S(...) custom-call(f32[81,4,128]{2,1,0:T(4,128)S(1)} %get-tuple-element.23.own, ...), custom_call_target="tpu_custom_call" | custom-call | flops 100000 | bytes 1745920 | tf_op jit(solution)/shard_map/first_kernel/pallas_call | solution.py:383
  18.2 0.1 collective-permute-start.4
  18.3 2.2 %collective-permute-start.5 = (bf16[32,8,128]{2,1,0:T(8,128)(2,1)S(1)}, bf16[32,8,128]{2,1,0:T(8,128)(2,1)S(1)}, u32[]{:S(2)}, u32[]{:S(2)}) collective-permute-start(bf16[32,8,128]{2,1,0:T(8,128)(2,1)S(1)} %get-tuple-element.28), channel_id=1, source_target_pairs={{0,28},{4,8},{8,4},{12,16},{16,12},{20,24},{24,20},{28,0},{1,29},{... | collective-permute-start | bytes 196616 | tf_op jit(solution)/shard_map/ppermute | solution.py:402
  20.4 0.0 collective-permute-done.4.near_in.near
  20.4 2.6 %collective-permute-done.5.far_in.far = bf16[32,8,128]{2,1,0:T(8,128)(2,1)S(1)} collective-permute-done((bf16[32,8,128]{2,1,0:T(8,128)(2,1)S(1)}, bf16[32,8,128]{2,1,0:T(8,128)(2,1)S(1)}, u32[]{:S(2)}, u32[]{:S(2)}) %collective-permute-start.5) | collective-permute-done | bytes 65568 | tf_op jit(solution)/shard_map/ppermute | solution.py:402
  23.0 0.4 second_kernel.1
  23.4 0.2 collective-permute-start.6
  23.5 2.0 %collective-permute-start.7 = (bf16[18,8,128]{2,1,0:T(8,128)(2,1)S(1)}, bf16[18,8,128]{2,1,0:T(8,128)(2,1)S(1)}, u32[]{:S(2)}, u32[]{:S(2)}) collective-permute-start(bf16[18,8,128]{2,1,0:T(8,128)(2,1)S(1)} %get-tuple-element.32), channel_id=1, source_target_pairs={{0,28},{4,8},{8,4},{12,16},{16,12},{20,24},{24,20},{28,0},{1,29},{... | collective-permute-start | bytes 110600 | tf_op jit(solution)/shard_map/ppermute | solution.py:402
  25.6 0.1 product_kernel.1.products
  25.6 0.0 collective-permute-done.6.near
  25.6 2.2 %collective-permute-done.7.far = bf16[18,8,128]{2,1,0:T(8,128)(2,1)S(1)} collective-permute-done((bf16[18,8,128]{2,1,0:T(8,128)(2,1)S(1)}, bf16[18,8,128]{2,1,0:T(8,128)(2,1)S(1)}, u32[]{:S(2)}, u32[]{:S(2)}) %collective-permute-start.7) | collective-permute-done | bytes 36896 | tf_op jit(solution)/shard_map/ppermute | solution.py:402
  27.8 0.9 %moment_kernel.1 = (f32[81,8,128]{2,1,0:T(8,128)S(1)}, f32[32,128]{1,0:T(8,128)}) custom-call(f32[81,8,128]{2,1,0:T(8,128)S(1)} %get-tuple-element.30.image, bf16[18,8,128]{2,1,0:T(8,128)(2,1)S(1)} %collective-permute-done.6.near, bf16[18,8,128]{2,1,0:T(8,128)(2,1)S(1)} %collective-permute-done.7.far, f32[27,8,128]{2,1,0:T(8,128)S(1)} %get-tuple-element.29.weight, ...), custom_call_target="tpu_custom_call" | custom-call | flops 100000 | bytes 1208320 | tf_op jit(solution)/shard_map/moment_kernel/pallas_call | solution.py:383
  28.7 2.7 %all-to-all-start = ((f32[32,1,128]{2,1,0:T(1,128)}), f32[32,1,128]{2,1,0:T(1,128)S(1)}, u32[]{:S(2)}, u32[]{:S(2)}) async-start(f32[32,1,128]{2,1,0:T(1,128)} %bitcast.6), calls=%async_computation | async-start | bytes 32768 | tf_op jit(solution)/shard_map/all_to_all | solution.py:467
  31.4 0.0 copy-start.6
  31.4 0.6 %copy-done.6 = s32[1,4,128]{2,1,0:T(4,128)S(1)} copy-done((s32[1,4,128]{2,1,0:T(4,128)S(1)}, s32[1,4,128]{2,1,0:T(4,128)}, u32[]{:S(2)}) %copy-start.6) | copy-done | bytes 2072
  32.1 1.0 %work_kernel.1 = f32[8,4,128]{2,1,0:T(4,128)} custom-call(bf16[648,4,128]{2,1,0:T(4,128)(2,1)S(1)} %bitcast.14, f32[8,4,128]{2,1,0:T(4,128)S(1)} %bitcast.19, f32[8,4,128]{2,1,0:T(4,128)S(1)} %bitcast.21, s32[4,128]{1,0:T(4,128)S(1)} %bitcast.25, f32[8,4,128]{2,1,0:T(4,128)S(1)} %bitcast.23, f32[54,8,128]{2,1,0:T(8,128)S(1)} %get-tuple-element.37.speeds, ...), custom_call_target="tpu_custom_call" | custom-call | flops 100000 | bytes 1083392 | tf_op jit(solution)/shard_map/work_kernel/pallas_call | solution.py:383
  33.0 0.8 %nodal_kernel.1.nodal = f32[3,48,384]{2,1,0:T(8,128)S(1)} custom-call(f32[81,8,128]{2,1,0:T(8,128)S(1)} %get-tuple-element.34.zeroth, f32[81,8,128]{2,1,0:T(8,128)S(1)} %get-tuple-element.33.first, f32[81,8,128]{2,1,0:T(8,128)S(1)} %get-tuple-element.36.second), custom_call_target="tpu_custom_call" | custom-call | flops 100000 | bytes 1216512 | tf_op jit(solution)/shard_map/nodal_kernel/pallas_call | solution.py:383
  33.9 4.6 %all-to-all-done = f32[32,1,128]{2,1,0:T(1,128)S(1)} async-done(((f32[32,1,128]{2,1,0:T(1,128)}), f32[32,1,128]{2,1,0:T(1,128)S(1)}, u32[]{:S(2)}, u32[]{:S(2)}) %all-to-all-start) | async-done | bytes 16416 | tf_op jit(solution)/shard_map/all_to_all | solution.py:467
  38.5 0.8 %last_kernel.1 = f32[3,2,8,257]{3,2,1,0:T(8,128)} custom-call(f32[32,128]{1,0:T(8,128)S(1)} %bitcast.22, f32[3,48,384]{2,1,0:T(8,128)S(1)} %nodal_kernel.1.nodal, f32[3,2,8,257]{3,2,1,0:T(8,128)S(1)} %copy-done.2), custom_call_target="tpu_custom_call" | custom-call | flops 100000 | bytes 336256 | tf_op jit(solution)/shard_map/last_kernel/pallas_call | solution.py:383
  (10 shorter events, 0.0 us)
Async XLA Ops:
  0.6 5.6 %copy-start.2 = (f32[3,2,8,257]{3,2,1,0:T(8,128)S(1)}, f32[3,2,8,257]{3,2,1,0:T(8,128)}, u32[]{:S(2)}) copy-start(f32[3,2,8,257]{3,2,1,0:T(8,128)} %velocity.3) | copy-start | bytes 148036
  2.1 4.4 %collective-permute-start = (bf16[27,4,128]{2,1,0:T(4,128)(2,1)S(1)}, bf16[27,4,128]{2,1,0:T(4,128)(2,1)S(1)}, u32[]{:S(2)}, u32[]{:S(2)}) collective-permute-start(bf16[27,4,128]{2,1,0:T(4,128)(2,1)S(1)} %get-tuple-element.21), channel_id=1, source_target_pairs={{0,4},{4,0},{8,12},{12,8},{16,20},{20,16},{24,28},{28,24},{1,5},{5... | collective-permute-start | bytes 82952 | tf_op jit(solution)/shard_map/ppermute | solution.py:403
  2.6 5.1 %copy-start.1 = (f32[27,1,4,128]{3,2,1,0:T(4,128)S(1)}, f32[27,1,4,128]{3,2,1,0:T(4,128)}, u32[]{:S(2)}) copy-start(f32[27,1,4,128]{3,2,1,0:T(4,128)} %param.12) | copy-start | bytes 165892
  2.7 5.1 %collective-permute-start.1 = (bf16[27,4,128]{2,1,0:T(4,128)(2,1)S(1)}, bf16[27,4,128]{2,1,0:T(4,128)(2,1)S(1)}, u32[]{:S(2)}, u32[]{:S(2)}) collective-permute-start(bf16[27,4,128]{2,1,0:T(4,128)(2,1)S(1)} %get-tuple-element.22), channel_id=1, source_target_pairs={{0,28},{4,8},{8,4},{12,16},{16,12},{20,24},{24,20},{28,0},{1,29},{... | collective-permute-start | bytes 82952 | tf_op jit(solution)/shard_map/ppermute | solution.py:402
  7.9 9.8 %collective-permute-start.3 = (bf16[126,2,128]{2,1,0:T(2,128)(2,1)S(1)}, bf16[126,2,128]{2,1,0:T(2,128)(2,1)S(1)}, u32[]{:S(2)}, u32[]{:S(2)}) collective-permute-start(bf16[126,2,128]{2,1,0:T(2,128)(2,1)S(1)} %get-tuple-element.25), channel_id=1, source_target_pairs={{0,3},{1,0},{2,1},{3,2},{4,7},{5,4},{6,5},{7,6},{8,11},{9,8},{10,9... | collective-permute-start | bytes 193544 | tf_op jit(solution)/shard_map/ppermute | solution.py:397
  11.7 6.0 %collective-permute-start.2 = (bf16[108,2,128]{2,1,0:T(2,128)(2,1)S(1)}, bf16[108,2,128]{2,1,0:T(2,128)(2,1)S(1)}, u32[]{:S(2)}, u32[]{:S(2)}) collective-permute-start(bf16[108,2,128]{2,1,0:T(2,128)(2,1)S(1)} %get-tuple-element.24), channel_id=1, source_target_pairs={{0,1},{1,2},{2,3},{3,0},{4,5},{5,6},{6,7},{7,4},{8,9},{9,10},{10,1... | collective-permute-start | bytes 165896 | tf_op jit(solution)/shard_map/ppermute | solution.py:397
  18.2 2.3 %collective-permute-start.4 = (bf16[32,8,128]{2,1,0:T(8,128)(2,1)S(1)}, bf16[32,8,128]{2,1,0:T(8,128)(2,1)S(1)}, u32[]{:S(2)}, u32[]{:S(2)}) collective-permute-start(bf16[32,8,128]{2,1,0:T(8,128)(2,1)S(1)} %get-tuple-element.27), channel_id=1, source_target_pairs={{0,4},{4,0},{8,12},{12,8},{16,20},{20,16},{24,28},{28,24},{1,5},{5... | collective-permute-start | bytes 196616 | tf_op jit(solution)/shard_map/ppermute | solution.py:403
  18.3 4.7 %collective-permute-start.5 = (bf16[32,8,128]{2,1,0:T(8,128)(2,1)S(1)}, bf16[32,8,128]{2,1,0:T(8,128)(2,1)S(1)}, u32[]{:S(2)}, u32[]{:S(2)}) collective-permute-start(bf16[32,8,128]{2,1,0:T(8,128)(2,1)S(1)} %get-tuple-element.28), channel_id=1, source_target_pairs={{0,28},{4,8},{8,4},{12,16},{16,12},{20,24},{24,20},{28,0},{1,29},{... | collective-permute-start | bytes 196616 | tf_op jit(solution)/shard_map/ppermute | solution.py:402
  23.4 2.2 %collective-permute-start.6 = (bf16[18,8,128]{2,1,0:T(8,128)(2,1)S(1)}, bf16[18,8,128]{2,1,0:T(8,128)(2,1)S(1)}, u32[]{:S(2)}, u32[]{:S(2)}) collective-permute-start(bf16[18,8,128]{2,1,0:T(8,128)(2,1)S(1)} %get-tuple-element.31), channel_id=1, source_target_pairs={{0,4},{4,0},{8,12},{12,8},{16,20},{20,16},{24,28},{28,24},{1,5},{5... | collective-permute-start | bytes 110600 | tf_op jit(solution)/shard_map/ppermute | solution.py:403
  23.5 4.3 %collective-permute-start.7 = (bf16[18,8,128]{2,1,0:T(8,128)(2,1)S(1)}, bf16[18,8,128]{2,1,0:T(8,128)(2,1)S(1)}, u32[]{:S(2)}, u32[]{:S(2)}) collective-permute-start(bf16[18,8,128]{2,1,0:T(8,128)(2,1)S(1)} %get-tuple-element.32), channel_id=1, source_target_pairs={{0,28},{4,8},{8,4},{12,16},{16,12},{20,24},{24,20},{28,0},{1,29},{... | collective-permute-start | bytes 110600 | tf_op jit(solution)/shard_map/ppermute | solution.py:402
  25.5 5.9 %copy-start = (bf16[81,8,1,4,128]{4,3,2,1,0:T(4,128)(2,1)S(1)}, bf16[81,8,1,4,128]{4,3,2,1,0:T(4,128)(2,1)}, u32[]{:S(2)}) copy-start(bf16[81,8,1,4,128]{4,3,2,1,0:T(4,128)(2,1)} %param.11) | copy-start | bytes 1990660
  27.8 3.6 %copy-start.5 = (f32[8,1,4,128]{3,2,1,0:T(4,128)S(1)}, f32[8,1,4,128]{3,2,1,0:T(4,128)}, u32[]{:S(2)}) copy-start(f32[8,1,4,128]{3,2,1,0:T(4,128)} %param.13) | copy-start | bytes 49156
  28.7 2.7 %copy-start.3 = (f32[8,1,4,128]{3,2,1,0:T(4,128)S(1)}, f32[8,1,4,128]{3,2,1,0:T(4,128)}, u32[]{:S(2)}) copy-start(f32[8,1,4,128]{3,2,1,0:T(4,128)} %param.9) | copy-start | bytes 49156
  28.7 2.7 %copy-start.4 = (f32[8,1,4,128]{3,2,1,0:T(4,128)S(1)}, f32[8,1,4,128]{3,2,1,0:T(4,128)}, u32[]{:S(2)}) copy-start(f32[8,1,4,128]{3,2,1,0:T(4,128)} %param.8) | copy-start | bytes 49156
  28.7 9.8 %all-to-all-start = ((f32[32,1,128]{2,1,0:T(1,128)}), f32[32,1,128]{2,1,0:T(1,128)S(1)}, u32[]{:S(2)}, u32[]{:S(2)}) async-start(f32[32,1,128]{2,1,0:T(1,128)} %bitcast.6), calls=%async_computation | async-start | bytes 32768 | tf_op jit(solution)/shard_map/all_to_all | solution.py:467
  31.4 0.7 %copy-start.6 = (s32[1,4,128]{2,1,0:T(4,128)S(1)}, s32[1,4,128]{2,1,0:T(4,128)}, u32[]{:S(2)}) copy-start(s32[1,4,128]{2,1,0:T(4,128)} %param.10) | copy-start | bytes 6148

commit v4 on v3

--- a/solution.py
+++ b/solution.py
@@ -74,8 +74,8 @@
     return values
 
 
-def is_even():
-    return lax.axis_index("slab") % 2 == 0
+def is_even(axis="slab"):
+    return lax.axis_index(axis) % 2 == 0
 
 
 def put(near, far, slot, left, right, even):
@@ -86,6 +86,12 @@
 def get(near, far, slot, even):
     one, other = near[slot].astype(F32), far[slot].astype(F32)
     return jnp.where(even, other, one), jnp.where(even, one, other)
+
+
+def pressure_of(density, energy, material):
+    gamma = jnp.where(material[...] == 0, 2.0 / 3.0, 0.4).astype(F32)
+    gamma = jnp.concatenate([gamma, gamma], axis=0)
+    return (gamma[None] * density[...] * energy[...]).astype(BF16).astype(F32)
 
 
 def force_kernel(
@@ -101,7 +107,7 @@
     ]
     parts = [
         pltpu.make_async_copy(
-            geometry_in.at[pl.ds(216 * comp, 216)], geometry.at[pl.ds(216 * comp, 216)], sems.at[comp]
+            geometry_in.at[pl.ds(108 * comp, 108)], geometry.at[pl.ds(108 * comp, 108)], sems.at[comp]
         )
         for comp in range(3)
     ]
@@ -109,8 +115,7 @@
         copy.start()
     for copy in small:
         copy.wait()
-    gamma = jnp.where(material[...] == 0, 2.0 / 3.0, 0.4).astype(F32)
-    pressure = (gamma[None] * density[...] * energy[...]).astype(BF16).astype(F32)
+    pressure = pressure_of(density, energy, material)
     gravity = from_points([mass_weight[q] * POINT_WEIGHT[q] for q in range(27)])
     even = is_even()
     for comp in range(3):
@@ -118,8 +123,8 @@
         values = []
         for n in range(27):
             r = 27 * comp + n
-            block = geometry[pl.ds(8 * r, 8)].astype(F32)
-            value = -jnp.sum(block * pressure, axis=0)
+            value = jnp.sum(geometry[pl.ds(4 * r, 4)].astype(F32) * pressure, axis=0)
+            value = -(value + pltpu.roll(value, OWN, 0))[:OWN]
             if comp == 2:
                 value = value - GRAVITY * gravity[n]
             field[r] = value
@@ -148,8 +153,9 @@
             out[3 * group + c] = moved[8 * group : 8 * group + 8, 128 * c : 128 * c + 128]
 
 
-def rim_kernel(field, near, far, mass_weight, spread, out, to_low, to_high):
-    even = is_even()
+def rim_kernel(field, far, near, mass_weight, spread, out, near_out, far_out):
+    even = is_even()
+    even_y = is_even("brick")
     for comp in range(3):
         values = [field[27 * comp + n] for n in range(27)]
         for n in range(9):
@@ -159,15 +165,15 @@
         for n in range(27):
             r = 27 * comp + n
             out[r] = values[n]
-            to_low[r] = values[n][:HALO].astype(BF16)
-            to_high[r] = values[n][OWN - HALO :].astype(BF16)
+            put(near_out, far_out, r, values[n][:HALO], values[n][OWN - HALO :], even_y)
     for q in range(27):
-        to_low[81 + q] = mass_weight[q, :HALO].astype(BF16)
-        to_high[81 + q] = mass_weight[q, OWN - HALO :].astype(BF16)
-    for comp in range(3):
-        for a in range(2):
-            for c in range(3):
-                to_low[108 + 6 * comp + 3 * a + c] = spread[12 * comp + 6 * a + c, :HALO].astype(BF16)
+        put(near_out, far_out, 81 + q, mass_weight[q, :HALO], mass_weight[q, OWN - HALO :], even_y)
+    row = lax.broadcasted_iota(jnp.int32, (8, 128), 0)
+    for slot in range(9):
+        first, second = [spread[12 * (k // 6) + 6 * (k // 3 % 2) + k % 3] for k in (2 * slot, 2 * slot + 1)]
+        both = jnp.where(row == 0, first, pltpu.roll(second, 1, 0))[:HALO].astype(BF16)
+        near_out[108 + slot] = both
+        far_out[108 + slot] = both
 
 
 def send_planes(values, comp, near, far, even):
@@ -184,19 +190,17 @@
 
 
 def first_kernel(
-    own, from_low, from_high, mass_weight, spread, field, weight, image, near, far, speeds, rows
+    own, far_in, near_in, mass_weight, spread, field, weight, image, near, far, speeds, rows
 ):
     even = is_even()
+    even_y = is_even("brick")
+    for r in range(108):
+        low, high = get(near_in, far_in, r, even_y)
+        rows[r, :HALO] = low
+        rows[r, HALO : HALO + OWN] = own[r] if r < 81 else mass_weight[r - 81]
+        rows[r, HALO + OWN :] = high
     for q in range(27):
-        rows[q, :HALO] = from_low[81 + q].astype(F32)
-        rows[q, HALO : HALO + OWN] = mass_weight[q]
-        rows[q, HALO + OWN :] = from_high[81 + q].astype(F32)
-    for q in range(27):
-        weight[q] = rows[q] * POINT_WEIGHT[q]
-    for r in range(81):
-        rows[r, :HALO] = from_low[r].astype(F32)
-        rows[r, HALO : HALO + OWN] = own[r]
-        rows[r, HALO + OWN :] = from_high[r].astype(F32)
+        weight[q] = rows[81 + q] * POINT_WEIGHT[q]
     for comp in range(3):
         values = [rows[27 * comp + n] for n in range(27)]
         values = assemble_y(assemble_z(values, comp == 2))
@@ -212,7 +216,8 @@
         for a in range(2):
             speed = [spread[12 * comp + 6 * a + n] for n in range(6)]
             for c in range(3):
-                beyond = from_high[108 + 6 * comp + 3 * a + c].astype(F32)[0:1]
+                k = 6 * comp + 3 * a + c
+                beyond = get(near_in, far_in, 108 + k // 2, even_y)[1][k % 2 : k % 2 + 1]
                 speed.append(jnp.where(row == OWN - 1, beyond, pltpu.roll(speed[c], 7, 0)))
             for n in range(9):
                 speeds[18 * comp + 9 * a + n] = speed[n]
@@ -239,7 +244,7 @@
     return values
 
 
-def second_kernel(image, near_in, far_in, weight, field, image_out, near, far):
+def second_kernel(image, far_in, near_in, weight, field, image_out, near, far):
     even = is_even()
     for comp in range(3):
         values = take_planes(image, near_in, far_in, comp, even)
@@ -251,20 +256,20 @@
         send_planes(values, comp, near, far, even)
 
 
-def work_kernel(geometry, density, energy, material, energy_mass, speeds, near, far, out):
-    even = is_even()
-    gamma = jnp.where(material[...] == 0, 2.0 / 3.0, 0.4).astype(F32)
-    pressure = (gamma[None] * density[...] * energy[...]).astype(BF16).astype(F32)
+def work_kernel(geometry, density, energy, material, energy_mass, speeds, far, near, out):
+    even = is_even()
+    pressure = pressure_of(density, energy, material)
     work = jnp.zeros_like(pressure)
+    upper = lax.broadcasted_iota(jnp.int32, (8, 128), 0) >= OWN
     for comp in range(3):
         for n in range(27):
             if n < 18:
-                speed = speeds[18 * comp + n, :OWN]
+                speed, odd = speeds[18 * comp + n], False
             else:
                 k = 9 * comp + n - 18
-                _, speed = get(near, far, 18 + k // 2, even)
-                speed = speed[OWN * (k % 2) : OWN * (k % 2) + OWN]
-            work = work + geometry[pl.ds(8 * (27 * comp + n), 8)].astype(F32) * speed[None]
+                speed, odd = get(near, far, 18 + k // 2, even)[1], k % 2 == 1
+            speed = jnp.where(upper == odd, speed, pltpu.roll(speed, OWN, 0))
+            work = work + geometry[pl.ds(4 * (27 * comp + n), 4)].astype(F32) * speed[None]
     out[...] = energy[...] + HALF_STEP * pressure * work / energy_mass[...]
 
 
@@ -286,7 +291,7 @@
         products[k] = total
 
 
-def moment_kernel(image, near, far, weight, first, products, second, moments):
+def moment_kernel(image, far, near, weight, first, products, second, moments):
     zero = jnp.zeros((8, 128), F32)
     cross, norm = zero, zero
     quadratic = [zero] * 3
@@ -392,27 +397,22 @@
     )(*args)
 
 
-def shift(x, axis, by):
+def swap(near, far, axis="slab"):
     count = lax.axis_size(axis)
-    return lax.ppermute(x, axis, [(i, (i + by) % count) for i in range(count)])
-
-
-def swap(near, far):
-    count = lax.axis_size("slab")
-    far = lax.ppermute(far, "slab", [(i, (i + (1 if i % 2 else -1)) % count) for i in range(count)])
-    near = lax.ppermute(near, "slab", [(i, i + (-1 if i % 2 else 1)) for i in range(count)])
+    far = lax.ppermute(far, axis, [(i, (i + (1 if i % 2 else -1)) % count) for i in range(count)])
+    near = lax.ppermute(near, axis, [(i, i + (-1 if i % 2 else 1)) for i in range(count)])
     return near, far
 
 
 def local(velocity, energy, density, material, geometry, mass_weight, energy_mass):
     tile = (4, 128)
-    geometry = geometry.reshape((648,) + tile)
-    density = density.reshape((8,) + tile)
-    energy = energy.reshape((8,) + tile)
-    energy_mass = energy_mass.reshape((8,) + tile)
+    full = (8, 128)
+    geometry = geometry.reshape((324,) + full)
+    density = density.reshape((4,) + full)
+    energy = energy.reshape((4,) + full)
+    energy_mass = energy_mass.reshape((4,) + full)
     mass_weight = mass_weight.reshape((27,) + tile)
     material = material.reshape(tile)
-    full = (8, 128)
     pair = (2, 128)
     devices = lax.axis_size("slab") * lax.axis_size("brick")
 
@@ -421,9 +421,9 @@
         [(81,) + tile, (27,) + tile, (27,) + tile],
         *[pltpu.with_memory_space_constraint(x, pltpu.HBM) for x in (geometry, density, energy, material, mass_weight)],
         scratch=[
-            pltpu.VMEM((648,) + tile, BF16),
-            pltpu.VMEM((8,) + tile, F32),
-            pltpu.VMEM((8,) + tile, F32),
+            pltpu.VMEM((324,) + full, BF16),
+            pltpu.VMEM((4,) + full, F32),
+            pltpu.VMEM((4,) + full, F32),
             pltpu.VMEM(tile, jnp.int32),
             pltpu.VMEM((27,) + tile, F32),
             pltpu.SemaphoreType.DMA((7,)),
@@ -433,35 +433,34 @@
     )
     (spread,) = call(spread_kernel, [(36,) + full], velocity)
     near, far = swap(near, far)
-    own, to_low, to_high = call(
+    own, near, far = call(
         rim_kernel,
-        [(81,) + tile, (126,) + pair, (108,) + pair],
-        force, near, far, mass_weight, spread,
+        [(81,) + tile, (117,) + pair, (117,) + pair],
+        force, far, near, mass_weight, spread,
         dtypes=[F32, BF16, BF16],
     )
-    from_high = shift(to_low, "brick", -1)
-    from_low = shift(to_high, "brick", 1)
+    near, far = swap(near, far, "brick")
     zeroth, weight, image, near, far, speeds = call(
         first_kernel,
         [(81,) + full, (27,) + full, (81,) + full, (32,) + full, (32,) + full, (54,) + full],
-        own, from_low, from_high, mass_weight, spread,
-        scratch=[pltpu.VMEM((81,) + full, F32)],
+        own, far, near, mass_weight, spread,
+        scratch=[pltpu.VMEM((108,) + full, F32)],
         dtypes=[F32, F32, F32, BF16, BF16, F32],
     )
     near, far = swap(near, far)
     first, image, near_out, far_out = call(
         second_kernel,
         [(81,) + full, (81,) + full, (18,) + full, (18,) + full],
-        image, near, far, weight,
+        image, far, near, weight,
         dtypes=[F32, F32, BF16, BF16],
     )
     (energy_half,) = call(
-        work_kernel, [(8,) + tile], geometry, density, energy, material, energy_mass, speeds, near, far
+        work_kernel, [(4,) + full], geometry, density, energy, material, energy_mass, speeds, far, near
     )
     near, far = swap(near_out, far_out)
     (products,) = call(product_kernel, [(3,) + full], zeroth, first)
     second, moments = call(
-        moment_kernel, [(81,) + full, (devices, 128)], image, near, far, weight, first, products
+        moment_kernel, [(81,) + full, (devices, 128)], image, far, near, weight, first, products
     )
     moments = pltpu.with_memory_space_constraint(moments, pltpu.VMEM)
     moments = lax.all_to_all(moments, ("slab", "brick"), 0, 0, tiled=True)

time: 39.5 us -> 37.9 us (0.959)
  starting transfers between devices: 15 us -> 13 us
  waiting for transfers between devices: 16.6 us -> 17.2 us
    ppermute x8, starting transfers between devices: 12.3 us -> 9.94 us  [the longest x4 9.4 us: swap(): lax.ppermute(far, axis, [(i, (i + (1 if i % 2 else -1)) % count) for i in...]
    ppermute x8, waiting for transfers between devices: 12 us -> 12.5 us  [the longest x4 10.6 us: swap(): lax.ppermute(far, axis, [(i, (i + (1 if i % 2 else -1)) % count) for i in...]
  transfers between devices with their start and end apart: 9 -> 9, of which waited for: 5 -> 6; matrix products, arithmetic and copies ran while one was open for 0% -> 0% of each run, Pallas kernels for 5% -> 5%
where the time goes in v4:
time: 37.9 us; the launch traced here: 37.7 us
  waiting for transfers between devices  17.2 us (45%)
  starting transfers between devices  13 us (34%)
  Pallas kernels  6.09 us (16%)
  between operations  0.73 us (2%)
  local copies, waits for them, and re-layouts  0.66 us (2%)
    ppermute x4, waiting for transfers between devices, swap(): lax.ppermute(far, axis, [(i, (i + (1 if i % 2 else -1)) % count) for i in...  10.6 us
    ppermute x4, starting transfers between devices, swap(): lax.ppermute(far, axis, [(i, (i + (1 if i % 2 else -1)) % count) for i in...  9.4 us
    pallas_call x10, Pallas kernels, call(): pl.pallas_call(kernel, out_shape=shapes, in_specs=[place] * len(args), ou...  6.09 us
    all_to_all x1, waiting for transfers between devices, local(): moments = lax.all_to_all(moments, ('slab', 'brick'), 0, 0, tiled=True)  4.79 us
    all_to_all x1, starting transfers between devices, local(): moments = lax.all_to_all(moments, ('slab', 'brick'), 0, 0, tiled=True)  3.01 us
    ppermute x4, waiting for transfers between devices, swap(): lax.ppermute(near, axis, [(i, i + (-1 if i % 2 else 1)) for i in range(co...  1.9 us
  transfers between devices with their start and end apart: 9, of which 6 were waited for; matrix products, arithmetic and copies ran while one was open for 0% of the time, Pallas kernels for 5%

profile of v4, /device:TPU:0, one launch (start us, length us, event | category | flops | bytes accessed | tf_op | source)
XLA Modules:
  0.0 37.7 jit_solution(15925095720079671659)
XLA Ops:
  0.6 0.0 copy-start.2
  0.6 1.4 %force_kernel.1 = (f32[81,4,128]{2,1,0:T(4,128)S(1)}, bf16[27,4,128]{2,1,0:T(4,128)(2,1)S(1)}, bf16[27,4,128]{2,1,0:T(4,128)(2,1)S(1)}) custom-call(bf16[324,8,128]{2,1,0:T(8,128)(2,1)} %bitcast.13, f32[4,8,128]{2,1,0:T(8,128)} %bitcast.18, f32[4,8,128]{2,1,0:T(8,128)} %bitcast.20, s32[4,128]{1,0:T(4,128)} %bitcast.24, f32[27,4,128]{2,1,0:T(4,128)} %bitcast.15), custom_call_target="tpu_custom_call" | custom-call | flops 100000 | bytes 1030144 | tf_op jit(solution)/shard_map/force_kernel/pallas_call | solution.py:388
  2.0 3.4 %collective-permute-start = (bf16[27,4,128]{2,1,0:T(4,128)(2,1)S(1)}, bf16[27,4,128]{2,1,0:T(4,128)(2,1)S(1)}, u32[]{:S(2)}, u32[]{:S(2)}) collective-permute-start(bf16[27,4,128]{2,1,0:T(4,128)(2,1)S(1)} %get-tuple-element.21), channel_id=1, source_target_pairs={{0,28},{4,8},{8,4},{12,16},{16,12},{20,24},{24,20},{28,0},{1,29},{... | collective-permute-start | bytes 82952 | tf_op jit(solution)/shard_map/ppermute | solution.py:402
  5.4 0.0 collective-permute-start.1
  5.4 0.0 copy-done.2
  5.4 0.3 spread_kernel.1.spread
  5.7 1.2 %collective-permute-done.far = bf16[27,4,128]{2,1,0:T(4,128)(2,1)S(1)} collective-permute-done((bf16[27,4,128]{2,1,0:T(4,128)(2,1)S(1)}, bf16[27,4,128]{2,1,0:T(4,128)(2,1)S(1)}, u32[]{:S(2)}, u32[]{:S(2)}) %collective-permute-start) | collective-permute-done | bytes 27680 | tf_op jit(solution)/shard_map/ppermute | solution.py:402
  7.0 0.0 collective-permute-done.1.near
  7.0 0.2 rim_kernel.1
  7.1 4.6 %collective-permute-start.2 = (bf16[117,2,128]{2,1,0:T(2,128)(2,1)S(1)}, bf16[117,2,128]{2,1,0:T(2,128)(2,1)S(1)}, u32[]{:S(2)}, u32[]{:S(2)}) collective-permute-start(bf16[117,2,128]{2,1,0:T(2,128)(2,1)S(1)} %get-tuple-element.24), channel_id=1, source_target_pairs={{0,3},{1,2},{2,1},{3,0},{4,7},{5,6},{6,5},{7,4},{8,11},{9,10},{10,... | collective-permute-start | bytes 179720 | tf_op jit(solution)/shard_map/ppermute | solution.py:402
  11.8 0.0 collective-permute-start.3
  11.8 2.3 %collective-permute-done.2.far_in = bf16[117,2,128]{2,1,0:T(2,128)(2,1)S(1)} collective-permute-done((bf16[117,2,128]{2,1,0:T(2,128)(2,1)S(1)}, bf16[117,2,128]{2,1,0:T(2,128)(2,1)S(1)}, u32[]{:S(2)}, u32[]{:S(2)}) %collective-permute-start.2) | collective-permute-done | bytes 59936 | tf_op jit(solution)/shard_map/ppermute | solution.py:402
  14.1 1.9 %collective-permute-done.3.near_in = bf16[117,2,128]{2,1,0:T(2,128)(2,1)S(1)} collective-permute-done((bf16[117,2,128]{2,1,0:T(2,128)(2,1)S(1)}, bf16[117,2,128]{2,1,0:T(2,128)(2,1)S(1)}, u32[]{:S(2)}, u32[]{:S(2)}) %collective-permute-start.3) | collective-permute-done | bytes 59936 | tf_op jit(solution)/shard_map/ppermute | solution.py:403
  16.0 0.6 %first_kernel.1 = (f32[81,8,128]{2,1,0:T(8,128)S(1)}, f32[27,8,128]{2,1,0:T(8,128)S(1)}, f32[81,8,128]{2,1,0:T(8,128)S(1)}, bf16[32,8,128]{2,1,0:T(8,128)(2,1)S(...) custom-call(f32[81,4,128]{2,1,0:T(4,128)S(1)} %get-tuple-element.23.own, ...), custom_call_target="tpu_custom_call" | custom-call | flops 100000 | bytes 1745920 | tf_op jit(solution)/shard_map/first_kernel/pallas_call | solution.py:388
  16.5 0.4 %collective-permute-start.4 = (bf16[32,8,128]{2,1,0:T(8,128)(2,1)S(1)}, bf16[32,8,128]{2,1,0:T(8,128)(2,1)S(1)}, u32[]{:S(2)}, u32[]{:S(2)}) collective-permute-start(bf16[32,8,128]{2,1,0:T(8,128)(2,1)S(1)} %get-tuple-element.27), channel_id=1, source_target_pairs={{0,28},{4,8},{8,4},{12,16},{16,12},{20,24},{24,20},{28,0},{1,29},{... | collective-permute-start | bytes 196616 | tf_op jit(solution)/shard_map/ppermute | solution.py:402
  17.0 0.5 %collective-permute-start.5 = (bf16[32,8,128]{2,1,0:T(8,128)(2,1)S(1)}, bf16[32,8,128]{2,1,0:T(8,128)(2,1)S(1)}, u32[]{:S(2)}, u32[]{:S(2)}) collective-permute-start(bf16[32,8,128]{2,1,0:T(8,128)(2,1)S(1)} %get-tuple-element.28), channel_id=1, source_target_pairs={{0,4},{4,0},{8,12},{12,8},{16,20},{20,16},{24,28},{28,24},{1,5},{5... | collective-permute-start | bytes 196616 | tf_op jit(solution)/shard_map/ppermute | solution.py:403
  17.5 3.7 %collective-permute-done.4.far_in.far = bf16[32,8,128]{2,1,0:T(8,128)(2,1)S(1)} collective-permute-done((bf16[32,8,128]{2,1,0:T(8,128)(2,1)S(1)}, bf16[32,8,128]{2,1,0:T(8,128)(2,1)S(1)}, u32[]{:S(2)}, u32[]{:S(2)}) %collective-permute-start.4) | collective-permute-done | bytes 65568 | tf_op jit(solution)/shard_map/ppermute | solution.py:402
  21.2 0.0 collective-permute-done.5.near_in.near
  21.2 0.4 second_kernel.1
  21.6 1.0 %collective-permute-start.6 = (bf16[18,8,128]{2,1,0:T(8,128)(2,1)S(1)}, bf16[18,8,128]{2,1,0:T(8,128)(2,1)S(1)}, u32[]{:S(2)}, u32[]{:S(2)}) collective-permute-start(bf16[18,8,128]{2,1,0:T(8,128)(2,1)S(1)} %get-tuple-element.31), channel_id=1, source_target_pairs={{0,28},{4,8},{8,4},{12,16},{16,12},{20,24},{24,20},{28,0},{1,29},{... | collective-permute-start | bytes 110600 | tf_op jit(solution)/shard_map/ppermute | solution.py:402
  22.5 0.0 collective-permute-start.7
  22.6 0.1 product_kernel.1.products
  22.6 3.3 %collective-permute-done.6.far = bf16[18,8,128]{2,1,0:T(8,128)(2,1)S(1)} collective-permute-done((bf16[18,8,128]{2,1,0:T(8,128)(2,1)S(1)}, bf16[18,8,128]{2,1,0:T(8,128)(2,1)S(1)}, u32[]{:S(2)}, u32[]{:S(2)}) %collective-permute-start.6) | collective-permute-done | bytes 36896 | tf_op jit(solution)/shard_map/ppermute | solution.py:402
  25.9 0.0 collective-permute-done.7.near
  25.9 0.9 %moment_kernel.1 = (f32[81,8,128]{2,1,0:T(8,128)S(1)}, f32[32,128]{1,0:T(8,128)}) custom-call(f32[81,8,128]{2,1,0:T(8,128)S(1)} %get-tuple-element.30.image, bf16[18,8,128]{2,1,0:T(8,128)(2,1)S(1)} %collective-permute-done.6.far, bf16[18,8,128]{2,1,0:T(8,128)(2,1)S(1)} %collective-permute-done.7.near, f32[27,8,128]{2,1,0:T(8,128)S(1)} %get-tuple-element.29.weight, ...), custom_call_target="tpu_custom_call" | custom-call | flops 100000 | bytes 1208320 | tf_op jit(solution)/shard_map/moment_kernel/pallas_call | solution.py:388
  26.8 3.0 %all-to-all-start = ((f32[32,1,128]{2,1,0:T(1,128)}), f32[32,1,128]{2,1,0:T(1,128)S(1)}, u32[]{:S(2)}, u32[]{:S(2)}) async-start(f32[32,1,128]{2,1,0:T(1,128)} %bitcast.6), calls=%async_computation | async-start | bytes 32768 | tf_op jit(solution)/shard_map/all_to_all | solution.py:466
  29.8 0.0 copy-start.6
  29.9 0.6 %copy-done.6 = s32[1,4,128]{2,1,0:T(4,128)S(1)} copy-done((s32[1,4,128]{2,1,0:T(4,128)S(1)}, s32[1,4,128]{2,1,0:T(4,128)}, u32[]{:S(2)}) %copy-start.6) | copy-done | bytes 2072
  30.5 0.8 %work_kernel.1 = f32[4,8,128]{2,1,0:T(8,128)} custom-call(bf16[324,8,128]{2,1,0:T(8,128)(2,1)S(1)} %bitcast.14, f32[4,8,128]{2,1,0:T(8,128)S(1)} %bitcast.19, f32[4,8,128]{2,1,0:T(8,128)S(1)} %bitcast.21, s32[4,128]{1,0:T(4,128)S(1)} %bitcast.25, f32[4,8,128]{2,1,0:T(8,128)S(1)} %bitcast.23, f32[54,8,128]{2,1,0:T(8,128)S(1)} %get-tuple-element.37.speeds, ...), custom_call_target="tpu_custom_call" | custom-call | flops 100000 | bytes 1083392 | tf_op jit(solution)/shard_map/work_kernel/pallas_call | solution.py:388
  31.3 0.8 %nodal_kernel.1.nodal = f32[3,48,384]{2,1,0:T(8,128)S(1)} custom-call(f32[81,8,128]{2,1,0:T(8,128)S(1)} %get-tuple-element.34.zeroth, f32[81,8,128]{2,1,0:T(8,128)S(1)} %get-tuple-element.33.first, f32[81,8,128]{2,1,0:T(8,128)S(1)} %get-tuple-element.36.second), custom_call_target="tpu_custom_call" | custom-call | flops 100000 | bytes 1216512 | tf_op jit(solution)/shard_map/nodal_kernel/pallas_call | solution.py:388
  32.1 4.8 %all-to-all-done = f32[32,1,128]{2,1,0:T(1,128)S(1)} async-done(((f32[32,1,128]{2,1,0:T(1,128)}), f32[32,1,128]{2,1,0:T(1,128)S(1)}, u32[]{:S(2)}, u32[]{:S(2)}) %all-to-all-start) | async-done | bytes 16416 | tf_op jit(solution)/shard_map/all_to_all | solution.py:466
  36.9 0.8 %last_kernel.1 = f32[3,2,8,257]{3,2,1,0:T(8,128)} custom-call(f32[32,128]{1,0:T(8,128)S(1)} %bitcast.22, f32[3,48,384]{2,1,0:T(8,128)S(1)} %nodal_kernel.1.nodal, f32[3,2,8,257]{3,2,1,0:T(8,128)S(1)} %copy-done.2), custom_call_target="tpu_custom_call" | custom-call | flops 100000 | bytes 336256 | tf_op jit(solution)/shard_map/last_kernel/pallas_call | solution.py:388
  (10 shorter events, 0.0 us)
Async XLA Ops:
  0.6 4.8 %copy-start.2 = (f32[3,2,8,257]{3,2,1,0:T(8,128)S(1)}, f32[3,2,8,257]{3,2,1,0:T(8,128)}, u32[]{:S(2)}) copy-start(f32[3,2,8,257]{3,2,1,0:T(8,128)} %velocity.3) | copy-start | bytes 148036
  2.0 4.9 %collective-permute-start = (bf16[27,4,128]{2,1,0:T(4,128)(2,1)S(1)}, bf16[27,4,128]{2,1,0:T(4,128)(2,1)S(1)}, u32[]{:S(2)}, u32[]{:S(2)}) collective-permute-start(bf16[27,4,128]{2,1,0:T(4,128)(2,1)S(1)} %get-tuple-element.21), channel_id=1, source_target_pairs={{0,28},{4,8},{8,4},{12,16},{16,12},{20,24},{24,20},{28,0},{1,29},{... | collective-permute-start | bytes 82952 | tf_op jit(solution)/shard_map/ppermute | solution.py:402
  5.4 1.6 %copy-start.1 = (f32[27,1,4,128]{3,2,1,0:T(4,128)S(1)}, f32[27,1,4,128]{3,2,1,0:T(4,128)}, u32[]{:S(2)}) copy-start(f32[27,1,4,128]{3,2,1,0:T(4,128)} %param.12) | copy-start | bytes 165892
  5.4 1.6 %collective-permute-start.1 = (bf16[27,4,128]{2,1,0:T(4,128)(2,1)S(1)}, bf16[27,4,128]{2,1,0:T(4,128)(2,1)S(1)}, u32[]{:S(2)}, u32[]{:S(2)}) collective-permute-start(bf16[27,4,128]{2,1,0:T(4,128)(2,1)S(1)} %get-tuple-element.22), channel_id=1, source_target_pairs={{0,4},{4,0},{8,12},{12,8},{16,20},{20,16},{24,28},{28,24},{1,5},{5... | collective-permute-start | bytes 82952 | tf_op jit(solution)/shard_map/ppermute | solution.py:403
  7.1 6.9 %collective-permute-start.2 = (bf16[117,2,128]{2,1,0:T(2,128)(2,1)S(1)}, bf16[117,2,128]{2,1,0:T(2,128)(2,1)S(1)}, u32[]{:S(2)}, u32[]{:S(2)}) collective-permute-start(bf16[117,2,128]{2,1,0:T(2,128)(2,1)S(1)} %get-tuple-element.24), channel_id=1, source_target_pairs={{0,3},{1,2},{2,1},{3,0},{4,7},{5,6},{6,5},{7,4},{8,11},{9,10},{10,... | collective-permute-start | bytes 179720 | tf_op jit(solution)/shard_map/ppermute | solution.py:402
  11.8 4.2 %collective-permute-start.3 = (bf16[117,2,128]{2,1,0:T(2,128)(2,1)S(1)}, bf16[117,2,128]{2,1,0:T(2,128)(2,1)S(1)}, u32[]{:S(2)}, u32[]{:S(2)}) collective-permute-start(bf16[117,2,128]{2,1,0:T(2,128)(2,1)S(1)} %get-tuple-element.25), channel_id=1, source_target_pairs={{0,1},{1,0},{2,3},{3,2},{4,5},{5,4},{6,7},{7,6},{8,9},{9,8},{10,11... | collective-permute-start | bytes 179720 | tf_op jit(solution)/shard_map/ppermute | solution.py:403
  16.5 4.7 %collective-permute-start.4 = (bf16[32,8,128]{2,1,0:T(8,128)(2,1)S(1)}, bf16[32,8,128]{2,1,0:T(8,128)(2,1)S(1)}, u32[]{:S(2)}, u32[]{:S(2)}) collective-permute-start(bf16[32,8,128]{2,1,0:T(8,128)(2,1)S(1)} %get-tuple-element.27), channel_id=1, source_target_pairs={{0,28},{4,8},{8,4},{12,16},{16,12},{20,24},{24,20},{28,0},{1,29},{... | collective-permute-start | bytes 196616 | tf_op jit(solution)/shard_map/ppermute | solution.py:402
  17.0 4.2 %collective-permute-start.5 = (bf16[32,8,128]{2,1,0:T(8,128)(2,1)S(1)}, bf16[32,8,128]{2,1,0:T(8,128)(2,1)S(1)}, u32[]{:S(2)}, u32[]{:S(2)}) collective-permute-start(bf16[32,8,128]{2,1,0:T(8,128)(2,1)S(1)} %get-tuple-element.28), channel_id=1, source_target_pairs={{0,4},{4,0},{8,12},{12,8},{16,20},{20,16},{24,28},{28,24},{1,5},{5... | collective-permute-start | bytes 196616 | tf_op jit(solution)/shard_map/ppermute | solution.py:403
  21.6 4.3 %collective-permute-start.6 = (bf16[18,8,128]{2,1,0:T(8,128)(2,1)S(1)}, bf16[18,8,128]{2,1,0:T(8,128)(2,1)S(1)}, u32[]{:S(2)}, u32[]{:S(2)}) collective-permute-start(bf16[18,8,128]{2,1,0:T(8,128)(2,1)S(1)} %get-tuple-element.31), channel_id=1, source_target_pairs={{0,28},{4,8},{8,4},{12,16},{16,12},{20,24},{24,20},{28,0},{1,29},{... | collective-permute-start | bytes 110600 | tf_op jit(solution)/shard_map/ppermute | solution.py:402
  22.5 3.4 %collective-permute-start.7 = (bf16[18,8,128]{2,1,0:T(8,128)(2,1)S(1)}, bf16[18,8,128]{2,1,0:T(8,128)(2,1)S(1)}, u32[]{:S(2)}, u32[]{:S(2)}) collective-permute-start(bf16[18,8,128]{2,1,0:T(8,128)(2,1)S(1)} %get-tuple-element.32), channel_id=1, source_target_pairs={{0,4},{4,0},{8,12},{12,8},{16,20},{20,16},{24,28},{28,24},{1,5},{5... | collective-permute-start | bytes 110600 | tf_op jit(solution)/shard_map/ppermute | solution.py:403
  22.5 7.3 %copy-start = (bf16[81,8,1,4,128]{4,3,2,1,0:T(4,128)(2,1)S(1)}, bf16[81,8,1,4,128]{4,3,2,1,0:T(4,128)(2,1)}, u32[]{:S(2)}) copy-start(bf16[81,8,1,4,128]{4,3,2,1,0:T(4,128)(2,1)} %param.11) | copy-start | bytes 1990660
  25.9 3.9 %copy-start.5 = (f32[8,1,4,128]{3,2,1,0:T(4,128)S(1)}, f32[8,1,4,128]{3,2,1,0:T(4,128)}, u32[]{:S(2)}) copy-start(f32[8,1,4,128]{3,2,1,0:T(4,128)} %param.13) | copy-start | bytes 49156
  26.8 3.1 %copy-start.3 = (f32[8,1,4,128]{3,2,1,0:T(4,128)S(1)}, f32[8,1,4,128]{3,2,1,0:T(4,128)}, u32[]{:S(2)}) copy-start(f32[8,1,4,128]{3,2,1,0:T(4,128)} %param.9) | copy-start | bytes 49156
  26.8 3.1 %copy-start.4 = (f32[8,1,4,128]{3,2,1,0:T(4,128)S(1)}, f32[8,1,4,128]{3,2,1,0:T(4,128)}, u32[]{:S(2)}) copy-start(f32[8,1,4,128]{3,2,1,0:T(4,128)} %param.8) | copy-start | bytes 49156
  26.8 10.1 %all-to-all-start = ((f32[32,1,128]{2,1,0:T(1,128)}), f32[32,1,128]{2,1,0:T(1,128)S(1)}, u32[]{:S(2)}, u32[]{:S(2)}) async-start(f32[32,1,128]{2,1,0:T(1,128)} %bitcast.6), calls=%async_computation | async-start | bytes 32768 | tf_op jit(solution)/shard_map/all_to_all | solution.py:466
  29.8 0.7 %copy-start.6 = (s32[1,4,128]{2,1,0:T(4,128)S(1)}, s32[1,4,128]{2,1,0:T(4,128)}, u32[]{:S(2)}) copy-start(s32[1,4,128]{2,1,0:T(4,128)} %param.10) | copy-start | bytes 6148

commit v5 on v4

--- a/solution.py
+++ b/solution.py
@@ -92,6 +92,18 @@
     gamma = jnp.where(material[...] == 0, 2.0 / 3.0, 0.4).astype(F32)
     gamma = jnp.concatenate([gamma, gamma], axis=0)
     return (gamma[None] * density[...] * energy[...]).astype(BF16).astype(F32)
+
+
+def to_lane(tile, lane, values, slot):
+    return jnp.where(lane == slot, pltpu.roll(values, slot + 1, 1), tile)
+
+
+def third_along_z(values, tops, lane, slot):
+    return jnp.where(lane == 127, pltpu.roll(tops, 127 - slot, 1), pltpu.roll(values, 127, 1))
+
+
+def double(values):
+    return jnp.concatenate([values, values], axis=0)
 
 
 def force_kernel(
@@ -116,7 +128,7 @@
     for copy in small:
         copy.wait()
     pressure = pressure_of(density, energy, material)
-    gravity = from_points([mass_weight[q] * POINT_WEIGHT[q] for q in range(27)])
+    gravity = from_points([double(mass_weight[q]) * POINT_WEIGHT[q] for q in range(27)])
     even = is_even()
     for comp in range(3):
         parts[comp].wait()
@@ -124,13 +136,13 @@
         for n in range(27):
             r = 27 * comp + n
             value = jnp.sum(geometry[pl.ds(4 * r, 4)].astype(F32) * pressure, axis=0)
-            value = -(value + pltpu.roll(value, OWN, 0))[:OWN]
+            value = -(value + pltpu.roll(value, OWN, 0))
             if comp == 2:
                 value = value - GRAVITY * gravity[n]
             field[r] = value
             values.append(value)
         for n in range(9):
-            put(near, far, 9 * comp + n, values[n], values[18 + n], even)
+            put(near, far, 9 * comp + n, values[n][:OWN], values[18 + n][:OWN], even)
 
 
 def spread_kernel(velocity, out):
@@ -153,34 +165,64 @@
             out[3 * group + c] = moved[8 * group : 8 * group + 8, 128 * c : 128 * c + 128]
 
 
+TOPS, WEIGHTS, SPEEDS, MESSAGE = 45, 46, 73, 79
+SPEED_LANE = 32
+
+
 def rim_kernel(field, far, near, mass_weight, spread, out, near_out, far_out):
     even = is_even()
     even_y = is_even("brick")
+    row = lax.broadcasted_iota(jnp.int32, (8, 128), 0)
+    lane = lane_of((8, 128))
+    tops = jnp.zeros((8, 128), F32)
+    outer = []
     for comp in range(3):
         values = [field[27 * comp + n] for n in range(27)]
         for n in range(9):
             left, right = get(near, far, 9 * comp + n, even)
-            values[n] = values[n] + left
-            values[18 + n] = values[18 + n] + right
-        for n in range(27):
-            r = 27 * comp + n
-            out[r] = values[n]
-            put(near_out, far_out, r, values[n][:HALO], values[n][OWN - HALO :], even_y)
+            values[n] = values[n] + double(left)
+            values[18 + n] = values[18 + n] + double(right)
+        values = assemble_z(values, comp == 2)
+        for a in range(3):
+            i = 3 * comp + a
+            for b in range(3):
+                tops = to_lane(tops, lane, values[9 * a + 3 * b + 2], 3 * i + b)
+            for c in range(2):
+                first, second, third = [values[9 * a + 3 * b + c] for b in range(3)]
+                for b, value in enumerate((first, second, third)):
+                    out[6 * i + 2 * b + c] = pltpu.roll(value, HALO, 0)
+                first = first + jnp.where(row % 2 == 1, pltpu.roll(third, 1, 0), 0.0)
+                for k, value in enumerate((first, second)):
+                    put(near_out, far_out, 4 * i + 2 * k + c, value[:HALO], value[HALO:OWN], even_y)
+                outer.append(third)
+    out[54] = pltpu.roll(tops, HALO, 0)
+    for slot in range(9):
+        both = jnp.where(row % 2 == 1, outer[2 * slot + 1], pltpu.roll(outer[2 * slot], 7, 0))
+        put(near_out, far_out, 36 + slot, both[:HALO], both[HALO:OWN], even_y)
+    inner = jnp.where(lane % 3 == 0, pltpu.roll(pltpu.roll(tops, 126, 1), 1, 0), 0.0)
+    tops = tops + jnp.where((row % 2 == 1) & (lane < 27), inner, 0.0)
+    for k in range(6):
+        speed = spread[6 * k + 2]
+        tops = to_lane(tops, lane, jnp.where(row == 0, speed, 0.0), SPEED_LANE + k)
+    put(near_out, far_out, TOPS, tops[:HALO], tops[HALO:OWN], even_y)
     for q in range(27):
-        put(near_out, far_out, 81 + q, mass_weight[q, :HALO], mass_weight[q, OWN - HALO :], even_y)
-    row = lax.broadcasted_iota(jnp.int32, (8, 128), 0)
-    for slot in range(9):
-        first, second = [spread[12 * (k // 6) + 6 * (k // 3 % 2) + k % 3] for k in (2 * slot, 2 * slot + 1)]
-        both = jnp.where(row == 0, first, pltpu.roll(second, 1, 0))[:HALO].astype(BF16)
-        near_out[108 + slot] = both
-        far_out[108 + slot] = both
-
-
-def send_planes(values, comp, near, far, even):
-    for b in range(2):
-        for c in range(3):
-            n = 3 * b + c
-            put(near, far, 6 * comp + n, values[n], values[18 + n], even)
+        put(near_out, far_out, WEIGHTS + q, mass_weight[q, :HALO], mass_weight[q, HALO:], even_y)
+    for k in range(6):
+        both = jnp.where(row == 0, spread[6 * k], pltpu.roll(spread[6 * k + 1], 1, 0))[:HALO].astype(BF16)
+        near_out[SPEEDS + k] = both
+        far_out[SPEEDS + k] = both
+
+
+def send_planes(planes, near, far, even, extra=None):
+    lane = lane_of((8, 128))
+    sides = [jnp.zeros((8, 128), F32) if extra is None else extra, jnp.zeros((8, 128), F32)]
+    for comp in range(3):
+        for b in range(2):
+            left, right = [[planes[comp][9 * a + 3 * b + c] for c in range(3)] for a in (0, 2)]
+            for c in range(2):
+                put(near, far, 4 * comp + 2 * b + c, left[c], right[c], even)
+            sides = [to_lane(side, lane, plane[2], 2 * comp + b) for side, plane in zip(sides, (left, right))]
+    put(near, far, 12, sides[0], sides[1], even)
 
 
 def apply_mass(values, weight, wall):
@@ -194,50 +236,83 @@
 ):
     even = is_even()
     even_y = is_even("brick")
-    for r in range(108):
-        low, high = get(near_in, far_in, r, even_y)
-        rows[r, :HALO] = low
-        rows[r, HALO : HALO + OWN] = own[r] if r < 81 else mass_weight[r - 81]
-        rows[r, HALO + OWN :] = high
+    row = lax.broadcasted_iota(jnp.int32, (8, 128), 0)
+    lane = lane_of((8, 128))
+    mine = (row >= HALO) & (row < HALO + OWN)
+    for k in range(SPEEDS):
+        low, high = get(near_in, far_in, k, even_y)
+        rows[k, :HALO] = low
+        rows[k, HALO + OWN :] = high
+        if k >= WEIGHTS:
+            rows[k, HALO : HALO + OWN] = mass_weight[k - WEIGHTS]
     for q in range(27):
-        weight[q] = rows[81 + q] * POINT_WEIGHT[q]
-    for comp in range(3):
-        values = [rows[27 * comp + n] for n in range(27)]
-        values = assemble_y(assemble_z(values, comp == 2))
+        weight[q] = rows[WEIGHTS + q] * POINT_WEIGHT[q]
+    edge = (row == 1) | (row == 7)
+    tops = jnp.where((lane % 3 == 2) & ~edge, 0.0, rows[TOPS])
+    tops = jnp.where(mine, own[54], tops)
+    planes = []
+    for comp in range(3):
+        values = []
+        for a in range(3):
+            i = 3 * comp + a
+            for b in range(3):
+                for c in range(2):
+                    if b < 2:
+                        halo = rows[4 * i + 2 * b + c]
+                    else:
+                        k = 2 * i + c
+                        halo = rows[36 + k // 2]
+                        halo = jnp.where(edge, halo if k % 2 == 1 else pltpu.roll(halo, 1, 0), 0.0)
+                    values.append(jnp.where(mine, own[6 * i + 2 * b + c], halo))
+                values.append(third_along_z(values[-2], tops, lane, 3 * i + b))
+        values = assemble_y(values)
         for n in range(27):
             field[27 * comp + n] = values[n]
         values = apply_mass(values, weight, comp == 2)
         for n in range(27):
             image[27 * comp + n] = values[n]
-        send_planes(values, comp, near, far, even)
-    row = lax.broadcasted_iota(jnp.int32, (8, 128), 0)
+        planes.append(values)
+    edge_tops = get(near_in, far_in, TOPS, even_y)[1]
+    edge_tops = jnp.concatenate([edge_tops] * 4, axis=0)
     plane = []
+    tops = jnp.zeros((8, 128), F32)
     for comp in range(3):
         for a in range(2):
-            speed = [spread[12 * comp + 6 * a + n] for n in range(6)]
-            for c in range(3):
-                k = 6 * comp + 3 * a + c
-                beyond = get(near_in, far_in, 108 + k // 2, even_y)[1][k % 2 : k % 2 + 1]
-                speed.append(jnp.where(row == OWN - 1, beyond, pltpu.roll(speed[c], 7, 0)))
+            k = 2 * comp + a
+            speed = [spread[6 * k + n] for n in range(6)]
+            beyond = get(near_in, far_in, SPEEDS + k, even_y)[1]
+            beyond = [beyond[c : c + 1] for c in range(2)]
+            for c in range(2):
+                speed.append(jnp.where(row == OWN - 1, beyond[c], pltpu.roll(speed[c], 7, 0)))
+            third = third_along_z(jnp.broadcast_to(beyond[0], (8, 128)), edge_tops, lane, SPEED_LANE + k)[0:1]
+            speed.append(jnp.where(row == OWN - 1, third, pltpu.roll(speed[2], 7, 0)))
             for n in range(9):
                 speeds[18 * comp + 9 * a + n] = speed[n]
             if a == 0:
-                plane += speed
-    for n in range(0, 27, 2):
-        upper = plane[n] if n == 26 else pltpu.roll(plane[n + 1], 4, 0)
-        both = jnp.where(row < OWN, plane[n], upper).astype(BF16)
-        near[18 + n // 2] = both
-        far[18 + n // 2] = both
+                for b in range(3):
+                    plane += speed[3 * b : 3 * b + 2]
+                    tops = to_lane(tops, lane, speed[3 * b + 2], SPEED_LANE + 3 * comp + b)
+    send_planes(planes, near, far, even, tops)
+    for k in range(9):
+        both = jnp.where(row < OWN, plane[2 * k], pltpu.roll(plane[2 * k + 1], OWN, 0)).astype(BF16)
+        near[13 + k] = both
+        far[13 + k] = both
 
 
 def take_planes(image, near, far, comp, even):
     values = [image[27 * comp + n] for n in range(27)]
+    lane = lane_of((8, 128))
+    tops = get(near, far, 12, even)
     for b in range(2):
-        for c in range(3):
+        for c in range(2):
             n = 3 * b + c
-            left, right = get(near, far, 6 * comp + n, even)
+            left, right = get(near, far, 4 * comp + 2 * b + c, even)
             values[n] = values[n] + left
             values[18 + n] = values[18 + n] + right
+        for a, top in zip((0, 18), tops):
+            n = a + 3 * b
+            top = values[n + 2] + pltpu.roll(top, 127 - 2 * comp - b, 1)
+            values[n + 2] = jnp.where(lane == 127, top, pltpu.roll(values[n], 127, 1))
     for a in (0, 18):
         for c in range(3):
             values[a + 6 + c] = pltpu.roll(values[a + c], 7, 0)
@@ -246,6 +321,7 @@
 
 def second_kernel(image, far_in, near_in, weight, field, image_out, near, far):
     even = is_even()
+    planes = []
     for comp in range(3):
         values = take_planes(image, near_in, far_in, comp, even)
         for n in range(27):
@@ -253,23 +329,26 @@
         values = apply_mass(values, weight, comp == 2)
         for n in range(27):
             image_out[27 * comp + n] = values[n]
-        send_planes(values, comp, near, far, even)
+        planes.append(values)
+    send_planes(planes, near, far, even)
 
 
 def work_kernel(geometry, density, energy, material, energy_mass, speeds, far, near, out):
     even = is_even()
     pressure = pressure_of(density, energy, material)
     work = jnp.zeros_like(pressure)
-    upper = lax.broadcasted_iota(jnp.int32, (8, 128), 0) >= OWN
-    for comp in range(3):
-        for n in range(27):
-            if n < 18:
-                speed, odd = speeds[18 * comp + n], False
-            else:
-                k = 9 * comp + n - 18
-                speed, odd = get(near, far, 18 + k // 2, even)[1], k % 2 == 1
-            speed = jnp.where(upper == odd, speed, pltpu.roll(speed, OWN, 0))
-            work = work + geometry[pl.ds(4 * (27 * comp + n), 4)].astype(F32) * speed[None]
+    row = lax.broadcasted_iota(jnp.int32, (8, 128), 0)
+    lane = lane_of((8, 128))
+    tops = get(near, far, 12, even)[1]
+    for comp in range(3):
+        speed = [speeds[18 * comp + n] for n in range(18)]
+        for b in range(3):
+            both = get(near, far, 13 + 3 * comp + b, even)[1]
+            speed += [both, pltpu.roll(both, OWN, 0)]
+            speed.append(third_along_z(both, tops, lane, SPEED_LANE + 3 * comp + b))
+        for n in range(27):
+            value = jnp.where(row < OWN, speed[n], pltpu.roll(speed[n], OWN, 0))
+            work = work + geometry[pl.ds(4 * (27 * comp + n), 4)].astype(F32) * value[None]
     out[...] = energy[...] + HALF_STEP * pressure * work / energy_mass[...]
 
 
@@ -418,7 +497,7 @@
 
     force, near, far = call(
         force_kernel,
-        [(81,) + tile, (27,) + tile, (27,) + tile],
+        [(81,) + full, (27,) + tile, (27,) + tile],
         *[pltpu.with_memory_space_constraint(x, pltpu.HBM) for x in (geometry, density, energy, material, mass_weight)],
         scratch=[
             pltpu.VMEM((324,) + full, BF16),
@@ -435,22 +514,22 @@
     near, far = swap(near, far)
     own, near, far = call(
         rim_kernel,
-        [(81,) + tile, (117,) + pair, (117,) + pair],
+        [(55,) + full, (MESSAGE,) + pair, (MESSAGE,) + pair],
         force, far, near, mass_weight, spread,
         dtypes=[F32, BF16, BF16],
     )
     near, far = swap(near, far, "brick")
     zeroth, weight, image, near, far, speeds = call(
         first_kernel,
-        [(81,) + full, (27,) + full, (81,) + full, (32,) + full, (32,) + full, (54,) + full],
+        [(81,) + full, (27,) + full, (81,) + full, (22,) + full, (22,) + full, (54,) + full],
         own, far, near, mass_weight, spread,
-        scratch=[pltpu.VMEM((108,) + full, F32)],
+        scratch=[pltpu.VMEM((SPEEDS,) + full, F32)],
         dtypes=[F32, F32, F32, BF16, BF16, F32],
     )
     near, far = swap(near, far)
     first, image, near_out, far_out = call(
         second_kernel,
-        [(81,) + full, (81,) + full, (18,) + full, (18,) + full],
+        [(81,) + full, (81,) + full, (13,) + full, (13,) + full],
         image, far, near, weight,
         dtypes=[F32, F32, BF16, BF16],
     )
@@ -462,7 +541,6 @@
     second, moments = call(
         moment_kernel, [(81,) + full, (devices, 128)], image, far, near, weight, first, products
     )
-    moments = pltpu.with_memory_space_constraint(moments, pltpu.VMEM)
     moments = lax.all_to_all(moments, ("slab", "brick"), 0, 0, tiled=True)
     (nodal,) = call(nodal_kernel, [(3, 48, 384)], zeroth, first, second)
     (velocity_half,) = call(last_kernel, [velocity.shape], moments, nodal, velocity)

time: 37.9 us -> 37.4 us (0.987)
  starting transfers between devices: 13 us -> 12.2 us
    ppermute x4, starting transfers between devices: 9.4 us -> 8.88 us  [swap(): lax.ppermute(far, axis, [(i, (i + (1 if i % 2 else -1)) % count) for i in...]
where the time goes in v5:
time: 37.4 us; the launch traced here: 37.2 us
  waiting for transfers between devices  17.4 us (47%)
  starting transfers between devices  12.2 us (33%)
  Pallas kernels  6.23 us (17%)
  between operations  0.73 us (2%)
  local copies, waits for them, and re-layouts  0.66 us (2%)
    ppermute x4, waiting for transfers between devices, swap(): lax.ppermute(far, axis, [(i, (i + (1 if i % 2 else -1)) % count) for i in...  10.6 us
    ppermute x4, starting transfers between devices, swap(): lax.ppermute(far, axis, [(i, (i + (1 if i % 2 else -1)) % count) for i in...  8.88 us
    pallas_call x10, Pallas kernels, call(): pl.pallas_call(kernel, out_shape=shapes, in_specs=[place] * len(args), ou...  6.23 us
    all_to_all x1, waiting for transfers between devices, local(): moments = lax.all_to_all(moments, ('slab', 'brick'), 0, 0, tiled=True)  4.8 us
    all_to_all x1, starting transfers between devices, local(): moments = lax.all_to_all(moments, ('slab', 'brick'), 0, 0, tiled=True)  2.93 us
    ppermute x4, waiting for transfers between devices, swap(): lax.ppermute(near, axis, [(i, i + (-1 if i % 2 else 1)) for i in range(co...  1.95 us
  transfers between devices with their start and end apart: 9, of which 6 were waited for; matrix products, arithmetic and copies ran while one was open for 0% of the time, Pallas kernels for 5%

profile of v5, /device:TPU:0, one launch (start us, length us, event | category | flops | bytes accessed | tf_op | source)
XLA Modules:
  0.0 37.2 jit_solution(9396144364292732635)
XLA Ops:
  0.6 0.0 copy-start.2
  0.6 1.4 %force_kernel.1 = (f32[81,8,128]{2,1,0:T(8,128)S(1)}, bf16[27,4,128]{2,1,0:T(4,128)(2,1)S(1)}, bf16[27,4,128]{2,1,0:T(4,128)(2,1)S(1)}) custom-call(bf16[324,8,128]{2,1,0:T(8,128)(2,1)} %bitcast.13, f32[4,8,128]{2,1,0:T(8,128)} %bitcast.18, f32[4,8,128]{2,1,0:T(8,128)} %bitcast.20, s32[4,128]{1,0:T(4,128)} %bitcast.24, f32[27,4,128]{2,1,0:T(4,128)} %bitcast.15), custom_call_target="tpu_custom_call" | custom-call | flops 100000 | bytes 1196032 | tf_op jit(solution)/shard_map/force_kernel/pallas_call | solution.py:467
  2.0 3.4 %collective-permute-start = (bf16[27,4,128]{2,1,0:T(4,128)(2,1)S(1)}, bf16[27,4,128]{2,1,0:T(4,128)(2,1)S(1)}, u32[]{:S(2)}, u32[]{:S(2)}) collective-permute-start(bf16[27,4,128]{2,1,0:T(4,128)(2,1)S(1)} %get-tuple-element.21), channel_id=1, source_target_pairs={{0,28},{4,8},{8,4},{12,16},{16,12},{20,24},{24,20},{28,0},{1,29},{... | collective-permute-start | bytes 82952 | tf_op jit(solution)/shard_map/ppermute | solution.py:481
  5.4 0.0 collective-permute-start.1
  5.4 0.0 copy-done.2
  5.4 0.3 spread_kernel.1.spread
  5.7 1.2 %collective-permute-done.far = bf16[27,4,128]{2,1,0:T(4,128)(2,1)S(1)} collective-permute-done((bf16[27,4,128]{2,1,0:T(4,128)(2,1)S(1)}, bf16[27,4,128]{2,1,0:T(4,128)(2,1)S(1)}, u32[]{:S(2)}, u32[]{:S(2)}) %collective-permute-start) | collective-permute-done | bytes 27680 | tf_op jit(solution)/shard_map/ppermute | solution.py:481
  7.0 0.0 collective-permute-done.1.near
  7.0 0.3 rim_kernel.1
  7.3 4.6 %collective-permute-start.2 = (bf16[79,2,128]{2,1,0:T(2,128)(2,1)S(1)}, bf16[79,2,128]{2,1,0:T(2,128)(2,1)S(1)}, u32[]{:S(2)}, u32[]{:S(2)}) collective-permute-start(bf16[79,2,128]{2,1,0:T(2,128)(2,1)S(1)} %get-tuple-element.24), channel_id=1, source_target_pairs={{0,3},{1,2},{2,1},{3,0},{4,7},{5,6},{6,5},{7,4},{8,11},{9,10},{10,... | collective-permute-start | bytes 121352 | tf_op jit(solution)/shard_map/ppermute | solution.py:481
  11.9 0.0 collective-permute-start.3
  11.9 2.0 %collective-permute-done.2.far_in = bf16[79,2,128]{2,1,0:T(2,128)(2,1)S(1)} collective-permute-done((bf16[79,2,128]{2,1,0:T(2,128)(2,1)S(1)}, bf16[79,2,128]{2,1,0:T(2,128)(2,1)S(1)}, u32[]{:S(2)}, u32[]{:S(2)}) %collective-permute-start.2) | collective-permute-done | bytes 40480 | tf_op jit(solution)/shard_map/ppermute | solution.py:481
  14.0 1.9 %collective-permute-done.3.near_in = bf16[79,2,128]{2,1,0:T(2,128)(2,1)S(1)} collective-permute-done((bf16[79,2,128]{2,1,0:T(2,128)(2,1)S(1)}, bf16[79,2,128]{2,1,0:T(2,128)(2,1)S(1)}, u32[]{:S(2)}, u32[]{:S(2)}) %collective-permute-start.3) | collective-permute-done | bytes 40480 | tf_op jit(solution)/shard_map/ppermute | solution.py:482
  15.9 0.5 %first_kernel.1 = (f32[81,8,128]{2,1,0:T(8,128)S(1)}, f32[27,8,128]{2,1,0:T(8,128)S(1)}, f32[81,8,128]{2,1,0:T(8,128)S(1)}, bf16[22,8,128]{2,1,0:T(8,128)(2,1)S(...) custom-call(f32[55,8,128]{2,1,0:T(8,128)S(1)} %get-tuple-element.23.own, ...), custom_call_target="tpu_custom_call" | custom-call | flops 100000 | bytes 1684480 | tf_op jit(solution)/shard_map/first_kernel/pallas_call | solution.py:467
  16.4 0.3 collective-permute-start.4
  16.8 0.4 %collective-permute-start.5 = (bf16[22,8,128]{2,1,0:T(8,128)(2,1)S(1)}, bf16[22,8,128]{2,1,0:T(8,128)(2,1)S(1)}, u32[]{:S(2)}, u32[]{:S(2)}) collective-permute-start(bf16[22,8,128]{2,1,0:T(8,128)(2,1)S(1)} %get-tuple-element.28), channel_id=1, source_target_pairs={{0,4},{4,0},{8,12},{12,8},{16,20},{20,16},{24,28},{28,24},{1,5},{5... | collective-permute-start | bytes 135176 | tf_op jit(solution)/shard_map/ppermute | solution.py:482
  17.2 3.7 %collective-permute-done.4.far_in.far = bf16[22,8,128]{2,1,0:T(8,128)(2,1)S(1)} collective-permute-done((bf16[22,8,128]{2,1,0:T(8,128)(2,1)S(1)}, bf16[22,8,128]{2,1,0:T(8,128)(2,1)S(1)}, u32[]{:S(2)}, u32[]{:S(2)}) %collective-permute-start.4) | collective-permute-done | bytes 45088 | tf_op jit(solution)/shard_map/ppermute | solution.py:481
  20.9 0.0 collective-permute-done.5.near_in.near
  20.9 0.4 %second_kernel.1 = (f32[81,8,128]{2,1,0:T(8,128)S(1)}, f32[81,8,128]{2,1,0:T(8,128)S(1)}, bf16[13,8,128]{2,1,0:T(8,128)(2,1)S(1)}, bf16[13,8,128]{2,1,0:T(8,128)(2,1)S(1)}) custom-call(f32[81,8,128]{2,1,0:T(8,128)S(1)} %get-tuple-element.26.image, bf16[22,8,128]{2,1,0:T(8,128)(2,1)S(1)} %collective-permute-done.4.far_in.far, ...), custom_call_target="tpu_custom_call" | custom-call | flops 100000 | bytes 1302528 | tf_op jit(solution)/shard_map/second_kernel/pallas_call | solution.py:467
  21.3 0.5 %collective-permute-start.6 = (bf16[13,8,128]{2,1,0:T(8,128)(2,1)S(1)}, bf16[13,8,128]{2,1,0:T(8,128)(2,1)S(1)}, u32[]{:S(2)}, u32[]{:S(2)}) collective-permute-start(bf16[13,8,128]{2,1,0:T(8,128)(2,1)S(1)} %get-tuple-element.31), channel_id=1, source_target_pairs={{0,28},{4,8},{8,4},{12,16},{16,12},{20,24},{24,20},{28,0},{1,29},{... | collective-permute-start | bytes 79880 | tf_op jit(solution)/shard_map/ppermute | solution.py:481
  21.8 0.0 collective-permute-start.7
  21.8 0.1 product_kernel.1.products
  21.9 3.6 %collective-permute-done.6.far = bf16[13,8,128]{2,1,0:T(8,128)(2,1)S(1)} collective-permute-done((bf16[13,8,128]{2,1,0:T(8,128)(2,1)S(1)}, bf16[13,8,128]{2,1,0:T(8,128)(2,1)S(1)}, u32[]{:S(2)}, u32[]{:S(2)}) %collective-permute-start.6) | collective-permute-done | bytes 26656 | tf_op jit(solution)/shard_map/ppermute | solution.py:481
  25.5 0.0 collective-permute-done.7.near
  25.5 0.9 %moment_kernel.1 = (f32[81,8,128]{2,1,0:T(8,128)S(1)}, f32[32,128]{1,0:T(8,128)}) custom-call(f32[81,8,128]{2,1,0:T(8,128)S(1)} %get-tuple-element.30.image, bf16[13,8,128]{2,1,0:T(8,128)(2,1)S(1)} %collective-permute-done.6.far, bf16[13,8,128]{2,1,0:T(8,128)(2,1)S(1)} %collective-permute-done.7.near, f32[27,8,128]{2,1,0:T(8,128)S(1)} %get-tuple-element.29.weight, ...), custom_call_target="tpu_custom_call" | custom-call | flops 100000 | bytes 1187840 | tf_op jit(solution)/shard_map/moment_kernel/pallas_call | solution.py:467
  26.4 2.9 %all-to-all-start = ((f32[32,1,128]{2,1,0:T(1,128)}), f32[32,1,128]{2,1,0:T(1,128)S(1)}, u32[]{:S(2)}, u32[]{:S(2)}) async-start(f32[32,1,128]{2,1,0:T(1,128)} %bitcast.6), calls=%async_computation | async-start | bytes 32768 | tf_op jit(solution)/shard_map/all_to_all | solution.py:544
  29.3 0.0 copy-start.6
  29.4 0.6 %copy-done.6 = s32[1,4,128]{2,1,0:T(4,128)S(1)} copy-done((s32[1,4,128]{2,1,0:T(4,128)S(1)}, s32[1,4,128]{2,1,0:T(4,128)}, u32[]{:S(2)}) %copy-start.6) | copy-done | bytes 2072
  30.0 0.8 %work_kernel.1 = f32[4,8,128]{2,1,0:T(8,128)} custom-call(bf16[324,8,128]{2,1,0:T(8,128)(2,1)S(1)} %bitcast.14, f32[4,8,128]{2,1,0:T(8,128)S(1)} %bitcast.19, f32[4,8,128]{2,1,0:T(8,128)S(1)} %bitcast.21, s32[4,128]{1,0:T(4,128)S(1)} %bitcast.25, f32[4,8,128]{2,1,0:T(8,128)S(1)} %bitcast.23, f32[54,8,128]{2,1,0:T(8,128)S(1)} %get-tuple-element.37.speeds, ...), custom_call_target="tpu_custom_call" | custom-call | flops 100000 | bytes 1042432 | tf_op jit(solution)/shard_map/work_kernel/pallas_call | solution.py:467
  30.8 0.8 %nodal_kernel.1.nodal = f32[3,48,384]{2,1,0:T(8,128)S(1)} custom-call(f32[81,8,128]{2,1,0:T(8,128)S(1)} %get-tuple-element.34.zeroth, f32[81,8,128]{2,1,0:T(8,128)S(1)} %get-tuple-element.33.first, f32[81,8,128]{2,1,0:T(8,128)S(1)} %get-tuple-element.36.second), custom_call_target="tpu_custom_call" | custom-call | flops 100000 | bytes 1216512 | tf_op jit(solution)/shard_map/nodal_kernel/pallas_call | solution.py:467
  31.6 4.8 %all-to-all-done = f32[32,1,128]{2,1,0:T(1,128)S(1)} async-done(((f32[32,1,128]{2,1,0:T(1,128)}), f32[32,1,128]{2,1,0:T(1,128)S(1)}, u32[]{:S(2)}, u32[]{:S(2)}) %all-to-all-start) | async-done | bytes 16416 | tf_op jit(solution)/shard_map/all_to_all | solution.py:544
  36.4 0.8 %last_kernel.1 = f32[3,2,8,257]{3,2,1,0:T(8,128)} custom-call(f32[32,128]{1,0:T(8,128)S(1)} %bitcast.22, f32[3,48,384]{2,1,0:T(8,128)S(1)} %nodal_kernel.1.nodal, f32[3,2,8,257]{3,2,1,0:T(8,128)S(1)} %copy-done.2), custom_call_target="tpu_custom_call" | custom-call | flops 100000 | bytes 336256 | tf_op jit(solution)/shard_map/last_kernel/pallas_call | solution.py:467
  (10 shorter events, 0.0 us)
Async XLA Ops:
  0.6 4.8 %copy-start.2 = (f32[3,2,8,257]{3,2,1,0:T(8,128)S(1)}, f32[3,2,8,257]{3,2,1,0:T(8,128)}, u32[]{:S(2)}) copy-start(f32[3,2,8,257]{3,2,1,0:T(8,128)} %velocity.3) | copy-start | bytes 148036
  2.0 4.9 %collective-permute-start = (bf16[27,4,128]{2,1,0:T(4,128)(2,1)S(1)}, bf16[27,4,128]{2,1,0:T(4,128)(2,1)S(1)}, u32[]{:S(2)}, u32[]{:S(2)}) collective-permute-start(bf16[27,4,128]{2,1,0:T(4,128)(2,1)S(1)} %get-tuple-element.21), channel_id=1, source_target_pairs={{0,28},{4,8},{8,4},{12,16},{16,12},{20,24},{24,20},{28,0},{1,29},{... | collective-permute-start | bytes 82952 | tf_op jit(solution)/shard_map/ppermute | solution.py:481
  5.4 1.6 %copy-start.1 = (f32[27,1,4,128]{3,2,1,0:T(4,128)S(1)}, f32[27,1,4,128]{3,2,1,0:T(4,128)}, u32[]{:S(2)}) copy-start(f32[27,1,4,128]{3,2,1,0:T(4,128)} %param.12) | copy-start | bytes 165892
  5.4 1.6 %collective-permute-start.1 = (bf16[27,4,128]{2,1,0:T(4,128)(2,1)S(1)}, bf16[27,4,128]{2,1,0:T(4,128)(2,1)S(1)}, u32[]{:S(2)}, u32[]{:S(2)}) collective-permute-start(bf16[27,4,128]{2,1,0:T(4,128)(2,1)S(1)} %get-tuple-element.22), channel_id=1, source_target_pairs={{0,4},{4,0},{8,12},{12,8},{16,20},{20,16},{24,28},{28,24},{1,5},{5... | collective-permute-start | bytes 82952 | tf_op jit(solution)/shard_map/ppermute | solution.py:482
  7.3 6.7 %collective-permute-start.2 = (bf16[79,2,128]{2,1,0:T(2,128)(2,1)S(1)}, bf16[79,2,128]{2,1,0:T(2,128)(2,1)S(1)}, u32[]{:S(2)}, u32[]{:S(2)}) collective-permute-start(bf16[79,2,128]{2,1,0:T(2,128)(2,1)S(1)} %get-tuple-element.24), channel_id=1, source_target_pairs={{0,3},{1,2},{2,1},{3,0},{4,7},{5,6},{6,5},{7,4},{8,11},{9,10},{10,... | collective-permute-start | bytes 121352 | tf_op jit(solution)/shard_map/ppermute | solution.py:481
  11.9 4.0 %collective-permute-start.3 = (bf16[79,2,128]{2,1,0:T(2,128)(2,1)S(1)}, bf16[79,2,128]{2,1,0:T(2,128)(2,1)S(1)}, u32[]{:S(2)}, u32[]{:S(2)}) collective-permute-start(bf16[79,2,128]{2,1,0:T(2,128)(2,1)S(1)} %get-tuple-element.25), channel_id=1, source_target_pairs={{0,1},{1,0},{2,3},{3,2},{4,5},{5,4},{6,7},{7,6},{8,9},{9,8},{10,11... | collective-permute-start | bytes 121352 | tf_op jit(solution)/shard_map/ppermute | solution.py:482
  16.4 4.4 %collective-permute-start.4 = (bf16[22,8,128]{2,1,0:T(8,128)(2,1)S(1)}, bf16[22,8,128]{2,1,0:T(8,128)(2,1)S(1)}, u32[]{:S(2)}, u32[]{:S(2)}) collective-permute-start(bf16[22,8,128]{2,1,0:T(8,128)(2,1)S(1)} %get-tuple-element.27), channel_id=1, source_target_pairs={{0,28},{4,8},{8,4},{12,16},{16,12},{20,24},{24,20},{28,0},{1,29},{... | collective-permute-start | bytes 135176 | tf_op jit(solution)/shard_map/ppermute | solution.py:481
  16.8 4.1 %collective-permute-start.5 = (bf16[22,8,128]{2,1,0:T(8,128)(2,1)S(1)}, bf16[22,8,128]{2,1,0:T(8,128)(2,1)S(1)}, u32[]{:S(2)}, u32[]{:S(2)}) collective-permute-start(bf16[22,8,128]{2,1,0:T(8,128)(2,1)S(1)} %get-tuple-element.28), channel_id=1, source_target_pairs={{0,4},{4,0},{8,12},{12,8},{16,20},{20,16},{24,28},{28,24},{1,5},{5... | collective-permute-start | bytes 135176 | tf_op jit(solution)/shard_map/ppermute | solution.py:482
  21.3 4.2 %collective-permute-start.6 = (bf16[13,8,128]{2,1,0:T(8,128)(2,1)S(1)}, bf16[13,8,128]{2,1,0:T(8,128)(2,1)S(1)}, u32[]{:S(2)}, u32[]{:S(2)}) collective-permute-start(bf16[13,8,128]{2,1,0:T(8,128)(2,1)S(1)} %get-tuple-element.31), channel_id=1, source_target_pairs={{0,28},{4,8},{8,4},{12,16},{16,12},{20,24},{24,20},{28,0},{1,29},{... | collective-permute-start | bytes 79880 | tf_op jit(solution)/shard_map/ppermute | solution.py:481
  21.8 3.7 %collective-permute-start.7 = (bf16[13,8,128]{2,1,0:T(8,128)(2,1)S(1)}, bf16[13,8,128]{2,1,0:T(8,128)(2,1)S(1)}, u32[]{:S(2)}, u32[]{:S(2)}) collective-permute-start(bf16[13,8,128]{2,1,0:T(8,128)(2,1)S(1)} %get-tuple-element.32), channel_id=1, source_target_pairs={{0,4},{4,0},{8,12},{12,8},{16,20},{20,16},{24,28},{28,24},{1,5},{5... | collective-permute-start | bytes 79880 | tf_op jit(solution)/shard_map/ppermute | solution.py:482
  21.8 7.5 %copy-start = (bf16[81,8,1,4,128]{4,3,2,1,0:T(4,128)(2,1)S(1)}, bf16[81,8,1,4,128]{4,3,2,1,0:T(4,128)(2,1)}, u32[]{:S(2)}) copy-start(bf16[81,8,1,4,128]{4,3,2,1,0:T(4,128)(2,1)} %param.11) | copy-start | bytes 1990660
  25.5 3.8 %copy-start.5 = (f32[8,1,4,128]{3,2,1,0:T(4,128)S(1)}, f32[8,1,4,128]{3,2,1,0:T(4,128)}, u32[]{:S(2)}) copy-start(f32[8,1,4,128]{3,2,1,0:T(4,128)} %param.13) | copy-start | bytes 49156
  26.4 3.0 %copy-start.3 = (f32[8,1,4,128]{3,2,1,0:T(4,128)S(1)}, f32[8,1,4,128]{3,2,1,0:T(4,128)}, u32[]{:S(2)}) copy-start(f32[8,1,4,128]{3,2,1,0:T(4,128)} %param.9) | copy-start | bytes 49156
  26.4 3.0 %copy-start.4 = (f32[8,1,4,128]{3,2,1,0:T(4,128)S(1)}, f32[8,1,4,128]{3,2,1,0:T(4,128)}, u32[]{:S(2)}) copy-start(f32[8,1,4,128]{3,2,1,0:T(4,128)} %param.8) | copy-start | bytes 49156
  26.4 10.0 %all-to-all-start = ((f32[32,1,128]{2,1,0:T(1,128)}), f32[32,1,128]{2,1,0:T(1,128)S(1)}, u32[]{:S(2)}, u32[]{:S(2)}) async-start(f32[32,1,128]{2,1,0:T(1,128)} %bitcast.6), calls=%async_computation | async-start | bytes 32768 | tf_op jit(solution)/shard_map/all_to_all | solution.py:544
  29.3 0.7 %copy-start.6 = (s32[1,4,128]{2,1,0:T(4,128)S(1)}, s32[1,4,128]{2,1,0:T(4,128)}, u32[]{:S(2)}) copy-start(s32[1,4,128]{2,1,0:T(4,128)} %param.10) | copy-start | bytes 6148

commit v6 on v5

--- a/solution.py
+++ b/solution.py
@@ -55,7 +55,7 @@
     values = list(values)
     lane = lane_of(values[0].shape)
     first, last = lane == 0, lane == 127
-    for i, _, k in lines(2):
+    for i, k in [(n, n + 2) for n in range(0, len(values), 3)]:
         total = values[i] + jnp.where(first, 0.0, pltpu.roll(values[k], 1, 1))
         top = values[k]
         if wall:
@@ -145,7 +145,7 @@
             put(near, far, 9 * comp + n, values[n][:OWN], values[18 + n][:OWN], even)
 
 
-def spread_kernel(velocity, out):
+def spread_velocity(velocity, out):
     rows = velocity[...].astype(BF16).reshape(48, velocity.shape[3])
     low = rows[:, :256]
     high = rows[:, 256:257].astype(F32)
@@ -169,53 +169,81 @@
 SPEED_LANE = 32
 
 
-def rim_kernel(field, far, near, mass_weight, spread, out, near_out, far_out):
+def fill_plane(values, comp, a, tops, out, near, far, even_y):
+    row = lax.broadcasted_iota(jnp.int32, (8, 128), 0)
+    lane = lane_of((8, 128))
+    i = 3 * comp + a
+    outer = []
+    for b in range(3):
+        tops = to_lane(tops, lane, values[9 * a + 3 * b + 2], 3 * i + b)
+    for c in range(2):
+        first, second, third = [values[9 * a + 3 * b + c] for b in range(3)]
+        for b, value in enumerate((first, second, third)):
+            out[6 * i + 2 * b + c] = pltpu.roll(value, HALO, 0)
+        first = first + jnp.where(row % 2 == 1, pltpu.roll(third, 1, 0), 0.0)
+        for k, value in enumerate((first, second)):
+            put(near, far, 4 * i + 2 * k + c, value[:HALO], value[HALO:OWN], even_y)
+        outer.append(third)
+    both = jnp.where(row % 2 == 1, outer[1], pltpu.roll(outer[0], 7, 0))
+    put(near, far, 36 + i, both[:HALO], both[HALO:OWN], even_y)
+    return tops
+
+
+def spread_kernel(velocity, field, mass_weight, spread, middle, near, far):
+    even_y = is_even("brick")
+    row = lax.broadcasted_iota(jnp.int32, (8, 128), 0)
+    lane = lane_of((8, 128))
+    spread_velocity(velocity, spread)
+    tops = jnp.zeros((8, 128), F32)
+    for comp in range(3):
+        values = [field[27 * comp + 9 + n] for n in range(9)]
+        values = [None] * 9 + assemble_z(values, comp == 2)
+        tops = fill_plane(values, comp, 1, tops, middle, near, far, even_y)
+    for k in range(6):
+        tops = to_lane(tops, lane, jnp.where(row == 0, spread[6 * k + 2], 0.0), SPEED_LANE + k)
+    middle[54] = tops
+    for q in range(27):
+        put(near, far, WEIGHTS + q, mass_weight[q, :HALO], mass_weight[q, HALO:], even_y)
+    for k in range(6):
+        both = jnp.where(row == 0, spread[6 * k], pltpu.roll(spread[6 * k + 1], 1, 0))[:HALO].astype(BF16)
+        near[SPEEDS + k] = both
+        far[SPEEDS + k] = both
+
+
+def rim_kernel(field, far, near, middle, near_in, far_in, out, near_out, far_out):
     even = is_even()
     even_y = is_even("brick")
     row = lax.broadcasted_iota(jnp.int32, (8, 128), 0)
     lane = lane_of((8, 128))
-    tops = jnp.zeros((8, 128), F32)
-    outer = []
-    for comp in range(3):
+    tops = middle[54]
+    for comp in range(3):
+        i = 3 * comp + 1
+        for k in range(6):
+            out[6 * i + k] = middle[6 * i + k]
+        for k in [4 * i, 4 * i + 1, 4 * i + 2, 4 * i + 3, 36 + i]:
+            near_out[k] = near_in[k]
+            far_out[k] = far_in[k]
         values = [field[27 * comp + n] for n in range(27)]
         for n in range(9):
             left, right = get(near, far, 9 * comp + n, even)
             values[n] = values[n] + double(left)
             values[18 + n] = values[18 + n] + double(right)
-        values = assemble_z(values, comp == 2)
-        for a in range(3):
-            i = 3 * comp + a
-            for b in range(3):
-                tops = to_lane(tops, lane, values[9 * a + 3 * b + 2], 3 * i + b)
-            for c in range(2):
-                first, second, third = [values[9 * a + 3 * b + c] for b in range(3)]
-                for b, value in enumerate((first, second, third)):
-                    out[6 * i + 2 * b + c] = pltpu.roll(value, HALO, 0)
-                first = first + jnp.where(row % 2 == 1, pltpu.roll(third, 1, 0), 0.0)
-                for k, value in enumerate((first, second)):
-                    put(near_out, far_out, 4 * i + 2 * k + c, value[:HALO], value[HALO:OWN], even_y)
-                outer.append(third)
+        values = assemble_z(values[:9] + values[18:], comp == 2)
+        values = values[:9] + [None] * 9 + values[9:]
+        for a in (0, 2):
+            tops = fill_plane(values, comp, a, tops, out, near_out, far_out, even_y)
     out[54] = pltpu.roll(tops, HALO, 0)
-    for slot in range(9):
-        both = jnp.where(row % 2 == 1, outer[2 * slot + 1], pltpu.roll(outer[2 * slot], 7, 0))
-        put(near_out, far_out, 36 + slot, both[:HALO], both[HALO:OWN], even_y)
     inner = jnp.where(lane % 3 == 0, pltpu.roll(pltpu.roll(tops, 126, 1), 1, 0), 0.0)
     tops = tops + jnp.where((row % 2 == 1) & (lane < 27), inner, 0.0)
-    for k in range(6):
-        speed = spread[6 * k + 2]
-        tops = to_lane(tops, lane, jnp.where(row == 0, speed, 0.0), SPEED_LANE + k)
     put(near_out, far_out, TOPS, tops[:HALO], tops[HALO:OWN], even_y)
-    for q in range(27):
-        put(near_out, far_out, WEIGHTS + q, mass_weight[q, :HALO], mass_weight[q, HALO:], even_y)
-    for k in range(6):
-        both = jnp.where(row == 0, spread[6 * k], pltpu.roll(spread[6 * k + 1], 1, 0))[:HALO].astype(BF16)
-        near_out[SPEEDS + k] = both
-        far_out[SPEEDS + k] = both
-
-
-def send_planes(planes, near, far, even, extra=None):
-    lane = lane_of((8, 128))
-    sides = [jnp.zeros((8, 128), F32) if extra is None else extra, jnp.zeros((8, 128), F32)]
+    for k in range(WEIGHTS, MESSAGE):
+        near_out[k] = near_in[k]
+        far_out[k] = far_in[k]
+
+
+def send_planes(planes, near, far, even):
+    lane = lane_of((8, 128))
+    sides = [jnp.zeros((8, 128), F32)] * 2
     for comp in range(3):
         for b in range(2):
             left, right = [[planes[comp][9 * a + 3 * b + c] for c in range(3)] for a in (0, 2)]
@@ -232,7 +260,7 @@
 
 
 def first_kernel(
-    own, far_in, near_in, mass_weight, spread, field, weight, image, near, far, speeds, rows
+    own, far_in, near_in, mass_weight, field, weight, image, near, far, rows
 ):
     even = is_even()
     even_y = is_even("brick")
@@ -272,6 +300,13 @@
         for n in range(27):
             image[27 * comp + n] = values[n]
         planes.append(values)
+    send_planes(planes, near, far, even)
+
+
+def speed_kernel(far_in, near_in, spread, speeds, plane_out):
+    even_y = is_even("brick")
+    row = lax.broadcasted_iota(jnp.int32, (8, 128), 0)
+    lane = lane_of((8, 128))
     edge_tops = get(near_in, far_in, TOPS, even_y)[1]
     edge_tops = jnp.concatenate([edge_tops] * 4, axis=0)
     plane = []
@@ -292,25 +327,69 @@
                 for b in range(3):
                     plane += speed[3 * b : 3 * b + 2]
                     tops = to_lane(tops, lane, speed[3 * b + 2], SPEED_LANE + 3 * comp + b)
-    send_planes(planes, near, far, even, tops)
     for k in range(9):
-        both = jnp.where(row < OWN, plane[2 * k], pltpu.roll(plane[2 * k + 1], OWN, 0)).astype(BF16)
-        near[13 + k] = both
-        far[13 + k] = both
+        plane_out[k] = jnp.where(row < OWN, plane[2 * k], pltpu.roll(plane[2 * k + 1], OWN, 0))
+    plane_out[9] = tops
+
+
+def send_own(planes, speeds, near, far, even):
+    row = lax.broadcasted_iota(jnp.int32, (8, 128), 0)
+    lane = lane_of((8, 128))
+    sides = [speeds[9], jnp.zeros((8, 128), F32)]
+    after = [jnp.zeros((8, 128), F32)] * 2
+    for comp in range(3):
+        for b in range(2):
+            both = []
+            for side, a in enumerate((0, 2)):
+                plane = [planes[comp][9 * a + 3 * b + c] for c in range(3)]
+                both.append(jnp.where(row < OWN, pltpu.roll(plane[0], 6, 0), pltpu.roll(plane[1], 2, 0)))
+                sides[side] = to_lane(sides[side], lane, plane[2], 2 * comp + b)
+                if b == 0:
+                    for c in range(2):
+                        k = 2 * comp + c
+                        after[side] = jnp.where(row == k, pltpu.roll(plane[c], (k + 2) % 8, 0), after[side])
+            put(near, far, 2 * comp + b, both[0], both[1], even)
+    put(near, far, 6, after[0], after[1], even)
+    put(near, far, 7, sides[0], sides[1], even)
+    for k in range(9):
+        near[8 + k] = speeds[k].astype(BF16)
+        far[8 + k] = speeds[k].astype(BF16)
 
 
 def take_planes(image, near, far, comp, even):
+    def read(b):
+        tiles = [get(near, far, 4 * comp + 2 * b + c, even) for c in range(2)]
+        return [[tile[side] for tile in tiles] for side in range(2)]
+
+    return add_planes(image, read, get(near, far, 12, even), comp)
+
+
+def take_own(image, near, far, comp, even):
+    row = lax.broadcasted_iota(jnp.int32, (8, 128), 0)
+    after = get(near, far, 6, even)
+
+    def read(b):
+        sides = []
+        for side, both in enumerate(get(near, far, 2 * comp + b, even)):
+            plane = [pltpu.roll(both, 2, 0), pltpu.roll(both, 6, 0)]
+            if b == 0:
+                for c in range(2):
+                    k = 2 * comp + c
+                    plane[c] = jnp.where(row == 6, pltpu.roll(after[side], 6 - k, 0), plane[c])
+            sides.append(plane)
+        return sides
+
+    return add_planes(image, read, get(near, far, 7, even), comp)
+
+
+def add_planes(image, read, tops, comp):
     values = [image[27 * comp + n] for n in range(27)]
     lane = lane_of((8, 128))
-    tops = get(near, far, 12, even)
     for b in range(2):
-        for c in range(2):
-            n = 3 * b + c
-            left, right = get(near, far, 4 * comp + 2 * b + c, even)
-            values[n] = values[n] + left
-            values[18 + n] = values[18 + n] + right
-        for a, top in zip((0, 18), tops):
+        for a, plane, top in zip((0, 18), read(b), tops):
             n = a + 3 * b
+            for c in range(2):
+                values[n + c] = values[n + c] + plane[c]
             top = values[n + 2] + pltpu.roll(top, 127 - 2 * comp - b, 1)
             values[n + 2] = jnp.where(lane == 127, top, pltpu.roll(values[n], 127, 1))
     for a in (0, 18):
@@ -319,7 +398,7 @@
     return values
 
 
-def second_kernel(image, far_in, near_in, weight, field, image_out, near, far):
+def second_kernel(image, far_in, near_in, weight, speeds, field, image_out, near, far):
     even = is_even()
     planes = []
     for comp in range(3):
@@ -330,7 +409,7 @@
         for n in range(27):
             image_out[27 * comp + n] = values[n]
         planes.append(values)
-    send_planes(planes, near, far, even)
+    send_own(planes, speeds, near, far, even)
 
 
 def work_kernel(geometry, density, energy, material, energy_mass, speeds, far, near, out):
@@ -339,11 +418,11 @@
     work = jnp.zeros_like(pressure)
     row = lax.broadcasted_iota(jnp.int32, (8, 128), 0)
     lane = lane_of((8, 128))
-    tops = get(near, far, 12, even)[1]
+    tops = get(near, far, 7, even)[1]
     for comp in range(3):
         speed = [speeds[18 * comp + n] for n in range(18)]
         for b in range(3):
-            both = get(near, far, 13 + 3 * comp + b, even)[1]
+            both = get(near, far, 8 + 3 * comp + b, even)[1]
             speed += [both, pltpu.roll(both, OWN, 0)]
             speed.append(third_along_z(both, tops, lane, SPEED_LANE + 3 * comp + b))
         for n in range(27):
@@ -376,7 +455,7 @@
     quadratic = [zero] * 3
     even = is_even()
     for comp in range(3):
-        values = take_planes(image, near, far, comp, even)
+        values = take_own(image, near, far, comp, even)
         for n in range(27):
             second[27 * comp + n] = values[n]
         values_at = {27 * comp + n: values[n] for n in range(27)}
@@ -510,33 +589,39 @@
         place=pl.BlockSpec(memory_space=pltpu.HBM),
         dtypes=[F32, BF16, BF16],
     )
-    (spread,) = call(spread_kernel, [(36,) + full], velocity)
+    spread, middle, near_part, far_part = call(
+        spread_kernel,
+        [(36,) + full, (55,) + full, (MESSAGE,) + pair, (MESSAGE,) + pair],
+        velocity, force, mass_weight,
+        dtypes=[F32, F32, BF16, BF16],
+    )
     near, far = swap(near, far)
     own, near, far = call(
         rim_kernel,
         [(55,) + full, (MESSAGE,) + pair, (MESSAGE,) + pair],
-        force, far, near, mass_weight, spread,
+        force, far, near, middle, near_part, far_part,
         dtypes=[F32, BF16, BF16],
     )
-    near, far = swap(near, far, "brick")
-    zeroth, weight, image, near, far, speeds = call(
+    near_rim, far_rim = swap(near, far, "brick")
+    zeroth, weight, image, near, far = call(
         first_kernel,
-        [(81,) + full, (27,) + full, (81,) + full, (22,) + full, (22,) + full, (54,) + full],
-        own, far, near, mass_weight, spread,
+        [(81,) + full, (27,) + full, (81,) + full, (13,) + full, (13,) + full],
+        own, far_rim, near_rim, mass_weight,
         scratch=[pltpu.VMEM((SPEEDS,) + full, F32)],
-        dtypes=[F32, F32, F32, BF16, BF16, F32],
+        dtypes=[F32, F32, F32, BF16, BF16],
     )
     near, far = swap(near, far)
-    first, image, near_out, far_out = call(
+    speeds, plane = call(speed_kernel, [(54,) + full, (10,) + full], far_rim, near_rim, spread)
+    first, image, near, far = call(
         second_kernel,
-        [(81,) + full, (81,) + full, (13,) + full, (13,) + full],
-        image, far, near, weight,
+        [(81,) + full, (81,) + full, (17,) + full, (17,) + full],
+        image, far, near, weight, plane,
         dtypes=[F32, F32, BF16, BF16],
     )
+    near, far = swap(near, far)
     (energy_half,) = call(
         work_kernel, [(4,) + full], geometry, density, energy, material, energy_mass, speeds, far, near
     )
-    near, far = swap(near_out, far_out)
     (products,) = call(product_kernel, [(3,) + full], zeroth, first)
     second, moments = call(
         moment_kernel, [(81,) + full, (devices, 128)], image, far, near, weight, first, products

time: 37.4 us -> 37.2 us (level)
    pallas_call x10 -> x11, Pallas kernels: 6.23 us -> 6.39 us  [call(): pl.pallas_call(kernel, out_shape=shapes, in_specs=[place] * len(args), ou...]
  transfers between devices with their start and end apart: 9 -> 9, of which waited for: 6 -> 6; matrix products, arithmetic and copies ran while one was open for 0% -> 0% of each run, Pallas kernels for 5% -> 6%
where the time goes in v6:
time: 37.2 us; the launch traced here: 37 us
  waiting for transfers between devices  17.2 us (46%)
  starting transfers between devices  12 us (32%)
  Pallas kernels  6.39 us (17%)
  between operations  0.76 us (2%)
  local copies, waits for them, and re-layouts  0.68 us (2%)
    ppermute x4, waiting for transfers between devices, swap(): lax.ppermute(far, axis, [(i, (i + (1 if i % 2 else -1)) % count) for i in...  10.5 us
    ppermute x4, starting transfers between devices, swap(): lax.ppermute(far, axis, [(i, (i + (1 if i % 2 else -1)) % count) for i in...  8.62 us
    pallas_call x11, Pallas kernels, call(): pl.pallas_call(kernel, out_shape=shapes, in_specs=[place] * len(args), ou...  6.39 us
    all_to_all x1, waiting for transfers between devices, local(): moments = lax.all_to_all(moments, ('slab', 'brick'), 0, 0, tiled=True)  4.76 us
    all_to_all x1, starting transfers between devices, local(): moments = lax.all_to_all(moments, ('slab', 'brick'), 0, 0, tiled=True)  2.93 us
    ppermute x4, waiting for transfers between devices, swap(): lax.ppermute(near, axis, [(i, i + (-1 if i % 2 else 1)) for i in range(co...  1.96 us
  transfers between devices with their start and end apart: 9, of which 6 were waited for; matrix products, arithmetic and copies ran while one was open for 0% of the time, Pallas kernels for 6%

profile of v6, /device:TPU:0, one launch (start us, length us, event | category | flops | bytes accessed | tf_op | source)
XLA Modules:
  0.0 37.0 jit_solution(8026734917091940064)
XLA Ops:
  0.6 1.4 %force_kernel.1 = (f32[81,8,128]{2,1,0:T(8,128)S(1)}, bf16[27,4,128]{2,1,0:T(4,128)(2,1)S(1)}, bf16[27,4,128]{2,1,0:T(4,128)(2,1)S(1)}) custom-call(bf16[324,8,128]{2,1,0:T(8,128)(2,1)} %bitcast.13, f32[4,8,128]{2,1,0:T(8,128)} %bitcast.18, f32[4,8,128]{2,1,0:T(8,128)} %bitcast.20, s32[4,128]{1,0:T(4,128)} %bitcast.24, f32[27,4,128]{2,1,0:T(4,128)} %bitcast.15), custom_call_target="tpu_custom_call" | custom-call | flops 100000 | bytes 1196032 | tf_op jit(solution)/shard_map/force_kernel/pallas_call | solution.py:546
  2.0 3.4 %collective-permute-start = (bf16[27,4,128]{2,1,0:T(4,128)(2,1)S(1)}, bf16[27,4,128]{2,1,0:T(4,128)(2,1)S(1)}, u32[]{:S(2)}, u32[]{:S(2)}) collective-permute-start(bf16[27,4,128]{2,1,0:T(4,128)(2,1)S(1)} %get-tuple-element.26), channel_id=1, source_target_pairs={{0,28},{4,8},{8,4},{12,16},{16,12},{20,24},{24,20},{28,0},{1,29},{... | collective-permute-start | bytes 82952 | tf_op jit(solution)/shard_map/ppermute | solution.py:560
  5.4 0.0 collective-permute-start.1
  5.5 0.3 spread_kernel.1
  5.8 1.2 %collective-permute-done.far = bf16[27,4,128]{2,1,0:T(4,128)(2,1)S(1)} collective-permute-done((bf16[27,4,128]{2,1,0:T(4,128)(2,1)S(1)}, bf16[27,4,128]{2,1,0:T(4,128)(2,1)S(1)}, u32[]{:S(2)}, u32[]{:S(2)}) %collective-permute-start) | collective-permute-done | bytes 27680 | tf_op jit(solution)/shard_map/ppermute | solution.py:560
  7.0 0.0 collective-permute-done.1.near
  7.0 0.3 rim_kernel.1
  7.3 4.5 %collective-permute-start.2 = (bf16[79,2,128]{2,1,0:T(2,128)(2,1)S(1)}, bf16[79,2,128]{2,1,0:T(2,128)(2,1)S(1)}, u32[]{:S(2)}, u32[]{:S(2)}) collective-permute-start(bf16[79,2,128]{2,1,0:T(2,128)(2,1)S(1)} %get-tuple-element.32), channel_id=1, source_target_pairs={{0,3},{1,2},{2,1},{3,0},{4,7},{5,6},{6,5},{7,4},{8,11},{9,10},{10,... | collective-permute-start | bytes 121352 | tf_op jit(solution)/shard_map/ppermute | solution.py:560
  11.9 2.0 %collective-permute-done.2.far_in = bf16[79,2,128]{2,1,0:T(2,128)(2,1)S(1)} collective-permute-done((bf16[79,2,128]{2,1,0:T(2,128)(2,1)S(1)}, bf16[79,2,128]{2,1,0:T(2,128)(2,1)S(1)}, u32[]{:S(2)}, u32[]{:S(2)}) %collective-permute-start.2) | collective-permute-done | bytes 40480 | tf_op jit(solution)/shard_map/ppermute | solution.py:560
  13.9 1.9 %collective-permute-done.3.near_in = bf16[79,2,128]{2,1,0:T(2,128)(2,1)S(1)} collective-permute-done((bf16[79,2,128]{2,1,0:T(2,128)(2,1)S(1)}, bf16[79,2,128]{2,1,0:T(2,128)(2,1)S(1)}, u32[]{:S(2)}, u32[]{:S(2)}) %collective-permute-start.3) | collective-permute-done | bytes 40480 | tf_op jit(solution)/shard_map/ppermute | solution.py:561
  15.9 0.5 %first_kernel.1 = (f32[81,8,128]{2,1,0:T(8,128)S(1)}, f32[27,8,128]{2,1,0:T(8,128)S(1)}, f32[81,8,128]{2,1,0:T(8,128)S(1)}, bf16[13,8,128]{2,1,0:T(8,128)(2,1)S(1)}, bf16[13,8,128]{2,1,0:T(8,128)(2,1)S(1)}) custom-call(f32[55,8,128]{2,1,0:T(8,128)S(1)} %get-tuple-element.31.own, bf16[79,2,128]{2,1,0:T(2,128)(2,1)S(1)} %collective-permute-done.2.far_in, ...), custom_call_target="tpu_custom_call" | custom-call | flops 100000 | bytes 1242112 | tf_op jit(solution)/shard_map/first_kernel/pallas_call | solution.py:546
  16.4 0.3 collective-permute-start.4
  16.7 0.4 %collective-permute-start.5 = (bf16[13,8,128]{2,1,0:T(8,128)(2,1)S(1)}, bf16[13,8,128]{2,1,0:T(8,128)(2,1)S(1)}, u32[]{:S(2)}, u32[]{:S(2)}) collective-permute-start(bf16[13,8,128]{2,1,0:T(8,128)(2,1)S(1)} %get-tuple-element.36), channel_id=1, source_target_pairs={{0,4},{4,0},{8,12},{12,8},{16,20},{20,16},{24,28},{28,24},{1,5},{5... | collective-permute-start | bytes 79880 | tf_op jit(solution)/shard_map/ppermute | solution.py:561
  17.1 0.1 speed_kernel.1
  17.3 3.3 %collective-permute-done.4.far_in = bf16[13,8,128]{2,1,0:T(8,128)(2,1)S(1)} collective-permute-done((bf16[13,8,128]{2,1,0:T(8,128)(2,1)S(1)}, bf16[13,8,128]{2,1,0:T(8,128)(2,1)S(1)}, u32[]{:S(2)}, u32[]{:S(2)}) %collective-permute-start.4) | collective-permute-done | bytes 26656 | tf_op jit(solution)/shard_map/ppermute | solution.py:560
  20.6 0.0 collective-permute-done.5.near_in
  20.6 0.4 %second_kernel.1 = (f32[81,8,128]{2,1,0:T(8,128)S(1)}, f32[81,8,128]{2,1,0:T(8,128)S(1)}, bf16[17,8,128]{2,1,0:T(8,128)(2,1)S(1)}, bf16[17,8,128]{2,1,0:T(8,128)(2,1)S(1)}) custom-call(f32[81,8,128]{2,1,0:T(8,128)S(1)} %get-tuple-element.34.image, bf16[13,8,128]{2,1,0:T(8,128)(2,1)S(1)} %collective-permute-done.4.far_in, ...), custom_call_target="tpu_custom_call" | custom-call | flops 100000 | bytes 1339392 | tf_op jit(solution)/shard_map/second_kernel/pallas_call | solution.py:546
  21.0 0.3 collective-permute-start.6
  21.4 0.0 collective-permute-start.7
  21.4 0.1 product_kernel.1.products
  21.4 3.9 %collective-permute-done.6.far = bf16[17,8,128]{2,1,0:T(8,128)(2,1)S(1)} collective-permute-done((bf16[17,8,128]{2,1,0:T(8,128)(2,1)S(1)}, bf16[17,8,128]{2,1,0:T(8,128)(2,1)S(1)}, u32[]{:S(2)}, u32[]{:S(2)}) %collective-permute-start.6) | collective-permute-done | bytes 34848 | tf_op jit(solution)/shard_map/ppermute | solution.py:560
  25.3 0.9 %moment_kernel.1 = (f32[81,8,128]{2,1,0:T(8,128)S(1)}, f32[32,128]{1,0:T(8,128)}) custom-call(f32[81,8,128]{2,1,0:T(8,128)S(1)} %get-tuple-element.40.image, bf16[17,8,128]{2,1,0:T(8,128)(2,1)S(1)} %collective-permute-done.6.far, bf16[17,8,128]{2,1,0:T(8,128)(2,1)S(1)} %collective-permute-done.7.near, f32[27,8,128]{2,1,0:T(8,128)S(1)} %get-tuple-element.37.weight, ...), custom_call_target="tpu_custom_call" | custom-call | flops 100000 | bytes 1204224 | tf_op jit(solution)/shard_map/moment_kernel/pallas_call | solution.py:546
  26.2 2.9 %all-to-all-start = ((f32[32,1,128]{2,1,0:T(1,128)}), f32[32,1,128]{2,1,0:T(1,128)S(1)}, u32[]{:S(2)}, u32[]{:S(2)}) async-start(f32[32,1,128]{2,1,0:T(1,128)} %bitcast.6), calls=%async_computation | async-start | bytes 32768 | tf_op jit(solution)/shard_map/all_to_all | solution.py:629
  29.2 0.0 copy-start.3
  29.2 0.0 copy-start.4
  29.2 0.0 copy-start.5
  29.2 0.8 %nodal_kernel.1.nodal = f32[3,48,384]{2,1,0:T(8,128)S(1)} custom-call(f32[81,8,128]{2,1,0:T(8,128)S(1)} %get-tuple-element.44.zeroth, f32[81,8,128]{2,1,0:T(8,128)S(1)} %get-tuple-element.43.first, f32[81,8,128]{2,1,0:T(8,128)S(1)} %get-tuple-element.46.second), custom_call_target="tpu_custom_call" | custom-call | flops 100000 | bytes 1216512 | tf_op jit(solution)/shard_map/nodal_kernel/pallas_call | solution.py:546
  30.0 0.0 copy-start.6
  30.1 0.6 %copy-done.6 = s32[1,4,128]{2,1,0:T(4,128)S(1)} copy-done((s32[1,4,128]{2,1,0:T(4,128)S(1)}, s32[1,4,128]{2,1,0:T(4,128)}, u32[]{:S(2)}) %copy-start.6) | copy-done | bytes 2072
  30.7 0.8 %work_kernel.1 = f32[4,8,128]{2,1,0:T(8,128)} custom-call(bf16[324,8,128]{2,1,0:T(8,128)(2,1)S(1)} %bitcast.14, f32[4,8,128]{2,1,0:T(8,128)S(1)} %bitcast.19, f32[4,8,128]{2,1,0:T(8,128)S(1)} %bitcast.21, s32[4,128]{1,0:T(4,128)S(1)} %bitcast.25, f32[4,8,128]{2,1,0:T(8,128)S(1)} %bitcast.23, f32[54,8,128]{2,1,0:T(8,128)S(1)} %get-tuple-element.47.speeds, ...), custom_call_target="tpu_custom_call" | custom-call | flops 100000 | bytes 1021952 | tf_op jit(solution)/shard_map/work_kernel/pallas_call | solution.py:546
  31.5 4.8 %all-to-all-done = f32[32,1,128]{2,1,0:T(1,128)S(1)} async-done(((f32[32,1,128]{2,1,0:T(1,128)}), f32[32,1,128]{2,1,0:T(1,128)S(1)}, u32[]{:S(2)}, u32[]{:S(2)}) %all-to-all-start) | async-done | bytes 16416 | tf_op jit(solution)/shard_map/all_to_all | solution.py:629
  36.3 0.8 %last_kernel.1 = f32[3,2,8,257]{3,2,1,0:T(8,128)} custom-call(f32[32,128]{1,0:T(8,128)S(1)} %bitcast.22, f32[3,48,384]{2,1,0:T(8,128)S(1)} %nodal_kernel.1.nodal, f32[3,2,8,257]{3,2,1,0:T(8,128)S(1)} %copy-done.2), custom_call_target="tpu_custom_call" | custom-call | flops 100000 | bytes 336256 | tf_op jit(solution)/shard_map/last_kernel/pallas_call | solution.py:546
  (11 shorter events, 0.0 us)
Async XLA Ops:
  0.6 4.8 %copy-start.1 = (f32[27,1,4,128]{3,2,1,0:T(4,128)S(1)}, f32[27,1,4,128]{3,2,1,0:T(4,128)}, u32[]{:S(2)}) copy-start(f32[27,1,4,128]{3,2,1,0:T(4,128)} %param.12) | copy-start | bytes 165892
  0.6 4.8 %copy-start.2 = (f32[3,2,8,257]{3,2,1,0:T(8,128)S(1)}, f32[3,2,8,257]{3,2,1,0:T(8,128)}, u32[]{:S(2)}) copy-start(f32[3,2,8,257]{3,2,1,0:T(8,128)} %velocity.3) | copy-start | bytes 148036
  2.0 4.9 %collective-permute-start = (bf16[27,4,128]{2,1,0:T(4,128)(2,1)S(1)}, bf16[27,4,128]{2,1,0:T(4,128)(2,1)S(1)}, u32[]{:S(2)}, u32[]{:S(2)}) collective-permute-start(bf16[27,4,128]{2,1,0:T(4,128)(2,1)S(1)} %get-tuple-element.26), channel_id=1, source_target_pairs={{0,28},{4,8},{8,4},{12,16},{16,12},{20,24},{24,20},{28,0},{1,29},{... | collective-permute-start | bytes 82952 | tf_op jit(solution)/shard_map/ppermute | solution.py:560
  5.4 1.6 %collective-permute-start.1 = (bf16[27,4,128]{2,1,0:T(4,128)(2,1)S(1)}, bf16[27,4,128]{2,1,0:T(4,128)(2,1)S(1)}, u32[]{:S(2)}, u32[]{:S(2)}) collective-permute-start(bf16[27,4,128]{2,1,0:T(4,128)(2,1)S(1)} %get-tuple-element.27), channel_id=1, source_target_pairs={{0,4},{4,0},{8,12},{12,8},{16,20},{20,16},{24,28},{28,24},{1,5},{5... | collective-permute-start | bytes 82952 | tf_op jit(solution)/shard_map/ppermute | solution.py:561
  7.3 6.6 %collective-permute-start.2 = (bf16[79,2,128]{2,1,0:T(2,128)(2,1)S(1)}, bf16[79,2,128]{2,1,0:T(2,128)(2,1)S(1)}, u32[]{:S(2)}, u32[]{:S(2)}) collective-permute-start(bf16[79,2,128]{2,1,0:T(2,128)(2,1)S(1)} %get-tuple-element.32), channel_id=1, source_target_pairs={{0,3},{1,2},{2,1},{3,0},{4,7},{5,6},{6,5},{7,4},{8,11},{9,10},{10,... | collective-permute-start | bytes 121352 | tf_op jit(solution)/shard_map/ppermute | solution.py:560
  11.9 4.0 %collective-permute-start.3 = (bf16[79,2,128]{2,1,0:T(2,128)(2,1)S(1)}, bf16[79,2,128]{2,1,0:T(2,128)(2,1)S(1)}, u32[]{:S(2)}, u32[]{:S(2)}) collective-permute-start(bf16[79,2,128]{2,1,0:T(2,128)(2,1)S(1)} %get-tuple-element.33), channel_id=1, source_target_pairs={{0,1},{1,0},{2,3},{3,2},{4,5},{5,4},{6,7},{7,6},{8,9},{9,8},{10,11... | collective-permute-start | bytes 121352 | tf_op jit(solution)/shard_map/ppermute | solution.py:561
  16.4 4.2 %collective-permute-start.4 = (bf16[13,8,128]{2,1,0:T(8,128)(2,1)S(1)}, bf16[13,8,128]{2,1,0:T(8,128)(2,1)S(1)}, u32[]{:S(2)}, u32[]{:S(2)}) collective-permute-start(bf16[13,8,128]{2,1,0:T(8,128)(2,1)S(1)} %get-tuple-element.35), channel_id=1, source_target_pairs={{0,28},{4,8},{8,4},{12,16},{16,12},{20,24},{24,20},{28,0},{1,29},{... | collective-permute-start | bytes 79880 | tf_op jit(solution)/shard_map/ppermute | solution.py:560
  16.7 3.9 %collective-permute-start.5 = (bf16[13,8,128]{2,1,0:T(8,128)(2,1)S(1)}, bf16[13,8,128]{2,1,0:T(8,128)(2,1)S(1)}, u32[]{:S(2)}, u32[]{:S(2)}) collective-permute-start(bf16[13,8,128]{2,1,0:T(8,128)(2,1)S(1)} %get-tuple-element.36), channel_id=1, source_target_pairs={{0,4},{4,0},{8,12},{12,8},{16,20},{20,16},{24,28},{28,24},{1,5},{5... | collective-permute-start | bytes 79880 | tf_op jit(solution)/shard_map/ppermute | solution.py:561
  21.0 4.3 %collective-permute-start.6 = (bf16[17,8,128]{2,1,0:T(8,128)(2,1)S(1)}, bf16[17,8,128]{2,1,0:T(8,128)(2,1)S(1)}, u32[]{:S(2)}, u32[]{:S(2)}) collective-permute-start(bf16[17,8,128]{2,1,0:T(8,128)(2,1)S(1)} %get-tuple-element.41), channel_id=1, source_target_pairs={{0,28},{4,8},{8,4},{12,16},{16,12},{20,24},{24,20},{28,0},{1,29},{... | collective-permute-start | bytes 104456 | tf_op jit(solution)/shard_map/ppermute | solution.py:560
  21.4 4.0 %collective-permute-start.7 = (bf16[17,8,128]{2,1,0:T(8,128)(2,1)S(1)}, bf16[17,8,128]{2,1,0:T(8,128)(2,1)S(1)}, u32[]{:S(2)}, u32[]{:S(2)}) collective-permute-start(bf16[17,8,128]{2,1,0:T(8,128)(2,1)S(1)} %get-tuple-element.42), channel_id=1, source_target_pairs={{0,4},{4,0},{8,12},{12,8},{16,20},{20,16},{24,28},{28,24},{1,5},{5... | collective-permute-start | bytes 104456 | tf_op jit(solution)/shard_map/ppermute | solution.py:561
  26.2 3.8 %copy-start = (bf16[81,8,1,4,128]{4,3,2,1,0:T(4,128)(2,1)S(1)}, bf16[81,8,1,4,128]{4,3,2,1,0:T(4,128)(2,1)}, u32[]{:S(2)}) copy-start(bf16[81,8,1,4,128]{4,3,2,1,0:T(4,128)(2,1)} %param.11) | copy-start | bytes 1990660
  26.2 10.0 %all-to-all-start = ((f32[32,1,128]{2,1,0:T(1,128)}), f32[32,1,128]{2,1,0:T(1,128)S(1)}, u32[]{:S(2)}, u32[]{:S(2)}) async-start(f32[32,1,128]{2,1,0:T(1,128)} %bitcast.6), calls=%async_computation | async-start | bytes 32768 | tf_op jit(solution)/shard_map/all_to_all | solution.py:629
  29.2 0.9 %copy-start.3 = (f32[8,1,4,128]{3,2,1,0:T(4,128)S(1)}, f32[8,1,4,128]{3,2,1,0:T(4,128)}, u32[]{:S(2)}) copy-start(f32[8,1,4,128]{3,2,1,0:T(4,128)} %param.9) | copy-start | bytes 49156
  29.2 0.9 %copy-start.4 = (f32[8,1,4,128]{3,2,1,0:T(4,128)S(1)}, f32[8,1,4,128]{3,2,1,0:T(4,128)}, u32[]{:S(2)}) copy-start(f32[8,1,4,128]{3,2,1,0:T(4,128)} %param.8) | copy-start | bytes 49156
  29.2 0.9 %copy-start.5 = (f32[8,1,4,128]{3,2,1,0:T(4,128)S(1)}, f32[8,1,4,128]{3,2,1,0:T(4,128)}, u32[]{:S(2)}) copy-start(f32[8,1,4,128]{3,2,1,0:T(4,128)} %param.13) | copy-start | bytes 49156
  30.0 0.7 %copy-start.6 = (s32[1,4,128]{2,1,0:T(4,128)S(1)}, s32[1,4,128]{2,1,0:T(4,128)}, u32[]{:S(2)}) copy-start(s32[1,4,128]{2,1,0:T(4,128)} %param.10) | copy-start | bytes 6148

commit v7 on v6

--- a/solution.py
+++ b/solution.py
@@ -14,8 +14,10 @@
 OFFSET = float(np.sqrt(0.6) / 2.0)
 SIDE = 0.3
 MIDDLE = 0.4
+ODD, EVEN = OFFSET / SIDE, MIDDLE / SIDE
 LINE_WEIGHTS = (5.0 / 18.0, 8.0 / 18.0, 5.0 / 18.0)
 POINT_WEIGHT = [a * b * c for a in LINE_WEIGHTS for b in LINE_WEIGHTS for c in LINE_WEIGHTS]
+POINT_SCALE = [a * b * c for a in (SIDE, 1.0, SIDE) for b in (SIDE, 1.0, SIDE) for c in (SIDE, 1.0, SIDE)]
 OWN = 4
 HALO = 2
 
@@ -29,8 +31,8 @@
     values = list(values)
     for direction in range(3):
         for i, j, k in lines(direction):
-            even = SIDE * (values[i] + values[k]) + MIDDLE * values[j]
-            odd = OFFSET * (values[i] - values[k])
+            even = (values[i] + values[k]) + EVEN * values[j]
+            odd = ODD * (values[i] - values[k])
             values[i], values[k] = even + odd, even - odd
     return values
 
@@ -40,10 +42,9 @@
     for direction in range(3):
         for i, j, k in lines(direction):
             total = values[i] + values[k]
-            odd = OFFSET * (values[i] - values[k])
-            even = SIDE * total
-            values[i], values[k] = even + odd, even - odd
-            values[j] = values[j] + MIDDLE * total
+            odd = ODD * (values[i] - values[k])
+            values[i], values[k] = total + odd, total - odd
+            values[j] = values[j] + EVEN * total
     return values
 
 
@@ -66,11 +67,29 @@
     return values
 
 
-def assemble_y(values):
-    values = list(values)
-    for i, _, k in lines(1):
-        values[i] = values[i] + pltpu.roll(values[k], 1, 0)
-        values[k] = pltpu.roll(values[i], 7, 0)
+def fold(values, wall):
+    lane = lane_of(values[0].shape)
+    folded = []
+    for a in (0, 9, 18):
+        columns = [[values[a + c] + pltpu.roll(values[a + 6 + c], 1, 0), values[a + 3 + c]] for c in range(3)]
+        for b in range(2):
+            first = columns[0][b] + jnp.where(lane == 0, 0.0, pltpu.roll(columns[2][b], 1, 1))
+            if wall:
+                first = jnp.where(lane == 0, 0.0, first)
+            folded += [first, columns[1][b], jnp.zeros_like(first) if wall else columns[2][b]]
+    return folded
+
+
+def unfold(folded):
+    lane = lane_of(folded[0].shape)
+    values = []
+    for a in (0, 6, 12):
+        planes = []
+        for b in (0, 3):
+            first, second, top = folded[a + b : a + b + 3]
+            planes.append([first, second, jnp.where(lane == 127, top, pltpu.roll(first, 127, 1))])
+        planes.append([pltpu.roll(value, 7, 0) for value in planes[0]])
+        values += planes[0] + planes[1] + planes[2]
     return values
 
 
@@ -106,43 +125,51 @@
     return jnp.concatenate([values, values], axis=0)
 
 
+def force_of(geometry, r, pressure):
+    value = jnp.sum(geometry[pl.ds(4 * r, 4)].astype(F32) * pressure, axis=0)
+    return -(value + pltpu.roll(value, OWN, 0))
+
+
 def force_kernel(
     geometry_in, density_in, energy_in, material_in, mass_weight_in,
-    field, near, far,
+    field, near, far, pressure_out, gravity_out,
     geometry, density, energy, material, mass_weight, sems,
 ):
     small = [
-        pltpu.make_async_copy(source, target, sems.at[3 + i])
+        pltpu.make_async_copy(source, target, sems.at[6 + i])
         for i, (source, target) in enumerate(
             [(density_in, density), (energy_in, energy), (material_in, material), (mass_weight_in, mass_weight)]
         )
     ]
     parts = [
         pltpu.make_async_copy(
-            geometry_in.at[pl.ds(108 * comp, 108)], geometry.at[pl.ds(108 * comp, 108)], sems.at[comp]
+            geometry_in.at[pl.ds(108 * comp + 36 * a, 36)], geometry.at[pl.ds(72 * comp + 18 * a, 36)], sems.at[2 * comp + a // 2]
         )
         for comp in range(3)
+        for a in (0, 2)
     ]
     for copy in small + parts:
         copy.start()
     for copy in small:
         copy.wait()
     pressure = pressure_of(density, energy, material)
-    gravity = from_points([double(mass_weight[q]) * POINT_WEIGHT[q] for q in range(27)])
+    gravity = from_points([double(mass_weight[q]) * (POINT_WEIGHT[q] * POINT_SCALE[q]) for q in range(27)])
+    pressure_out[...] = pressure
+    for n in range(9):
+        gravity_out[n] = GRAVITY * gravity[9 + n]
     even = is_even()
     for comp in range(3):
-        parts[comp].wait()
+        parts[2 * comp].wait()
+        parts[2 * comp + 1].wait()
         values = []
-        for n in range(27):
-            r = 27 * comp + n
-            value = jnp.sum(geometry[pl.ds(4 * r, 4)].astype(F32) * pressure, axis=0)
-            value = -(value + pltpu.roll(value, OWN, 0))
+        for n in range(18):
+            value = force_of(geometry, 18 * comp + n, pressure)
             if comp == 2:
-                value = value - GRAVITY * gravity[n]
-            field[r] = value
+                value = value - GRAVITY * gravity[n if n < 9 else n + 9]
+            field[18 * comp + n] = value
             values.append(value)
         for n in range(9):
-            put(near, far, 9 * comp + n, values[n][:OWN], values[18 + n][:OWN], even)
+            put(near, far, 9 * comp + n, values[n][:OWN], values[9 + n][:OWN], even)
 
 
 def spread_velocity(velocity, out):
@@ -169,15 +196,25 @@
 SPEED_LANE = 32
 
 
-def fill_plane(values, comp, a, tops, out, near, far, even_y):
+def add_tops(values, comp, a, tops, sent):
+    if comp == 2:
+        return tops, sent
     row = lax.broadcasted_iota(jnp.int32, (8, 128), 0)
     lane = lane_of((8, 128))
     i = 3 * comp + a
+    first, second, third = [values[3 * b + 2] for b in range(3)]
+    for b, value in enumerate((first, second, third)):
+        tops = to_lane(tops, lane, value, 3 * i + b)
+    first = first + jnp.where(row % 2 == 1, pltpu.roll(third, 1, 0), 0.0)
+    return tops, to_lane(sent, lane, first, 3 * i)
+
+
+def fill_plane(values, comp, a, out, near, far, even_y):
+    row = lax.broadcasted_iota(jnp.int32, (8, 128), 0)
+    i = 3 * comp + a
     outer = []
-    for b in range(3):
-        tops = to_lane(tops, lane, values[9 * a + 3 * b + 2], 3 * i + b)
     for c in range(2):
-        first, second, third = [values[9 * a + 3 * b + c] for b in range(3)]
+        first, second, third = [values[3 * b + c] for b in range(3)]
         for b, value in enumerate((first, second, third)):
             out[6 * i + 2 * b + c] = pltpu.roll(value, HALO, 0)
         first = first + jnp.where(row % 2 == 1, pltpu.roll(third, 1, 0), 0.0)
@@ -186,36 +223,51 @@
         outer.append(third)
     both = jnp.where(row % 2 == 1, outer[1], pltpu.roll(outer[0], 7, 0))
     put(near, far, 36 + i, both[:HALO], both[HALO:OWN], even_y)
-    return tops
-
-
-def spread_kernel(velocity, field, mass_weight, spread, middle, near, far):
+
+
+def spread_kernel(
+    geometry_in, velocity, pressure_in, gravity, mass_weight, spread, middle, near, far, geometry, sems
+):
+    parts = [
+        pltpu.make_async_copy(
+            geometry_in.at[pl.ds(108 * comp + 36, 36)], geometry.at[pl.ds(36 * comp, 36)], sems.at[comp]
+        )
+        for comp in range(3)
+    ]
+    for copy in parts:
+        copy.start()
     even_y = is_even("brick")
     row = lax.broadcasted_iota(jnp.int32, (8, 128), 0)
     lane = lane_of((8, 128))
     spread_velocity(velocity, spread)
     tops = jnp.zeros((8, 128), F32)
-    for comp in range(3):
-        values = [field[27 * comp + 9 + n] for n in range(9)]
-        values = [None] * 9 + assemble_z(values, comp == 2)
-        tops = fill_plane(values, comp, 1, tops, middle, near, far, even_y)
+    sent = tops
     for k in range(6):
         tops = to_lane(tops, lane, jnp.where(row == 0, spread[6 * k + 2], 0.0), SPEED_LANE + k)
-    middle[54] = tops
     for q in range(27):
         put(near, far, WEIGHTS + q, mass_weight[q, :HALO], mass_weight[q, HALO:], even_y)
     for k in range(6):
         both = jnp.where(row == 0, spread[6 * k], pltpu.roll(spread[6 * k + 1], 1, 0))[:HALO].astype(BF16)
         near[SPEEDS + k] = both
         far[SPEEDS + k] = both
+    pressure = pressure_in[...]
+    for comp in range(3):
+        parts[comp].wait()
+        values = []
+        for n in range(9):
+            value = force_of(geometry, 9 * comp + n, pressure)
+            values.append(value - gravity[n] if comp == 2 else value)
+        tops, sent = add_tops(values, comp, 1, tops, sent)
+        fill_plane(assemble_z(values, comp == 2), comp, 1, middle, near, far, even_y)
+    middle[54] = tops
+    middle[55] = sent
 
 
 def rim_kernel(field, far, near, middle, near_in, far_in, out, near_out, far_out):
     even = is_even()
     even_y = is_even("brick")
-    row = lax.broadcasted_iota(jnp.int32, (8, 128), 0)
     lane = lane_of((8, 128))
-    tops = middle[54]
+    tops, sent = middle[54], middle[55]
     for comp in range(3):
         i = 3 * comp + 1
         for k in range(6):
@@ -223,18 +275,16 @@
         for k in [4 * i, 4 * i + 1, 4 * i + 2, 4 * i + 3, 36 + i]:
             near_out[k] = near_in[k]
             far_out[k] = far_in[k]
-        values = [field[27 * comp + n] for n in range(27)]
+        values = [field[18 * comp + n] for n in range(18)]
         for n in range(9):
             left, right = get(near, far, 9 * comp + n, even)
             values[n] = values[n] + double(left)
-            values[18 + n] = values[18 + n] + double(right)
-        values = assemble_z(values[:9] + values[18:], comp == 2)
-        values = values[:9] + [None] * 9 + values[9:]
-        for a in (0, 2):
-            tops = fill_plane(values, comp, a, tops, out, near_out, far_out, even_y)
+            values[9 + n] = values[9 + n] + double(right)
+        for a, plane in ((0, values[:9]), (2, values[9:])):
+            tops, sent = add_tops(plane, comp, a, tops, sent)
+            fill_plane(assemble_z(plane, comp == 2), comp, a, out, near_out, far_out, even_y)
     out[54] = pltpu.roll(tops, HALO, 0)
-    inner = jnp.where(lane % 3 == 0, pltpu.roll(pltpu.roll(tops, 126, 1), 1, 0), 0.0)
-    tops = tops + jnp.where((row % 2 == 1) & (lane < 27), inner, 0.0)
+    tops = jnp.where((lane % 3 == 0) & (lane < 27), sent, tops)
     put(near_out, far_out, TOPS, tops[:HALO], tops[HALO:OWN], even_y)
     for k in range(WEIGHTS, MESSAGE):
         near_out[k] = near_in[k]
@@ -246,7 +296,7 @@
     sides = [jnp.zeros((8, 128), F32)] * 2
     for comp in range(3):
         for b in range(2):
-            left, right = [[planes[comp][9 * a + 3 * b + c] for c in range(3)] for a in (0, 2)]
+            left, right = [planes[comp][a + 3 * b : a + 3 * b + 3] for a in (0, 12)]
             for c in range(2):
                 put(near, far, 4 * comp + 2 * b + c, left[c], right[c], even)
             sides = [to_lane(side, lane, plane[2], 2 * comp + b) for side, plane in zip(sides, (left, right))]
@@ -256,7 +306,7 @@
 def apply_mass(values, weight, wall):
     points = to_points(values)
     points = [points[q] * weight[q] for q in range(27)]
-    return assemble_y(assemble_z(from_points(points), wall))
+    return fold(from_points(points), wall)
 
 
 def first_kernel(
@@ -274,31 +324,30 @@
         if k >= WEIGHTS:
             rows[k, HALO : HALO + OWN] = mass_weight[k - WEIGHTS]
     for q in range(27):
-        weight[q] = rows[WEIGHTS + q] * POINT_WEIGHT[q]
+        weight[q] = rows[WEIGHTS + q] * (POINT_WEIGHT[q] * POINT_SCALE[q] ** 2)
     edge = (row == 1) | (row == 7)
     tops = jnp.where((lane % 3 == 2) & ~edge, 0.0, rows[TOPS])
     tops = jnp.where(mine, own[54], tops)
+    tops = tops + jnp.where(lane % 3 == 0, pltpu.roll(pltpu.roll(tops, 126, 1), 1, 0), 0.0)
     planes = []
     for comp in range(3):
         values = []
         for a in range(3):
             i = 3 * comp + a
-            for b in range(3):
-                for c in range(2):
-                    if b < 2:
-                        halo = rows[4 * i + 2 * b + c]
-                    else:
-                        k = 2 * i + c
-                        halo = rows[36 + k // 2]
-                        halo = jnp.where(edge, halo if k % 2 == 1 else pltpu.roll(halo, 1, 0), 0.0)
-                    values.append(jnp.where(mine, own[6 * i + 2 * b + c], halo))
-                values.append(third_along_z(values[-2], tops, lane, 3 * i + b))
-        values = assemble_y(values)
-        for n in range(27):
-            field[27 * comp + n] = values[n]
-        values = apply_mass(values, weight, comp == 2)
-        for n in range(27):
-            image[27 * comp + n] = values[n]
+            columns = []
+            for c in range(2):
+                k = 2 * i + c
+                halos = [rows[4 * i + c], rows[4 * i + 2 + c], rows[36 + k // 2]]
+                halos[2] = jnp.where(edge, halos[2] if k % 2 == 1 else pltpu.roll(halos[2], 1, 0), 0.0)
+                column = [jnp.where(mine, own[6 * i + 2 * b + c], halos[b]) for b in range(3)]
+                columns.append([column[0] + pltpu.roll(column[2], 1, 0), column[1]])
+            for b in range(2):
+                values += [columns[0][b], columns[1][b], pltpu.roll(tops, 127 - 3 * i - b, 1)]
+        for n in range(18):
+            field[18 * comp + n] = values[n]
+        values = apply_mass(unfold(values), weight, comp == 2)
+        for n in range(18):
+            image[18 * comp + n] = values[n]
         planes.append(values)
     send_planes(planes, near, far, even)
 
@@ -340,8 +389,8 @@
     for comp in range(3):
         for b in range(2):
             both = []
-            for side, a in enumerate((0, 2)):
-                plane = [planes[comp][9 * a + 3 * b + c] for c in range(3)]
+            for side, a in enumerate((0, 12)):
+                plane = planes[comp][a + 3 * b : a + 3 * b + 3]
                 both.append(jnp.where(row < OWN, pltpu.roll(plane[0], 6, 0), pltpu.roll(plane[1], 2, 0)))
                 sides[side] = to_lane(sides[side], lane, plane[2], 2 * comp + b)
                 if b == 0:
@@ -383,18 +432,13 @@
 
 
 def add_planes(image, read, tops, comp):
-    values = [image[27 * comp + n] for n in range(27)]
-    lane = lane_of((8, 128))
+    values = [image[18 * comp + n] for n in range(18)]
     for b in range(2):
-        for a, plane, top in zip((0, 18), read(b), tops):
+        for a, plane, top in zip((0, 12), read(b), tops):
             n = a + 3 * b
             for c in range(2):
                 values[n + c] = values[n + c] + plane[c]
-            top = values[n + 2] + pltpu.roll(top, 127 - 2 * comp - b, 1)
-            values[n + 2] = jnp.where(lane == 127, top, pltpu.roll(values[n], 127, 1))
-    for a in (0, 18):
-        for c in range(3):
-            values[a + 6 + c] = pltpu.roll(values[a + c], 7, 0)
+            values[n + 2] = values[n + 2] + pltpu.roll(top, 127 - 2 * comp - b, 1)
     return values
 
 
@@ -403,11 +447,11 @@
     planes = []
     for comp in range(3):
         values = take_planes(image, near_in, far_in, comp, even)
-        for n in range(27):
-            field[27 * comp + n] = values[n]
-        values = apply_mass(values, weight, comp == 2)
-        for n in range(27):
-            image_out[27 * comp + n] = values[n]
+        for n in range(18):
+            field[18 * comp + n] = values[n]
+        values = apply_mass(unfold(values), weight, comp == 2)
+        for n in range(18):
+            image_out[18 * comp + n] = values[n]
         planes.append(values)
     send_own(planes, speeds, near, far, even)
 
@@ -435,7 +479,7 @@
     last = lane_of((8, 128)) == 127
     for a in range(2):
         for b in range(2):
-            n = 27 * comp + 9 * a + 3 * b
+            n = 18 * comp + 6 * a + 3 * b
             total = total + first[n] * second[n] + first[n + 1] * second[n + 1]
             total = total + jnp.where(last, first[n + 2] * second[n + 2], 0.0)
     return total
@@ -456,12 +500,12 @@
     even = is_even()
     for comp in range(3):
         values = take_own(image, near, far, comp, even)
-        for n in range(27):
-            second[27 * comp + n] = values[n]
-        values_at = {27 * comp + n: values[n] for n in range(27)}
+        for n in range(18):
+            second[18 * comp + n] = values[n]
+        values_at = {18 * comp + n: values[n] for n in range(18)}
         cross = dot_owned(first, values_at, comp, cross)
         norm = dot_owned(values_at, values_at, comp, norm)
-        points = to_points(values)
+        points = to_points(unfold(values))
         for q in range(27):
             quadratic[q % 3] = quadratic[q % 3] + points[q] * points[q] * weight[q]
     quadratic = quadratic[0] + quadratic[1] + quadratic[2]
@@ -517,7 +561,7 @@
             for comp in range(3):
                 for a in range(2):
                     for b in range(2):
-                        column.append(field[27 * comp + 9 * a + 3 * b + c])
+                        column.append(field[18 * comp + 6 * a + 3 * b + c])
             blocks.append(jnp.concatenate(column, axis=0))
         high, low = halves(jnp.concatenate(blocks, axis=1))
         moved = jnp.dot(move, high, preferred_element_type=F32) + jnp.dot(move, low, preferred_element_type=F32)
@@ -540,13 +584,16 @@
 VMEM = pl.BlockSpec(memory_space=pltpu.VMEM)
 
 
-def call(kernel, outs, *args, scratch=(), flops=100000, place=VMEM, dtypes=None):
+HBM = pl.BlockSpec(memory_space=pltpu.HBM)
+
+
+def call(kernel, outs, *args, scratch=(), flops=100000, in_hbm=0, dtypes=None):
     shapes = [jax.ShapeDtypeStruct(shape, dtype) for shape, dtype in zip(outs, dtypes or [F32] * len(outs))]
     moved = sum(a.size * a.dtype.itemsize for a in args) + sum(4 * int(np.prod(s)) for s in outs)
     return pl.pallas_call(
         kernel,
         out_shape=shapes,
-        in_specs=[place] * len(args),
+        in_specs=[HBM] * in_hbm + [VMEM] * (len(args) - in_hbm),
         out_specs=[VMEM] * len(outs),
         scratch_shapes=list(scratch),
         compiler_params=pltpu.CompilerParams(vmem_limit_bytes=32 * 1024 * 1024),
@@ -574,25 +621,30 @@
     pair = (2, 128)
     devices = lax.axis_size("slab") * lax.axis_size("brick")
 
-    force, near, far = call(
+    stays = [
+        pltpu.with_memory_space_constraint(x, pltpu.HBM) for x in (geometry, density, energy, material, mass_weight)
+    ]
+    force, near, far, pressure, gravity = call(
         force_kernel,
-        [(81,) + full, (27,) + tile, (27,) + tile],
-        *[pltpu.with_memory_space_constraint(x, pltpu.HBM) for x in (geometry, density, energy, material, mass_weight)],
+        [(54,) + full, (27,) + tile, (27,) + tile, (4,) + full, (9,) + full],
+        *stays,
         scratch=[
-            pltpu.VMEM((324,) + full, BF16),
+            pltpu.VMEM((216,) + full, BF16),
             pltpu.VMEM((4,) + full, F32),
             pltpu.VMEM((4,) + full, F32),
             pltpu.VMEM(tile, jnp.int32),
             pltpu.VMEM((27,) + tile, F32),
-            pltpu.SemaphoreType.DMA((7,)),
+            pltpu.SemaphoreType.DMA((10,)),
         ],
-        place=pl.BlockSpec(memory_space=pltpu.HBM),
-        dtypes=[F32, BF16, BF16],
+        in_hbm=5,
+        dtypes=[F32, BF16, BF16, F32, F32],
     )
     spread, middle, near_part, far_part = call(
         spread_kernel,
-        [(36,) + full, (55,) + full, (MESSAGE,) + pair, (MESSAGE,) + pair],
-        velocity, force, mass_weight,
+        [(36,) + full, (56,) + full, (MESSAGE,) + pair, (MESSAGE,) + pair],
+        stays[0], velocity, pressure, gravity, mass_weight,
+        scratch=[pltpu.VMEM((108,) + full, BF16), pltpu.SemaphoreType.DMA((3,))],
+        in_hbm=1,
         dtypes=[F32, F32, BF16, BF16],
     )
     near, far = swap(near, far)
@@ -605,7 +657,7 @@
     near_rim, far_rim = swap(near, far, "brick")
     zeroth, weight, image, near, far = call(
         first_kernel,
-        [(81,) + full, (27,) + full, (81,) + full, (13,) + full, (13,) + full],
+        [(54,) + full, (27,) + full, (54,) + full, (13,) + full, (13,) + full],
         own, far_rim, near_rim, mass_weight,
         scratch=[pltpu.VMEM((SPEEDS,) + full, F32)],
         dtypes=[F32, F32, F32, BF16, BF16],
@@ -614,7 +666,7 @@
     speeds, plane = call(speed_kernel, [(54,) + full, (10,) + full], far_rim, near_rim, spread)
     first, image, near, far = call(
         second_kernel,
-        [(81,) + full, (81,) + full, (17,) + full, (17,) + full],
+        [(54,) + full, (54,) + full, (17,) + full, (17,) + full],
         image, far, near, weight, plane,
         dtypes=[F32, F32, BF16, BF16],
     )
@@ -624,7 +676,7 @@
     )
     (products,) = call(product_kernel, [(3,) + full], zeroth, first)
     second, moments = call(
-        moment_kernel, [(81,) + full, (devices, 128)], image, far, near, weight, first, products
+        moment_kernel, [(54,) + full, (devices, 128)], image, far, near, weight, first, products
     )
     moments = lax.all_to_all(moments, ("slab", "brick"), 0, 0, tiled=True)
     (nodal,) = call(nodal_kernel, [(3, 48, 384)], zeroth, first, second)

time: 37.2 us -> 36.9 us (level)
  waiting for transfers between devices: 17.2 us -> 16.3 us
  Pallas kernels: 6.39 us -> 6.84 us
    ppermute x4, waiting for transfers between devices: 10.5 us -> 9.51 us  [swap(): lax.ppermute(far, axis, [(i, (i + (1 if i % 2 else -1)) % count) for i in...]
    pallas_call x11, Pallas kernels: 6.39 us -> 6.84 us  [call(): pl.pallas_call(kernel, out_shape=shapes, in_specs=[HBM] * in_hbm + [VMEM]...]
  transfers between devices with their start and end apart: 9 -> 9, of which waited for: 6 -> 6; matrix products, arithmetic and copies ran while one was open for 0% -> 0% of each run, Pallas kernels for 6% -> 8%
where the time goes in v7:
time: 36.9 us; the launch traced here: 36.6 us
  waiting for transfers between devices  16.3 us (44%)
  starting transfers between devices  12 us (33%)
  Pallas kernels  6.84 us (19%)
  between operations  0.77 us (2%)
  local copies, waits for them, and re-layouts  0.68 us (2%)
    ppermute x4, waiting for transfers between devices, swap(): lax.ppermute(far, axis, [(i, (i + (1 if i % 2 else -1)) % count) for i in...  9.51 us
    ppermute x4, starting transfers between devices, swap(): lax.ppermute(far, axis, [(i, (i + (1 if i % 2 else -1)) % count) for i in...  8.68 us
    pallas_call x11, Pallas kernels, call(): pl.pallas_call(kernel, out_shape=shapes, in_specs=[HBM] * in_hbm + [VMEM]...  6.84 us
    all_to_all x1, waiting for transfers between devices, local(): moments = lax.all_to_all(moments, ('slab', 'brick'), 0, 0, tiled=True)  4.77 us
    all_to_all x1, starting transfers between devices, local(): moments = lax.all_to_all(moments, ('slab', 'brick'), 0, 0, tiled=True)  2.93 us
    ppermute x4, waiting for transfers between devices, swap(): lax.ppermute(near, axis, [(i, i + (-1 if i % 2 else 1)) for i in range(co...  2 us
  transfers between devices with their start and end apart: 9, of which 6 were waited for; matrix products, arithmetic and copies ran while one was open for 0% of the time, Pallas kernels for 8%

profile of v7, /device:TPU:0, one launch (start us, length us, event | category | flops | bytes accessed | tf_op | source)
XLA Modules:
  0.0 36.6 jit_solution(11590081064818777248)
XLA Ops:
  0.6 1.3 %force_kernel.1 = (f32[54,8,128]{2,1,0:T(8,128)S(1)}, bf16[27,4,128]{2,1,0:T(4,128)(2,1)S(1)}, bf16[27,4,128]{2,1,0:T(4,128)(2,1)S(1)}, f32[4,8,128]{2,1,0:T(8,128)S(1)}, f32[9,8,128]{2,1,0:T(8,128)S(1)}) custom-call(bf16[324,8,128]{2,1,0:T(8,128)(2,1)} %bitcast.13, f32[4,8,128]{2,1,0:T(8,128)} %bitcast.19, f32[4,8,128]{2,1,0:T(8,128)} %bitcast.21, ...), custom_call_target="tpu_custom_call" | custom-call | flops 100000 | bytes 1138688 | tf_op jit(solution)/shard_map/force_kernel/pallas_call | solution.py:593
  2.0 3.4 %collective-permute-start = (bf16[27,4,128]{2,1,0:T(4,128)(2,1)S(1)}, bf16[27,4,128]{2,1,0:T(4,128)(2,1)S(1)}, u32[]{:S(2)}, u32[]{:S(2)}) collective-permute-start(bf16[27,4,128]{2,1,0:T(4,128)(2,1)S(1)} %get-tuple-element.28), channel_id=1, source_target_pairs={{0,28},{4,8},{8,4},{12,16},{16,12},{20,24},{24,20},{28,0},{1,29},{... | collective-permute-start | bytes 82952 | tf_op jit(solution)/shard_map/ppermute | solution.py:607
  5.4 0.0 collective-permute-start.1
  5.4 1.3 %spread_kernel.1 = (f32[36,8,128]{2,1,0:T(8,128)S(1)}, f32[56,8,128]{2,1,0:T(8,128)S(1)}, bf16[79,2,128]{2,1,0:T(2,128)(2,1)S(1)}, bf16[79,2,128]{2,1,0:T(2,128)(2,1)S(1)}) custom-call(bf16[324,8,128]{2,1,0:T(8,128)(2,1)} %bitcast.14, f32[3,2,8,257]{3,2,1,0:T(8,128)S(1)} %copy-done.2, f32[4,8,128]{2,1,0:T(8,128)S(1)} %get-tuple-element.30.pressure_in, ...), custom_call_target="tpu_custom_call" | custom-call | flops 100000 | bytes 1360064 | tf_op jit(solution)/shard_map/spread_kernel/pallas_call | solution.py:593
  6.7 0.2 collective-permute-done.far
  6.9 0.0 collective-permute-done.1.near
  6.9 0.1 rim_kernel.1
  7.1 4.6 %collective-permute-start.2 = (bf16[79,2,128]{2,1,0:T(2,128)(2,1)S(1)}, bf16[79,2,128]{2,1,0:T(2,128)(2,1)S(1)}, u32[]{:S(2)}, u32[]{:S(2)}) collective-permute-start(bf16[79,2,128]{2,1,0:T(2,128)(2,1)S(1)} %get-tuple-element.36), channel_id=1, source_target_pairs={{0,3},{1,2},{2,1},{3,0},{4,7},{5,6},{6,5},{7,4},{8,11},{9,10},{10,... | collective-permute-start | bytes 121352 | tf_op jit(solution)/shard_map/ppermute | solution.py:607
  11.7 2.0 %collective-permute-done.2.far_in = bf16[79,2,128]{2,1,0:T(2,128)(2,1)S(1)} collective-permute-done((bf16[79,2,128]{2,1,0:T(2,128)(2,1)S(1)}, bf16[79,2,128]{2,1,0:T(2,128)(2,1)S(1)}, u32[]{:S(2)}, u32[]{:S(2)}) %collective-permute-start.2) | collective-permute-done | bytes 40480 | tf_op jit(solution)/shard_map/ppermute | solution.py:607
  13.7 2.0 %collective-permute-done.3.near_in = bf16[79,2,128]{2,1,0:T(2,128)(2,1)S(1)} collective-permute-done((bf16[79,2,128]{2,1,0:T(2,128)(2,1)S(1)}, bf16[79,2,128]{2,1,0:T(2,128)(2,1)S(1)}, u32[]{:S(2)}, u32[]{:S(2)}) %collective-permute-start.3) | collective-permute-done | bytes 40480 | tf_op jit(solution)/shard_map/ppermute | solution.py:608
  15.7 0.4 %first_kernel.1 = (f32[54,8,128]{2,1,0:T(8,128)S(1)}, f32[27,8,128]{2,1,0:T(8,128)S(1)}, f32[54,8,128]{2,1,0:T(8,128)S(1)}, bf16[13,8,128]{2,1,0:T(8,128)(2,1)S(1)}, bf16[13,8,128]{2,1,0:T(8,128)(2,1)S(1)}) custom-call(f32[55,8,128]{2,1,0:T(8,128)S(1)} %get-tuple-element.35.own, bf16[79,2,128]{2,1,0:T(2,128)(2,1)S(1)} %collective-permute-done.2.far_in, ...), custom_call_target="tpu_custom_call" | custom-call | flops 100000 | bytes 1020928 | tf_op jit(solution)/shard_map/first_kernel/pallas_call | solution.py:593
  16.1 0.3 collective-permute-start.4
  16.4 0.4 %collective-permute-start.5 = (bf16[13,8,128]{2,1,0:T(8,128)(2,1)S(1)}, bf16[13,8,128]{2,1,0:T(8,128)(2,1)S(1)}, u32[]{:S(2)}, u32[]{:S(2)}) collective-permute-start(bf16[13,8,128]{2,1,0:T(8,128)(2,1)S(1)} %get-tuple-element.40), channel_id=1, source_target_pairs={{0,4},{4,0},{8,12},{12,8},{16,20},{20,16},{24,28},{28,24},{1,5},{5... | collective-permute-start | bytes 79880 | tf_op jit(solution)/shard_map/ppermute | solution.py:608
  16.8 0.1 speed_kernel.1
  17.0 3.3 %collective-permute-done.4.far_in = bf16[13,8,128]{2,1,0:T(8,128)(2,1)S(1)} collective-permute-done((bf16[13,8,128]{2,1,0:T(8,128)(2,1)S(1)}, bf16[13,8,128]{2,1,0:T(8,128)(2,1)S(1)}, u32[]{:S(2)}, u32[]{:S(2)}) %collective-permute-start.4) | collective-permute-done | bytes 26656 | tf_op jit(solution)/shard_map/ppermute | solution.py:607
  20.3 0.0 collective-permute-done.5.near_in
  20.3 0.3 second_kernel.1
  20.6 0.3 collective-permute-start.6
  20.9 0.1 product_kernel.1.products
  21.0 3.9 %collective-permute-done.6.far = bf16[17,8,128]{2,1,0:T(8,128)(2,1)S(1)} collective-permute-done((bf16[17,8,128]{2,1,0:T(8,128)(2,1)S(1)}, bf16[17,8,128]{2,1,0:T(8,128)(2,1)S(1)}, u32[]{:S(2)}, u32[]{:S(2)}) %collective-permute-start.6) | collective-permute-done | bytes 34848 | tf_op jit(solution)/shard_map/ppermute | solution.py:607
  24.9 0.0 collective-permute-done.7.near
  24.9 0.9 %moment_kernel.1 = (f32[54,8,128]{2,1,0:T(8,128)S(1)}, f32[32,128]{1,0:T(8,128)}) custom-call(f32[54,8,128]{2,1,0:T(8,128)S(1)} %get-tuple-element.44.image, bf16[17,8,128]{2,1,0:T(8,128)(2,1)S(1)} %collective-permute-done.6.far, bf16[17,8,128]{2,1,0:T(8,128)(2,1)S(1)} %collective-permute-done.7.near, f32[27,8,128]{2,1,0:T(8,128)S(1)} %get-tuple-element.41.weight, ...), custom_call_target="tpu_custom_call" | custom-call | flops 100000 | bytes 872448 | tf_op jit(solution)/shard_map/moment_kernel/pallas_call | solution.py:593
  25.8 2.9 %all-to-all-start = ((f32[32,1,128]{2,1,0:T(1,128)}), f32[32,1,128]{2,1,0:T(1,128)S(1)}, u32[]{:S(2)}, u32[]{:S(2)}) async-start(f32[32,1,128]{2,1,0:T(1,128)} %bitcast.6), calls=%async_computation | async-start | bytes 32768 | tf_op jit(solution)/shard_map/all_to_all | solution.py:681
  28.7 0.0 copy-start.3
  28.7 0.0 copy-start.4
  28.7 0.0 copy-start.5
  28.8 0.8 %nodal_kernel.1.nodal = f32[3,48,384]{2,1,0:T(8,128)S(1)} custom-call(f32[54,8,128]{2,1,0:T(8,128)S(1)} %get-tuple-element.48.zeroth, f32[54,8,128]{2,1,0:T(8,128)S(1)} %get-tuple-element.47.first, f32[54,8,128]{2,1,0:T(8,128)S(1)} %get-tuple-element.50.second), custom_call_target="tpu_custom_call" | custom-call | flops 100000 | bytes 884736 | tf_op jit(solution)/shard_map/nodal_kernel/pallas_call | solution.py:593
  29.6 0.0 copy-start.6
  29.6 0.6 %copy-done.6 = s32[1,4,128]{2,1,0:T(4,128)S(1)} copy-done((s32[1,4,128]{2,1,0:T(4,128)S(1)}, s32[1,4,128]{2,1,0:T(4,128)}, u32[]{:S(2)}) %copy-start.6) | copy-done | bytes 2072
  30.3 0.8 %work_kernel.1 = f32[4,8,128]{2,1,0:T(8,128)} custom-call(bf16[324,8,128]{2,1,0:T(8,128)(2,1)S(1)} %bitcast.15, f32[4,8,128]{2,1,0:T(8,128)S(1)} %bitcast.20, f32[4,8,128]{2,1,0:T(8,128)S(1)} %bitcast.22, s32[4,128]{1,0:T(4,128)S(1)} %bitcast.26, f32[4,8,128]{2,1,0:T(8,128)S(1)} %bitcast.24, f32[54,8,128]{2,1,0:T(8,128)S(1)} %get-tuple-element.51.speeds, ...), custom_call_target="tpu_custom_call" | custom-call | flops 100000 | bytes 1021952 | tf_op jit(solution)/shard_map/work_kernel/pallas_call | solution.py:593
  31.1 4.8 %all-to-all-done = f32[32,1,128]{2,1,0:T(1,128)S(1)} async-done(((f32[32,1,128]{2,1,0:T(1,128)}), f32[32,1,128]{2,1,0:T(1,128)S(1)}, u32[]{:S(2)}, u32[]{:S(2)}) %all-to-all-start) | async-done | bytes 16416 | tf_op jit(solution)/shard_map/all_to_all | solution.py:681
  35.8 0.8 %last_kernel.1 = f32[3,2,8,257]{3,2,1,0:T(8,128)} custom-call(f32[32,128]{1,0:T(8,128)S(1)} %bitcast.23, f32[3,48,384]{2,1,0:T(8,128)S(1)} %nodal_kernel.1.nodal, f32[3,2,8,257]{3,2,1,0:T(8,128)S(1)} %copy-done.2), custom_call_target="tpu_custom_call" | custom-call | flops 100000 | bytes 336256 | tf_op jit(solution)/shard_map/last_kernel/pallas_call | solution.py:593
  (11 shorter events, 0.0 us)
Async XLA Ops:
  0.6 4.7 %copy-start.1 = (f32[27,1,4,128]{3,2,1,0:T(4,128)S(1)}, f32[27,1,4,128]{3,2,1,0:T(4,128)}, u32[]{:S(2)}) copy-start(f32[27,1,4,128]{3,2,1,0:T(4,128)} %param.12) | copy-start | bytes 165892
  0.6 4.7 %copy-start.2 = (f32[3,2,8,257]{3,2,1,0:T(8,128)S(1)}, f32[3,2,8,257]{3,2,1,0:T(8,128)}, u32[]{:S(2)}) copy-start(f32[3,2,8,257]{3,2,1,0:T(8,128)} %velocity.3) | copy-start | bytes 148036
  2.0 4.9 %collective-permute-start = (bf16[27,4,128]{2,1,0:T(4,128)(2,1)S(1)}, bf16[27,4,128]{2,1,0:T(4,128)(2,1)S(1)}, u32[]{:S(2)}, u32[]{:S(2)}) collective-permute-start(bf16[27,4,128]{2,1,0:T(4,128)(2,1)S(1)} %get-tuple-element.28), channel_id=1, source_target_pairs={{0,28},{4,8},{8,4},{12,16},{16,12},{20,24},{24,20},{28,0},{1,29},{... | collective-permute-start | bytes 82952 | tf_op jit(solution)/shard_map/ppermute | solution.py:607
  5.4 1.6 %collective-permute-start.1 = (bf16[27,4,128]{2,1,0:T(4,128)(2,1)S(1)}, bf16[27,4,128]{2,1,0:T(4,128)(2,1)S(1)}, u32[]{:S(2)}, u32[]{:S(2)}) collective-permute-start(bf16[27,4,128]{2,1,0:T(4,128)(2,1)S(1)} %get-tuple-element.29), channel_id=1, source_target_pairs={{0,4},{4,0},{8,12},{12,8},{16,20},{20,16},{24,28},{28,24},{1,5},{5... | collective-permute-start | bytes 82952 | tf_op jit(solution)/shard_map/ppermute | solution.py:608
  7.1 6.6 %collective-permute-start.2 = (bf16[79,2,128]{2,1,0:T(2,128)(2,1)S(1)}, bf16[79,2,128]{2,1,0:T(2,128)(2,1)S(1)}, u32[]{:S(2)}, u32[]{:S(2)}) collective-permute-start(bf16[79,2,128]{2,1,0:T(2,128)(2,1)S(1)} %get-tuple-element.36), channel_id=1, source_target_pairs={{0,3},{1,2},{2,1},{3,0},{4,7},{5,6},{6,5},{7,4},{8,11},{9,10},{10,... | collective-permute-start | bytes 121352 | tf_op jit(solution)/shard_map/ppermute | solution.py:607
  11.7 4.0 %collective-permute-start.3 = (bf16[79,2,128]{2,1,0:T(2,128)(2,1)S(1)}, bf16[79,2,128]{2,1,0:T(2,128)(2,1)S(1)}, u32[]{:S(2)}, u32[]{:S(2)}) collective-permute-start(bf16[79,2,128]{2,1,0:T(2,128)(2,1)S(1)} %get-tuple-element.37), channel_id=1, source_target_pairs={{0,1},{1,0},{2,3},{3,2},{4,5},{5,4},{6,7},{7,6},{8,9},{9,8},{10,11... | collective-permute-start | bytes 121352 | tf_op jit(solution)/shard_map/ppermute | solution.py:608
  16.1 4.2 %collective-permute-start.4 = (bf16[13,8,128]{2,1,0:T(8,128)(2,1)S(1)}, bf16[13,8,128]{2,1,0:T(8,128)(2,1)S(1)}, u32[]{:S(2)}, u32[]{:S(2)}) collective-permute-start(bf16[13,8,128]{2,1,0:T(8,128)(2,1)S(1)} %get-tuple-element.39), channel_id=1, source_target_pairs={{0,28},{4,8},{8,4},{12,16},{16,12},{20,24},{24,20},{28,0},{1,29},{... | collective-permute-start | bytes 79880 | tf_op jit(solution)/shard_map/ppermute | solution.py:607
  16.4 3.9 %collective-permute-start.5 = (bf16[13,8,128]{2,1,0:T(8,128)(2,1)S(1)}, bf16[13,8,128]{2,1,0:T(8,128)(2,1)S(1)}, u32[]{:S(2)}, u32[]{:S(2)}) collective-permute-start(bf16[13,8,128]{2,1,0:T(8,128)(2,1)S(1)} %get-tuple-element.40), channel_id=1, source_target_pairs={{0,4},{4,0},{8,12},{12,8},{16,20},{20,16},{24,28},{28,24},{1,5},{5... | collective-permute-start | bytes 79880 | tf_op jit(solution)/shard_map/ppermute | solution.py:608
  20.6 4.3 %collective-permute-start.6 = (bf16[17,8,128]{2,1,0:T(8,128)(2,1)S(1)}, bf16[17,8,128]{2,1,0:T(8,128)(2,1)S(1)}, u32[]{:S(2)}, u32[]{:S(2)}) collective-permute-start(bf16[17,8,128]{2,1,0:T(8,128)(2,1)S(1)} %get-tuple-element.45), channel_id=1, source_target_pairs={{0,28},{4,8},{8,4},{12,16},{16,12},{20,24},{24,20},{28,0},{1,29},{... | collective-permute-start | bytes 104456 | tf_op jit(solution)/shard_map/ppermute | solution.py:607
  20.9 4.0 %collective-permute-start.7 = (bf16[17,8,128]{2,1,0:T(8,128)(2,1)S(1)}, bf16[17,8,128]{2,1,0:T(8,128)(2,1)S(1)}, u32[]{:S(2)}, u32[]{:S(2)}) collective-permute-start(bf16[17,8,128]{2,1,0:T(8,128)(2,1)S(1)} %get-tuple-element.46), channel_id=1, source_target_pairs={{0,4},{4,0},{8,12},{12,8},{16,20},{20,16},{24,28},{28,24},{1,5},{5... | collective-permute-start | bytes 104456 | tf_op jit(solution)/shard_map/ppermute | solution.py:608
  24.9 4.7 %copy-start = (bf16[81,8,1,4,128]{4,3,2,1,0:T(4,128)(2,1)S(1)}, bf16[81,8,1,4,128]{4,3,2,1,0:T(4,128)(2,1)}, u32[]{:S(2)}) copy-start(bf16[81,8,1,4,128]{4,3,2,1,0:T(4,128)(2,1)} %param.11) | copy-start | bytes 1990660
  25.8 10.0 %all-to-all-start = ((f32[32,1,128]{2,1,0:T(1,128)}), f32[32,1,128]{2,1,0:T(1,128)S(1)}, u32[]{:S(2)}, u32[]{:S(2)}) async-start(f32[32,1,128]{2,1,0:T(1,128)} %bitcast.6), calls=%async_computation | async-start | bytes 32768 | tf_op jit(solution)/shard_map/all_to_all | solution.py:681
  28.7 0.9 %copy-start.3 = (f32[8,1,4,128]{3,2,1,0:T(4,128)S(1)}, f32[8,1,4,128]{3,2,1,0:T(4,128)}, u32[]{:S(2)}) copy-start(f32[8,1,4,128]{3,2,1,0:T(4,128)} %param.9) | copy-start | bytes 49156
  28.7 0.9 %copy-start.4 = (f32[8,1,4,128]{3,2,1,0:T(4,128)S(1)}, f32[8,1,4,128]{3,2,1,0:T(4,128)}, u32[]{:S(2)}) copy-start(f32[8,1,4,128]{3,2,1,0:T(4,128)} %param.8) | copy-start | bytes 49156
  28.7 0.9 %copy-start.5 = (f32[8,1,4,128]{3,2,1,0:T(4,128)S(1)}, f32[8,1,4,128]{3,2,1,0:T(4,128)}, u32[]{:S(2)}) copy-start(f32[8,1,4,128]{3,2,1,0:T(4,128)} %param.13) | copy-start | bytes 49156
  29.6 0.7 %copy-start.6 = (s32[1,4,128]{2,1,0:T(4,128)S(1)}, s32[1,4,128]{2,1,0:T(4,128)}, u32[]{:S(2)}) copy-start(s32[1,4,128]{2,1,0:T(4,128)} %param.10) | copy-start | bytes 6148

commit v8 on v7

--- a/solution.py
+++ b/solution.py
@@ -456,9 +456,9 @@
     send_own(planes, speeds, near, far, even)
 
 
-def work_kernel(geometry, density, energy, material, energy_mass, speeds, far, near, out):
+def work_kernel(geometry, pressure_in, energy, energy_mass, speeds, far, near, out):
     even = is_even()
-    pressure = pressure_of(density, energy, material)
+    pressure = pressure_in[...]
     work = jnp.zeros_like(pressure)
     row = lax.broadcasted_iota(jnp.int32, (8, 128), 0)
     lane = lane_of((8, 128))
@@ -672,7 +672,7 @@
     )
     near, far = swap(near, far)
     (energy_half,) = call(
-        work_kernel, [(4,) + full], geometry, density, energy, material, energy_mass, speeds, far, near
+        work_kernel, [(4,) + full], geometry, pressure, energy, energy_mass, speeds, far, near
     )
     (products,) = call(product_kernel, [(3,) + full], zeroth, first)
     second, moments = call(

time: 36.9 us -> 36.8 us (level)
  local copies, waits for them, and re-layouts: 0.68 us -> 0.03 us
  waiting for transfers between devices: 16.3 us -> 16.9 us
    all_to_all x1, waiting for transfers between devices: 4.77 us -> 5.44 us  [local(): moments = lax.all_to_all(moments, ('slab', 'brick'), 0, 0, tiled=True)]
    unnamed x14 -> x10, local copies, waits for them, and re-layouts: 0.68 us -> 0.03 us
where the time goes in v8:
time: 36.8 us; the launch traced here: 36.6 us
  waiting for transfers between devices  16.9 us (46%)
  starting transfers between devices  12 us (33%)
  Pallas kernels  6.84 us (19%)
  between operations  0.74 us (2%)
    ppermute x4, waiting for transfers between devices, swap(): lax.ppermute(far, axis, [(i, (i + (1 if i % 2 else -1)) % count) for i in...  9.51 us
    ppermute x4, starting transfers between devices, swap(): lax.ppermute(far, axis, [(i, (i + (1 if i % 2 else -1)) % count) for i in...  8.68 us
    pallas_call x11, Pallas kernels, call(): pl.pallas_call(kernel, out_shape=shapes, in_specs=[HBM] * in_hbm + [VMEM]...  6.84 us
    all_to_all x1, waiting for transfers between devices, local(): moments = lax.all_to_all(moments, ('slab', 'brick'), 0, 0, tiled=True)  5.44 us
    all_to_all x1, starting transfers between devices, local(): moments = lax.all_to_all(moments, ('slab', 'brick'), 0, 0, tiled=True)  2.93 us
    ppermute x4, waiting for transfers between devices, swap(): lax.ppermute(near, axis, [(i, i + (-1 if i % 2 else 1)) for i in range(co...  2 us
  transfers between devices with their start and end apart: 9, of which 6 were waited for; matrix products, arithmetic and copies ran while one was open for 0% of the time, Pallas kernels for 8%

profile of v8, /device:TPU:0, one launch (start us, length us, event | category | flops | bytes accessed | tf_op | source)
XLA Modules:
  0.0 36.6 jit_solution(2781808229046479431)
XLA Ops:
  0.7 1.3 %force_kernel.1 = (f32[54,8,128]{2,1,0:T(8,128)S(1)}, bf16[27,4,128]{2,1,0:T(4,128)(2,1)S(1)}, bf16[27,4,128]{2,1,0:T(4,128)(2,1)S(1)}, f32[4,8,128]{2,1,0:T(8,128)S(1)}, f32[9,8,128]{2,1,0:T(8,128)S(1)}) custom-call(bf16[324,8,128]{2,1,0:T(8,128)(2,1)} %bitcast.13, f32[4,8,128]{2,1,0:T(8,128)} %bitcast.24, f32[4,8,128]{2,1,0:T(8,128)} %bitcast.19, ...), custom_call_target="tpu_custom_call" | custom-call | flops 100000 | bytes 1138688 | tf_op jit(solution)/shard_map/force_kernel/pallas_call | solution.py:593
  2.0 3.4 %collective-permute-start = (bf16[27,4,128]{2,1,0:T(4,128)(2,1)S(1)}, bf16[27,4,128]{2,1,0:T(4,128)(2,1)S(1)}, u32[]{:S(2)}, u32[]{:S(2)}) collective-permute-start(bf16[27,4,128]{2,1,0:T(4,128)(2,1)S(1)} %get-tuple-element.28), channel_id=1, source_target_pairs={{0,28},{4,8},{8,4},{12,16},{16,12},{20,24},{24,20},{28,0},{1,29},{... | collective-permute-start | bytes 82952 | tf_op jit(solution)/shard_map/ppermute | solution.py:607
  5.4 0.0 collective-permute-start.1
  5.4 1.3 %spread_kernel.1 = (f32[36,8,128]{2,1,0:T(8,128)S(1)}, f32[56,8,128]{2,1,0:T(8,128)S(1)}, bf16[79,2,128]{2,1,0:T(2,128)(2,1)S(1)}, bf16[79,2,128]{2,1,0:T(2,128)(2,1)S(1)}) custom-call(bf16[324,8,128]{2,1,0:T(8,128)(2,1)} %bitcast.14, f32[3,2,8,257]{3,2,1,0:T(8,128)S(1)} %copy-done.2, f32[4,8,128]{2,1,0:T(8,128)S(1)} %get-tuple-element.30.pressure_in, ...), custom_call_target="tpu_custom_call" | custom-call | flops 100000 | bytes 1360064 | tf_op jit(solution)/shard_map/spread_kernel/pallas_call | solution.py:593
  6.7 0.2 collective-permute-done.far
  6.9 0.0 collective-permute-done.1.near
  6.9 0.1 rim_kernel.1
  7.1 4.6 %collective-permute-start.2 = (bf16[79,2,128]{2,1,0:T(2,128)(2,1)S(1)}, bf16[79,2,128]{2,1,0:T(2,128)(2,1)S(1)}, u32[]{:S(2)}, u32[]{:S(2)}) collective-permute-start(bf16[79,2,128]{2,1,0:T(2,128)(2,1)S(1)} %get-tuple-element.36), channel_id=1, source_target_pairs={{0,3},{1,2},{2,1},{3,0},{4,7},{5,6},{6,5},{7,4},{8,11},{9,10},{10,... | collective-permute-start | bytes 121352 | tf_op jit(solution)/shard_map/ppermute | solution.py:607
  11.7 0.0 collective-permute-start.3
  11.7 2.0 %collective-permute-done.2.far_in = bf16[79,2,128]{2,1,0:T(2,128)(2,1)S(1)} collective-permute-done((bf16[79,2,128]{2,1,0:T(2,128)(2,1)S(1)}, bf16[79,2,128]{2,1,0:T(2,128)(2,1)S(1)}, u32[]{:S(2)}, u32[]{:S(2)}) %collective-permute-start.2) | collective-permute-done | bytes 40480 | tf_op jit(solution)/shard_map/ppermute | solution.py:607
  13.7 2.0 %collective-permute-done.3.near_in = bf16[79,2,128]{2,1,0:T(2,128)(2,1)S(1)} collective-permute-done((bf16[79,2,128]{2,1,0:T(2,128)(2,1)S(1)}, bf16[79,2,128]{2,1,0:T(2,128)(2,1)S(1)}, u32[]{:S(2)}, u32[]{:S(2)}) %collective-permute-start.3) | collective-permute-done | bytes 40480 | tf_op jit(solution)/shard_map/ppermute | solution.py:608
  15.7 0.4 %first_kernel.1 = (f32[54,8,128]{2,1,0:T(8,128)S(1)}, f32[27,8,128]{2,1,0:T(8,128)S(1)}, f32[54,8,128]{2,1,0:T(8,128)S(1)}, bf16[13,8,128]{2,1,0:T(8,128)(2,1)S(1)}, bf16[13,8,128]{2,1,0:T(8,128)(2,1)S(1)}) custom-call(f32[55,8,128]{2,1,0:T(8,128)S(1)} %get-tuple-element.35.own, bf16[79,2,128]{2,1,0:T(2,128)(2,1)S(1)} %collective-permute-done.2.far_in, ...), custom_call_target="tpu_custom_call" | custom-call | flops 100000 | bytes 1020928 | tf_op jit(solution)/shard_map/first_kernel/pallas_call | solution.py:593
  16.1 0.3 collective-permute-start.4
  16.4 0.4 %collective-permute-start.5 = (bf16[13,8,128]{2,1,0:T(8,128)(2,1)S(1)}, bf16[13,8,128]{2,1,0:T(8,128)(2,1)S(1)}, u32[]{:S(2)}, u32[]{:S(2)}) collective-permute-start(bf16[13,8,128]{2,1,0:T(8,128)(2,1)S(1)} %get-tuple-element.40), channel_id=1, source_target_pairs={{0,4},{4,0},{8,12},{12,8},{16,20},{20,16},{24,28},{28,24},{1,5},{5... | collective-permute-start | bytes 79880 | tf_op jit(solution)/shard_map/ppermute | solution.py:608
  16.8 0.1 speed_kernel.1
  17.0 3.3 %collective-permute-done.4.far_in = bf16[13,8,128]{2,1,0:T(8,128)(2,1)S(1)} collective-permute-done((bf16[13,8,128]{2,1,0:T(8,128)(2,1)S(1)}, bf16[13,8,128]{2,1,0:T(8,128)(2,1)S(1)}, u32[]{:S(2)}, u32[]{:S(2)}) %collective-permute-start.4) | collective-permute-done | bytes 26656 | tf_op jit(solution)/shard_map/ppermute | solution.py:607
  20.3 0.0 collective-permute-done.5.near_in
  20.3 0.3 second_kernel.1
  20.6 0.3 collective-permute-start.6
  20.9 0.0 collective-permute-start.7
  20.9 0.1 product_kernel.1.products
  21.0 3.9 %collective-permute-done.6.far = bf16[17,8,128]{2,1,0:T(8,128)(2,1)S(1)} collective-permute-done((bf16[17,8,128]{2,1,0:T(8,128)(2,1)S(1)}, bf16[17,8,128]{2,1,0:T(8,128)(2,1)S(1)}, u32[]{:S(2)}, u32[]{:S(2)}) %collective-permute-start.6) | collective-permute-done | bytes 34848 | tf_op jit(solution)/shard_map/ppermute | solution.py:607
  24.9 0.0 collective-permute-done.7.near
  24.9 0.9 %moment_kernel.1 = (f32[54,8,128]{2,1,0:T(8,128)S(1)}, f32[32,128]{1,0:T(8,128)}) custom-call(f32[54,8,128]{2,1,0:T(8,128)S(1)} %get-tuple-element.44.image, bf16[17,8,128]{2,1,0:T(8,128)(2,1)S(1)} %collective-permute-done.6.far, bf16[17,8,128]{2,1,0:T(8,128)(2,1)S(1)} %collective-permute-done.7.near, f32[27,8,128]{2,1,0:T(8,128)S(1)} %get-tuple-element.41.weight, ...), custom_call_target="tpu_custom_call" | custom-call | flops 100000 | bytes 872448 | tf_op jit(solution)/shard_map/moment_kernel/pallas_call | solution.py:593
  25.8 2.9 %all-to-all-start = ((f32[32,1,128]{2,1,0:T(1,128)}), f32[32,1,128]{2,1,0:T(1,128)S(1)}, u32[]{:S(2)}, u32[]{:S(2)}) async-start(f32[32,1,128]{2,1,0:T(1,128)} %bitcast.6), calls=%async_computation | async-start | bytes 32768 | tf_op jit(solution)/shard_map/all_to_all | solution.py:681
  28.7 0.0 copy-start.3
  28.7 0.0 copy-start.4
  28.8 0.8 %nodal_kernel.1.nodal = f32[3,48,384]{2,1,0:T(8,128)S(1)} custom-call(f32[54,8,128]{2,1,0:T(8,128)S(1)} %get-tuple-element.48.zeroth, f32[54,8,128]{2,1,0:T(8,128)S(1)} %get-tuple-element.47.first, f32[54,8,128]{2,1,0:T(8,128)S(1)} %get-tuple-element.50.second), custom_call_target="tpu_custom_call" | custom-call | flops 100000 | bytes 884736 | tf_op jit(solution)/shard_map/nodal_kernel/pallas_call | solution.py:593
  29.6 0.0 copy-done
  29.6 0.8 %work_kernel.1 = f32[4,8,128]{2,1,0:T(8,128)} custom-call(bf16[324,8,128]{2,1,0:T(8,128)(2,1)S(1)} %bitcast.15, f32[4,8,128]{2,1,0:T(8,128)S(1)} %get-tuple-element.30.pressure_in, f32[4,8,128]{2,1,0:T(8,128)S(1)} %bitcast.20, f32[4,8,128]{2,1,0:T(8,128)S(1)} %bitcast.22, f32[54,8,128]{2,1,0:T(8,128)S(1)} %get-tuple-element.51.speeds, ...), custom_call_target="tpu_custom_call" | custom-call | flops 100000 | bytes 1019904 | tf_op jit(solution)/shard_map/work_kernel/pallas_call | solution.py:593
  30.4 5.4 %all-to-all-done = f32[32,1,128]{2,1,0:T(1,128)S(1)} async-done(((f32[32,1,128]{2,1,0:T(1,128)}), f32[32,1,128]{2,1,0:T(1,128)S(1)}, u32[]{:S(2)}, u32[]{:S(2)}) %all-to-all-start) | async-done | bytes 16416 | tf_op jit(solution)/shard_map/all_to_all | solution.py:681
  35.8 0.8 %last_kernel.1 = f32[3,2,8,257]{3,2,1,0:T(8,128)} custom-call(f32[32,128]{1,0:T(8,128)S(1)} %bitcast.21, f32[3,48,384]{2,1,0:T(8,128)S(1)} %nodal_kernel.1.nodal, f32[3,2,8,257]{3,2,1,0:T(8,128)S(1)} %copy-done.2), custom_call_target="tpu_custom_call" | custom-call | flops 100000 | bytes 336256 | tf_op jit(solution)/shard_map/last_kernel/pallas_call | solution.py:593
  (7 shorter events, 0.0 us)
Async XLA Ops:
  0.6 4.7 %copy-start.1 = (f32[27,1,4,128]{3,2,1,0:T(4,128)S(1)}, f32[27,1,4,128]{3,2,1,0:T(4,128)}, u32[]{:S(2)}) copy-start(f32[27,1,4,128]{3,2,1,0:T(4,128)} %param.12) | copy-start | bytes 165892
  0.6 4.7 %copy-start.2 = (f32[3,2,8,257]{3,2,1,0:T(8,128)S(1)}, f32[3,2,8,257]{3,2,1,0:T(8,128)}, u32[]{:S(2)}) copy-start(f32[3,2,8,257]{3,2,1,0:T(8,128)} %velocity.3) | copy-start | bytes 148036
  2.0 4.9 %collective-permute-start = (bf16[27,4,128]{2,1,0:T(4,128)(2,1)S(1)}, bf16[27,4,128]{2,1,0:T(4,128)(2,1)S(1)}, u32[]{:S(2)}, u32[]{:S(2)}) collective-permute-start(bf16[27,4,128]{2,1,0:T(4,128)(2,1)S(1)} %get-tuple-element.28), channel_id=1, source_target_pairs={{0,28},{4,8},{8,4},{12,16},{16,12},{20,24},{24,20},{28,0},{1,29},{... | collective-permute-start | bytes 82952 | tf_op jit(solution)/shard_map/ppermute | solution.py:607
  5.4 1.6 %collective-permute-start.1 = (bf16[27,4,128]{2,1,0:T(4,128)(2,1)S(1)}, bf16[27,4,128]{2,1,0:T(4,128)(2,1)S(1)}, u32[]{:S(2)}, u32[]{:S(2)}) collective-permute-start(bf16[27,4,128]{2,1,0:T(4,128)(2,1)S(1)} %get-tuple-element.29), channel_id=1, source_target_pairs={{0,4},{4,0},{8,12},{12,8},{16,20},{20,16},{24,28},{28,24},{1,5},{5... | collective-permute-start | bytes 82952 | tf_op jit(solution)/shard_map/ppermute | solution.py:608
  7.1 6.6 %collective-permute-start.2 = (bf16[79,2,128]{2,1,0:T(2,128)(2,1)S(1)}, bf16[79,2,128]{2,1,0:T(2,128)(2,1)S(1)}, u32[]{:S(2)}, u32[]{:S(2)}) collective-permute-start(bf16[79,2,128]{2,1,0:T(2,128)(2,1)S(1)} %get-tuple-element.36), channel_id=1, source_target_pairs={{0,3},{1,2},{2,1},{3,0},{4,7},{5,6},{6,5},{7,4},{8,11},{9,10},{10,... | collective-permute-start | bytes 121352 | tf_op jit(solution)/shard_map/ppermute | solution.py:607
  11.7 4.0 %collective-permute-start.3 = (bf16[79,2,128]{2,1,0:T(2,128)(2,1)S(1)}, bf16[79,2,128]{2,1,0:T(2,128)(2,1)S(1)}, u32[]{:S(2)}, u32[]{:S(2)}) collective-permute-start(bf16[79,2,128]{2,1,0:T(2,128)(2,1)S(1)} %get-tuple-element.37), channel_id=1, source_target_pairs={{0,1},{1,0},{2,3},{3,2},{4,5},{5,4},{6,7},{7,6},{8,9},{9,8},{10,11... | collective-permute-start | bytes 121352 | tf_op jit(solution)/shard_map/ppermute | solution.py:608
  16.1 4.2 %collective-permute-start.4 = (bf16[13,8,128]{2,1,0:T(8,128)(2,1)S(1)}, bf16[13,8,128]{2,1,0:T(8,128)(2,1)S(1)}, u32[]{:S(2)}, u32[]{:S(2)}) collective-permute-start(bf16[13,8,128]{2,1,0:T(8,128)(2,1)S(1)} %get-tuple-element.39), channel_id=1, source_target_pairs={{0,28},{4,8},{8,4},{12,16},{16,12},{20,24},{24,20},{28,0},{1,29},{... | collective-permute-start | bytes 79880 | tf_op jit(solution)/shard_map/ppermute | solution.py:607
  16.4 3.9 %collective-permute-start.5 = (bf16[13,8,128]{2,1,0:T(8,128)(2,1)S(1)}, bf16[13,8,128]{2,1,0:T(8,128)(2,1)S(1)}, u32[]{:S(2)}, u32[]{:S(2)}) collective-permute-start(bf16[13,8,128]{2,1,0:T(8,128)(2,1)S(1)} %get-tuple-element.40), channel_id=1, source_target_pairs={{0,4},{4,0},{8,12},{12,8},{16,20},{20,16},{24,28},{28,24},{1,5},{5... | collective-permute-start | bytes 79880 | tf_op jit(solution)/shard_map/ppermute | solution.py:608
  20.6 4.3 %collective-permute-start.6 = (bf16[17,8,128]{2,1,0:T(8,128)(2,1)S(1)}, bf16[17,8,128]{2,1,0:T(8,128)(2,1)S(1)}, u32[]{:S(2)}, u32[]{:S(2)}) collective-permute-start(bf16[17,8,128]{2,1,0:T(8,128)(2,1)S(1)} %get-tuple-element.45), channel_id=1, source_target_pairs={{0,28},{4,8},{8,4},{12,16},{16,12},{20,24},{24,20},{28,0},{1,29},{... | collective-permute-start | bytes 104456 | tf_op jit(solution)/shard_map/ppermute | solution.py:607
  20.9 4.0 %collective-permute-start.7 = (bf16[17,8,128]{2,1,0:T(8,128)(2,1)S(1)}, bf16[17,8,128]{2,1,0:T(8,128)(2,1)S(1)}, u32[]{:S(2)}, u32[]{:S(2)}) collective-permute-start(bf16[17,8,128]{2,1,0:T(8,128)(2,1)S(1)} %get-tuple-element.46), channel_id=1, source_target_pairs={{0,4},{4,0},{8,12},{12,8},{16,20},{20,16},{24,28},{28,24},{1,5},{5... | collective-permute-start | bytes 104456 | tf_op jit(solution)/shard_map/ppermute | solution.py:608
  24.9 4.7 %copy-start = (bf16[81,8,1,4,128]{4,3,2,1,0:T(4,128)(2,1)S(1)}, bf16[81,8,1,4,128]{4,3,2,1,0:T(4,128)(2,1)}, u32[]{:S(2)}) copy-start(bf16[81,8,1,4,128]{4,3,2,1,0:T(4,128)(2,1)} %param.11) | copy-start | bytes 1990660
  25.8 10.0 %all-to-all-start = ((f32[32,1,128]{2,1,0:T(1,128)}), f32[32,1,128]{2,1,0:T(1,128)S(1)}, u32[]{:S(2)}, u32[]{:S(2)}) async-start(f32[32,1,128]{2,1,0:T(1,128)} %bitcast.6), calls=%async_computation | async-start | bytes 32768 | tf_op jit(solution)/shard_map/all_to_all | solution.py:681
  28.7 0.9 %copy-start.3 = (f32[8,1,4,128]{3,2,1,0:T(4,128)S(1)}, f32[8,1,4,128]{3,2,1,0:T(4,128)}, u32[]{:S(2)}) copy-start(f32[8,1,4,128]{3,2,1,0:T(4,128)} %param.8) | copy-start | bytes 49156
  28.7 0.9 %copy-start.4 = (f32[8,1,4,128]{3,2,1,0:T(4,128)S(1)}, f32[8,1,4,128]{3,2,1,0:T(4,128)}, u32[]{:S(2)}) copy-start(f32[8,1,4,128]{3,2,1,0:T(4,128)} %param.13) | copy-start | bytes 49156

commit v9 on v8

--- a/solution.py
+++ b/solution.py
@@ -352,7 +352,7 @@
     send_planes(planes, near, far, even)
 
 
-def speed_kernel(far_in, near_in, spread, speeds, plane_out):
+def speed_kernel(far_in, near_in, spread, speeds, near, far):
     even_y = is_even("brick")
     row = lax.broadcasted_iota(jnp.int32, (8, 128), 0)
     lane = lane_of((8, 128))
@@ -376,15 +376,16 @@
                 for b in range(3):
                     plane += speed[3 * b : 3 * b + 2]
                     tops = to_lane(tops, lane, speed[3 * b + 2], SPEED_LANE + 3 * comp + b)
-    for k in range(9):
-        plane_out[k] = jnp.where(row < OWN, plane[2 * k], pltpu.roll(plane[2 * k + 1], OWN, 0))
-    plane_out[9] = tops
-
-
-def send_own(planes, speeds, near, far, even):
+    tiles = [jnp.where(row < OWN, plane[2 * k], pltpu.roll(plane[2 * k + 1], OWN, 0)) for k in range(9)]
+    for k, value in enumerate(tiles + [tops]):
+        near[k] = value.astype(BF16)
+        far[k] = value.astype(BF16)
+
+
+def send_own(planes, near, far, even):
     row = lax.broadcasted_iota(jnp.int32, (8, 128), 0)
     lane = lane_of((8, 128))
-    sides = [speeds[9], jnp.zeros((8, 128), F32)]
+    sides = [jnp.zeros((8, 128), F32)] * 2
     after = [jnp.zeros((8, 128), F32)] * 2
     for comp in range(3):
         for b in range(2):
@@ -400,9 +401,6 @@
             put(near, far, 2 * comp + b, both[0], both[1], even)
     put(near, far, 6, after[0], after[1], even)
     put(near, far, 7, sides[0], sides[1], even)
-    for k in range(9):
-        near[8 + k] = speeds[k].astype(BF16)
-        far[8 + k] = speeds[k].astype(BF16)
 
 
 def take_planes(image, near, far, comp, even):
@@ -453,7 +451,7 @@
         for n in range(18):
             image_out[18 * comp + n] = values[n]
         planes.append(values)
-    send_own(planes, speeds, near, far, even)
+    send_own(planes, near, far, even)
 
 
 def work_kernel(geometry, pressure_in, energy, energy_mass, speeds, far, near, out):
@@ -462,11 +460,11 @@
     work = jnp.zeros_like(pressure)
     row = lax.broadcasted_iota(jnp.int32, (8, 128), 0)
     lane = lane_of((8, 128))
-    tops = get(near, far, 7, even)[1]
+    tops = get(near, far, 9, even)[1]
     for comp in range(3):
         speed = [speeds[18 * comp + n] for n in range(18)]
         for b in range(3):
-            both = get(near, far, 8 + 3 * comp + b, even)[1]
+            both = get(near, far, 3 * comp + b, even)[1]
             speed += [both, pltpu.roll(both, OWN, 0)]
             speed.append(third_along_z(both, tops, lane, SPEED_LANE + 3 * comp + b))
         for n in range(27):
@@ -485,7 +483,7 @@
     return total
 
 
-def product_kernel(zeroth, first, products):
+def product_kernel(zeroth, first, far_speed, near_speed, products):
     for k, (one, other) in enumerate([(zeroth, zeroth), (zeroth, first), (first, first)]):
         total = jnp.zeros((8, 128), F32)
         for comp in range(3):
@@ -663,18 +661,24 @@
         dtypes=[F32, F32, F32, BF16, BF16],
     )
     near, far = swap(near, far)
-    speeds, plane = call(speed_kernel, [(54,) + full, (10,) + full], far_rim, near_rim, spread)
+    speeds, near_speed, far_speed = call(
+        speed_kernel,
+        [(54,) + full, (10,) + full, (10,) + full],
+        far_rim, near_rim, spread,
+        dtypes=[F32, BF16, BF16],
+    )
+    near_speed, far_speed = swap(near_speed, far_speed)
     first, image, near, far = call(
         second_kernel,
-        [(54,) + full, (54,) + full, (17,) + full, (17,) + full],
-        image, far, near, weight, plane,
+        [(54,) + full, (54,) + full, (8,) + full, (8,) + full],
+        image, far, near, weight, speeds,
         dtypes=[F32, F32, BF16, BF16],
     )
     near, far = swap(near, far)
     (energy_half,) = call(
-        work_kernel, [(4,) + full], geometry, pressure, energy, energy_mass, speeds, far, near
-    )
-    (products,) = call(product_kernel, [(3,) + full], zeroth, first)
+        work_kernel, [(4,) + full], geometry, pressure, energy, energy_mass, speeds, far_speed, near_speed
+    )
+    (products,) = call(product_kernel, [(3,) + full], zeroth, first, far_speed, near_speed)
     second, moments = call(
         moment_kernel, [(54,) + full, (devices, 128)], image, far, near, weight, first, products
     )

time: 36.8 us -> 36.7 us (level)
  waiting for transfers between devices: 16.9 us -> 14.4 us
  starting transfers between devices: 12 us -> 14.4 us
    ppermute x4 -> x5, waiting for transfers between devices: 9.51 us -> 6.94 us  [swap(): lax.ppermute(far, axis, [(i, (i + (1 if i % 2 else -1)) % count) for i in...]
    ppermute x4 -> x5, starting transfers between devices: 8.68 us -> 10.7 us  [swap(): lax.ppermute(far, axis, [(i, (i + (1 if i % 2 else -1)) % count) for i in...]
    ppermute x4 -> x5, starting transfers between devices: 0.43 us -> 0.8 us  [swap(): lax.ppermute(near, axis, [(i, i + (-1 if i % 2 else 1)) for i in range(co...]
    ppermute x4 -> x5, waiting for transfers between devices: 2 us -> 2 us  [swap(): lax.ppermute(near, axis, [(i, i + (-1 if i % 2 else 1)) for i in range(co...]
  transfers between devices with their start and end apart: 9 -> 11, of which waited for: 6 -> 7; matrix products, arithmetic and copies ran while one was open for 0% -> 0% of each run, Pallas kernels for 8% -> 9%
where the time goes in v9:
time: 36.7 us; the launch traced here: 36.4 us
  starting transfers between devices  14.4 us (39%)
  waiting for transfers between devices  14.4 us (39%)
  Pallas kernels  6.86 us (19%)
  between operations  0.74 us (2%)
    ppermute x5, starting transfers between devices, swap(): lax.ppermute(far, axis, [(i, (i + (1 if i % 2 else -1)) % count) for i in...  10.7 us
    ppermute x5, waiting for transfers between devices, swap(): lax.ppermute(far, axis, [(i, (i + (1 if i % 2 else -1)) % count) for i in...  6.94 us
    pallas_call x11, Pallas kernels, call(): pl.pallas_call(kernel, out_shape=shapes, in_specs=[HBM] * in_hbm + [VMEM]...  6.86 us
    all_to_all x1, waiting for transfers between devices, local(): moments = lax.all_to_all(moments, ('slab', 'brick'), 0, 0, tiled=True)  5.46 us
    all_to_all x1, starting transfers between devices, local(): moments = lax.all_to_all(moments, ('slab', 'brick'), 0, 0, tiled=True)  2.93 us
    ppermute x5, waiting for transfers between devices, swap(): lax.ppermute(near, axis, [(i, i + (-1 if i % 2 else 1)) for i in range(co...  2 us
    ppermute x5, starting transfers between devices, swap(): lax.ppermute(near, axis, [(i, i + (-1 if i % 2 else 1)) for i in range(co...  0.8 us
  transfers between devices with their start and end apart: 11, of which 7 were waited for; matrix products, arithmetic and copies ran while one was open for 0% of the time, Pallas kernels for 9%

profile of v9, /device:TPU:0, one launch (start us, length us, event | category | flops | bytes accessed | tf_op | source)
XLA Modules:
  0.0 36.4 jit_solution(6926183158120951629)
XLA Ops:
  0.7 1.3 %force_kernel.1 = (f32[54,8,128]{2,1,0:T(8,128)S(1)}, bf16[27,4,128]{2,1,0:T(4,128)(2,1)S(1)}, bf16[27,4,128]{2,1,0:T(4,128)(2,1)S(1)}, f32[4,8,128]{2,1,0:T(8,128)S(1)}, f32[9,8,128]{2,1,0:T(8,128)S(1)}) custom-call(bf16[324,8,128]{2,1,0:T(8,128)(2,1)} %bitcast.13, f32[4,8,128]{2,1,0:T(8,128)} %bitcast.24, f32[4,8,128]{2,1,0:T(8,128)} %bitcast.19, ...), custom_call_target="tpu_custom_call" | custom-call | flops 100000 | bytes 1138688 | tf_op jit(solution)/shard_map/force_kernel/pallas_call | solution.py:591
  2.0 3.4 %collective-permute-start = (bf16[27,4,128]{2,1,0:T(4,128)(2,1)S(1)}, bf16[27,4,128]{2,1,0:T(4,128)(2,1)S(1)}, u32[]{:S(2)}, u32[]{:S(2)}) collective-permute-start(bf16[27,4,128]{2,1,0:T(4,128)(2,1)S(1)} %get-tuple-element.29), channel_id=1, source_target_pairs={{0,28},{4,8},{8,4},{12,16},{16,12},{20,24},{24,20},{28,0},{1,29},{... | collective-permute-start | bytes 82952 | tf_op jit(solution)/shard_map/ppermute | solution.py:605
  5.4 0.0 collective-permute-start.1
  5.4 1.3 %spread_kernel.1 = (f32[36,8,128]{2,1,0:T(8,128)S(1)}, f32[56,8,128]{2,1,0:T(8,128)S(1)}, bf16[79,2,128]{2,1,0:T(2,128)(2,1)S(1)}, bf16[79,2,128]{2,1,0:T(2,128)(2,1)S(1)}) custom-call(bf16[324,8,128]{2,1,0:T(8,128)(2,1)} %bitcast.14, f32[3,2,8,257]{3,2,1,0:T(8,128)S(1)} %copy-done.2, f32[4,8,128]{2,1,0:T(8,128)S(1)} %get-tuple-element.31.pressure_in, ...), custom_call_target="tpu_custom_call" | custom-call | flops 100000 | bytes 1360064 | tf_op jit(solution)/shard_map/spread_kernel/pallas_call | solution.py:591
  6.7 0.2 collective-permute-done.far
  6.9 0.1 rim_kernel.1
  7.1 4.6 %collective-permute-start.2 = (bf16[79,2,128]{2,1,0:T(2,128)(2,1)S(1)}, bf16[79,2,128]{2,1,0:T(2,128)(2,1)S(1)}, u32[]{:S(2)}, u32[]{:S(2)}) collective-permute-start(bf16[79,2,128]{2,1,0:T(2,128)(2,1)S(1)} %get-tuple-element.37), channel_id=1, source_target_pairs={{0,3},{1,2},{2,1},{3,0},{4,7},{5,6},{6,5},{7,4},{8,11},{9,10},{10,... | collective-permute-start | bytes 121352 | tf_op jit(solution)/shard_map/ppermute | solution.py:605
  11.7 0.0 collective-permute-start.3
  11.7 2.0 %collective-permute-done.2.far_in = bf16[79,2,128]{2,1,0:T(2,128)(2,1)S(1)} collective-permute-done((bf16[79,2,128]{2,1,0:T(2,128)(2,1)S(1)}, bf16[79,2,128]{2,1,0:T(2,128)(2,1)S(1)}, u32[]{:S(2)}, u32[]{:S(2)}) %collective-permute-start.2) | collective-permute-done | bytes 40480 | tf_op jit(solution)/shard_map/ppermute | solution.py:605
  13.7 2.0 %collective-permute-done.3.near_in = bf16[79,2,128]{2,1,0:T(2,128)(2,1)S(1)} collective-permute-done((bf16[79,2,128]{2,1,0:T(2,128)(2,1)S(1)}, bf16[79,2,128]{2,1,0:T(2,128)(2,1)S(1)}, u32[]{:S(2)}, u32[]{:S(2)}) %collective-permute-start.3) | collective-permute-done | bytes 40480 | tf_op jit(solution)/shard_map/ppermute | solution.py:606
  15.7 0.4 %first_kernel.1 = (f32[54,8,128]{2,1,0:T(8,128)S(1)}, f32[27,8,128]{2,1,0:T(8,128)S(1)}, f32[54,8,128]{2,1,0:T(8,128)S(1)}, bf16[13,8,128]{2,1,0:T(8,128)(2,1)S(1)}, bf16[13,8,128]{2,1,0:T(8,128)(2,1)S(1)}) custom-call(f32[55,8,128]{2,1,0:T(8,128)S(1)} %get-tuple-element.36.own, bf16[79,2,128]{2,1,0:T(2,128)(2,1)S(1)} %collective-permute-done.2.far_in, ...), custom_call_target="tpu_custom_call" | custom-call | flops 100000 | bytes 1020928 | tf_op jit(solution)/shard_map/first_kernel/pallas_call | solution.py:591
  16.1 0.3 collective-permute-start.4
  16.4 0.4 %collective-permute-start.5 = (bf16[13,8,128]{2,1,0:T(8,128)(2,1)S(1)}, bf16[13,8,128]{2,1,0:T(8,128)(2,1)S(1)}, u32[]{:S(2)}, u32[]{:S(2)}) collective-permute-start(bf16[13,8,128]{2,1,0:T(8,128)(2,1)S(1)} %get-tuple-element.41), channel_id=1, source_target_pairs={{0,4},{4,0},{8,12},{12,8},{16,20},{20,16},{24,28},{28,24},{1,5},{5... | collective-permute-start | bytes 79880 | tf_op jit(solution)/shard_map/ppermute | solution.py:606
  16.8 0.2 speed_kernel.1
  17.0 2.0 %collective-permute-start.8 = (bf16[10,8,128]{2,1,0:T(8,128)(2,1)S(1)}, bf16[10,8,128]{2,1,0:T(8,128)(2,1)S(1)}, u32[]{:S(2)}, u32[]{:S(2)}) collective-permute-start(bf16[10,8,128]{2,1,0:T(8,128)(2,1)S(1)} %get-tuple-element.50), channel_id=1, source_target_pairs={{0,28},{4,8},{8,4},{12,16},{16,12},{20,24},{24,20},{28,0},{1,29},{... | collective-permute-start | bytes 61448 | tf_op jit(solution)/shard_map/ppermute | solution.py:605
  19.0 0.4 %collective-permute-start.9 = (bf16[10,8,128]{2,1,0:T(8,128)(2,1)S(1)}, bf16[10,8,128]{2,1,0:T(8,128)(2,1)S(1)}, u32[]{:S(2)}, u32[]{:S(2)}) collective-permute-start(bf16[10,8,128]{2,1,0:T(8,128)(2,1)S(1)} %get-tuple-element.51), channel_id=1, source_target_pairs={{0,4},{4,0},{8,12},{12,8},{16,20},{20,16},{24,28},{28,24},{1,5},{5... | collective-permute-start | bytes 61448 | tf_op jit(solution)/shard_map/ppermute | solution.py:606
  19.3 1.0 %collective-permute-done.4.far_in = bf16[13,8,128]{2,1,0:T(8,128)(2,1)S(1)} collective-permute-done((bf16[13,8,128]{2,1,0:T(8,128)(2,1)S(1)}, bf16[13,8,128]{2,1,0:T(8,128)(2,1)S(1)}, u32[]{:S(2)}, u32[]{:S(2)}) %collective-permute-start.4) | collective-permute-done | bytes 26656 | tf_op jit(solution)/shard_map/ppermute | solution.py:605
  20.3 0.3 second_kernel.1
  20.6 0.0 copy-start
  20.6 0.3 collective-permute-start.6
  20.9 0.0 collective-permute-start.7
  20.9 0.1 collective-permute-done.8.far_speed.far
  21.1 0.0 collective-permute-done.9.near_speed.near
  21.1 0.1 product_kernel.1.products
  21.2 3.6 %collective-permute-done.6.far = bf16[8,8,128]{2,1,0:T(8,128)(2,1)S(1)} collective-permute-done((bf16[8,8,128]{2,1,0:T(8,128)(2,1)S(1)}, bf16[8,8,128]{2,1,0:T(8,128)(2,1)S(1)}, u32[]{:S(2)}, u32[]{:S(2)}) %collective-permute-start.6) | collective-permute-done | bytes 16416 | tf_op jit(solution)/shard_map/ppermute | solution.py:605
  24.7 0.0 collective-permute-done.7.near
  24.7 0.9 %moment_kernel.1 = (f32[54,8,128]{2,1,0:T(8,128)S(1)}, f32[32,128]{1,0:T(8,128)}) custom-call(f32[54,8,128]{2,1,0:T(8,128)S(1)} %get-tuple-element.45.image, bf16[8,8,128]{2,1,0:T(8,128)(2,1)S(1)} %collective-permute-done.6.far, bf16[8,8,128]{2,1,0:T(8,128)(2,1)S(1)} %collective-permute-done.7.near, f32[27,8,128]{2,1,0:T(8,128)S(1)} %get-tuple-element.42.weight, ...), custom_call_target="tpu_custom_call" | custom-call | flops 100000 | bytes 835584 | tf_op jit(solution)/shard_map/moment_kernel/pallas_call | solution.py:591
  25.6 2.9 %all-to-all-start = ((f32[32,1,128]{2,1,0:T(1,128)}), f32[32,1,128]{2,1,0:T(1,128)S(1)}, u32[]{:S(2)}, u32[]{:S(2)}) async-start(f32[32,1,128]{2,1,0:T(1,128)} %bitcast.6), calls=%async_computation | async-start | bytes 32768 | tf_op jit(solution)/shard_map/all_to_all | solution.py:685
  28.6 0.8 %work_kernel.1 = f32[4,8,128]{2,1,0:T(8,128)} custom-call(bf16[324,8,128]{2,1,0:T(8,128)(2,1)S(1)} %bitcast.15, f32[4,8,128]{2,1,0:T(8,128)S(1)} %get-tuple-element.31.pressure_in, f32[4,8,128]{2,1,0:T(8,128)S(1)} %bitcast.20, f32[4,8,128]{2,1,0:T(8,128)S(1)} %bitcast.22, f32[54,8,128]{2,1,0:T(8,128)S(1)} %get-tuple-element.44.speeds, ...), custom_call_target="tpu_custom_call" | custom-call | flops 100000 | bytes 991232 | tf_op jit(solution)/shard_map/work_kernel/pallas_call | solution.py:591
  29.4 0.8 %nodal_kernel.1.nodal = f32[3,48,384]{2,1,0:T(8,128)S(1)} custom-call(f32[54,8,128]{2,1,0:T(8,128)S(1)} %get-tuple-element.49.zeroth, f32[54,8,128]{2,1,0:T(8,128)S(1)} %get-tuple-element.48.first, f32[54,8,128]{2,1,0:T(8,128)S(1)} %get-tuple-element.53.second), custom_call_target="tpu_custom_call" | custom-call | flops 100000 | bytes 884736 | tf_op jit(solution)/shard_map/nodal_kernel/pallas_call | solution.py:591
  30.2 5.5 %all-to-all-done = f32[32,1,128]{2,1,0:T(1,128)S(1)} async-done(((f32[32,1,128]{2,1,0:T(1,128)}), f32[32,1,128]{2,1,0:T(1,128)S(1)}, u32[]{:S(2)}, u32[]{:S(2)}) %all-to-all-start) | async-done | bytes 16416 | tf_op jit(solution)/shard_map/all_to_all | solution.py:685
  35.6 0.8 %last_kernel.1 = f32[3,2,8,257]{3,2,1,0:T(8,128)} custom-call(f32[32,128]{1,0:T(8,128)S(1)} %bitcast.21, f32[3,48,384]{2,1,0:T(8,128)S(1)} %nodal_kernel.1.nodal, f32[3,2,8,257]{3,2,1,0:T(8,128)S(1)} %copy-done.2), custom_call_target="tpu_custom_call" | custom-call | flops 100000 | bytes 336256 | tf_op jit(solution)/shard_map/last_kernel/pallas_call | solution.py:591
  (11 shorter events, 0.0 us)
Async XLA Ops:
  0.6 4.7 %copy-start.1 = (f32[27,1,4,128]{3,2,1,0:T(4,128)S(1)}, f32[27,1,4,128]{3,2,1,0:T(4,128)}, u32[]{:S(2)}) copy-start(f32[27,1,4,128]{3,2,1,0:T(4,128)} %param.12) | copy-start | bytes 165892
  0.6 4.7 %copy-start.2 = (f32[3,2,8,257]{3,2,1,0:T(8,128)S(1)}, f32[3,2,8,257]{3,2,1,0:T(8,128)}, u32[]{:S(2)}) copy-start(f32[3,2,8,257]{3,2,1,0:T(8,128)} %velocity.3) | copy-start | bytes 148036
  2.0 4.9 %collective-permute-start = (bf16[27,4,128]{2,1,0:T(4,128)(2,1)S(1)}, bf16[27,4,128]{2,1,0:T(4,128)(2,1)S(1)}, u32[]{:S(2)}, u32[]{:S(2)}) collective-permute-start(bf16[27,4,128]{2,1,0:T(4,128)(2,1)S(1)} %get-tuple-element.29), channel_id=1, source_target_pairs={{0,28},{4,8},{8,4},{12,16},{16,12},{20,24},{24,20},{28,0},{1,29},{... | collective-permute-start | bytes 82952 | tf_op jit(solution)/shard_map/ppermute | solution.py:605
  5.4 1.6 %collective-permute-start.1 = (bf16[27,4,128]{2,1,0:T(4,128)(2,1)S(1)}, bf16[27,4,128]{2,1,0:T(4,128)(2,1)S(1)}, u32[]{:S(2)}, u32[]{:S(2)}) collective-permute-start(bf16[27,4,128]{2,1,0:T(4,128)(2,1)S(1)} %get-tuple-element.30), channel_id=1, source_target_pairs={{0,4},{4,0},{8,12},{12,8},{16,20},{20,16},{24,28},{28,24},{1,5},{5... | collective-permute-start | bytes 82952 | tf_op jit(solution)/shard_map/ppermute | solution.py:606
  7.1 6.6 %collective-permute-start.2 = (bf16[79,2,128]{2,1,0:T(2,128)(2,1)S(1)}, bf16[79,2,128]{2,1,0:T(2,128)(2,1)S(1)}, u32[]{:S(2)}, u32[]{:S(2)}) collective-permute-start(bf16[79,2,128]{2,1,0:T(2,128)(2,1)S(1)} %get-tuple-element.37), channel_id=1, source_target_pairs={{0,3},{1,2},{2,1},{3,0},{4,7},{5,6},{6,5},{7,4},{8,11},{9,10},{10,... | collective-permute-start | bytes 121352 | tf_op jit(solution)/shard_map/ppermute | solution.py:605
  11.7 4.0 %collective-permute-start.3 = (bf16[79,2,128]{2,1,0:T(2,128)(2,1)S(1)}, bf16[79,2,128]{2,1,0:T(2,128)(2,1)S(1)}, u32[]{:S(2)}, u32[]{:S(2)}) collective-permute-start(bf16[79,2,128]{2,1,0:T(2,128)(2,1)S(1)} %get-tuple-element.38), channel_id=1, source_target_pairs={{0,1},{1,0},{2,3},{3,2},{4,5},{5,4},{6,7},{7,6},{8,9},{9,8},{10,11... | collective-permute-start | bytes 121352 | tf_op jit(solution)/shard_map/ppermute | solution.py:606
  16.1 4.2 %collective-permute-start.4 = (bf16[13,8,128]{2,1,0:T(8,128)(2,1)S(1)}, bf16[13,8,128]{2,1,0:T(8,128)(2,1)S(1)}, u32[]{:S(2)}, u32[]{:S(2)}) collective-permute-start(bf16[13,8,128]{2,1,0:T(8,128)(2,1)S(1)} %get-tuple-element.40), channel_id=1, source_target_pairs={{0,28},{4,8},{8,4},{12,16},{16,12},{20,24},{24,20},{28,0},{1,29},{... | collective-permute-start | bytes 79880 | tf_op jit(solution)/shard_map/ppermute | solution.py:605
  16.4 3.9 %collective-permute-start.5 = (bf16[13,8,128]{2,1,0:T(8,128)(2,1)S(1)}, bf16[13,8,128]{2,1,0:T(8,128)(2,1)S(1)}, u32[]{:S(2)}, u32[]{:S(2)}) collective-permute-start(bf16[13,8,128]{2,1,0:T(8,128)(2,1)S(1)} %get-tuple-element.41), channel_id=1, source_target_pairs={{0,4},{4,0},{8,12},{12,8},{16,20},{20,16},{24,28},{28,24},{1,5},{5... | collective-permute-start | bytes 79880 | tf_op jit(solution)/shard_map/ppermute | solution.py:606
  17.0 4.1 %collective-permute-start.8 = (bf16[10,8,128]{2,1,0:T(8,128)(2,1)S(1)}, bf16[10,8,128]{2,1,0:T(8,128)(2,1)S(1)}, u32[]{:S(2)}, u32[]{:S(2)}) collective-permute-start(bf16[10,8,128]{2,1,0:T(8,128)(2,1)S(1)} %get-tuple-element.50), channel_id=1, source_target_pairs={{0,28},{4,8},{8,4},{12,16},{16,12},{20,24},{24,20},{28,0},{1,29},{... | collective-permute-start | bytes 61448 | tf_op jit(solution)/shard_map/ppermute | solution.py:605
  19.0 2.1 %collective-permute-start.9 = (bf16[10,8,128]{2,1,0:T(8,128)(2,1)S(1)}, bf16[10,8,128]{2,1,0:T(8,128)(2,1)S(1)}, u32[]{:S(2)}, u32[]{:S(2)}) collective-permute-start(bf16[10,8,128]{2,1,0:T(8,128)(2,1)S(1)} %get-tuple-element.51), channel_id=1, source_target_pairs={{0,4},{4,0},{8,12},{12,8},{16,20},{20,16},{24,28},{28,24},{1,5},{5... | collective-permute-start | bytes 61448 | tf_op jit(solution)/shard_map/ppermute | solution.py:606
  20.6 8.0 %copy-start = (bf16[81,8,1,4,128]{4,3,2,1,0:T(4,128)(2,1)S(1)}, bf16[81,8,1,4,128]{4,3,2,1,0:T(4,128)(2,1)}, u32[]{:S(2)}) copy-start(bf16[81,8,1,4,128]{4,3,2,1,0:T(4,128)(2,1)} %param.11) | copy-start | bytes 1990660
  20.6 4.1 %collective-permute-start.6 = (bf16[8,8,128]{2,1,0:T(8,128)(2,1)S(1)}, bf16[8,8,128]{2,1,0:T(8,128)(2,1)S(1)}, u32[]{:S(2)}, u32[]{:S(2)}) collective-permute-start(bf16[8,8,128]{2,1,0:T(8,128)(2,1)S(1)} %get-tuple-element.46), channel_id=1, source_target_pairs={{0,28},{4,8},{8,4},{12,16},{16,12},{20,24},{24,20},{28,0},{1,29},{... | collective-permute-start | bytes 49160 | tf_op jit(solution)/shard_map/ppermute | solution.py:605
  20.9 3.8 %collective-permute-start.7 = (bf16[8,8,128]{2,1,0:T(8,128)(2,1)S(1)}, bf16[8,8,128]{2,1,0:T(8,128)(2,1)S(1)}, u32[]{:S(2)}, u32[]{:S(2)}) collective-permute-start(bf16[8,8,128]{2,1,0:T(8,128)(2,1)S(1)} %get-tuple-element.47), channel_id=1, source_target_pairs={{0,4},{4,0},{8,12},{12,8},{16,20},{20,16},{24,28},{28,24},{1,5},{5... | collective-permute-start | bytes 49160 | tf_op jit(solution)/shard_map/ppermute | solution.py:606
  25.6 3.0 %copy-start.3 = (f32[8,1,4,128]{3,2,1,0:T(4,128)S(1)}, f32[8,1,4,128]{3,2,1,0:T(4,128)}, u32[]{:S(2)}) copy-start(f32[8,1,4,128]{3,2,1,0:T(4,128)} %param.8) | copy-start | bytes 49156
  25.6 3.0 %copy-start.4 = (f32[8,1,4,128]{3,2,1,0:T(4,128)S(1)}, f32[8,1,4,128]{3,2,1,0:T(4,128)}, u32[]{:S(2)}) copy-start(f32[8,1,4,128]{3,2,1,0:T(4,128)} %param.13) | copy-start | bytes 49156
  25.6 10.0 %all-to-all-start = ((f32[32,1,128]{2,1,0:T(1,128)}), f32[32,1,128]{2,1,0:T(1,128)S(1)}, u32[]{:S(2)}, u32[]{:S(2)}) async-start(f32[32,1,128]{2,1,0:T(1,128)} %bitcast.6), calls=%async_computation | async-start | bytes 32768 | tf_op jit(solution)/shard_map/all_to_all | solution.py:685

commit v10 on v9

--- a/solution.py
+++ b/solution.py
@@ -352,7 +352,7 @@
     send_planes(planes, near, far, even)
 
 
-def speed_kernel(far_in, near_in, spread, speeds, near, far):
+def speed_kernel(far_in, near_in, spread, speeds, plane_out):
     even_y = is_even("brick")
     row = lax.broadcasted_iota(jnp.int32, (8, 128), 0)
     lane = lane_of((8, 128))
@@ -378,8 +378,7 @@
                     tops = to_lane(tops, lane, speed[3 * b + 2], SPEED_LANE + 3 * comp + b)
     tiles = [jnp.where(row < OWN, plane[2 * k], pltpu.roll(plane[2 * k + 1], OWN, 0)) for k in range(9)]
     for k, value in enumerate(tiles + [tops]):
-        near[k] = value.astype(BF16)
-        far[k] = value.astype(BF16)
+        plane_out[k] = value.astype(BF16)
 
 
 def send_own(planes, near, far, even):
@@ -454,17 +453,17 @@
     send_own(planes, near, far, even)
 
 
-def work_kernel(geometry, pressure_in, energy, energy_mass, speeds, far, near, out):
+def work_kernel(geometry, pressure_in, energy, energy_mass, speeds, beyond, out):
     even = is_even()
     pressure = pressure_in[...]
     work = jnp.zeros_like(pressure)
     row = lax.broadcasted_iota(jnp.int32, (8, 128), 0)
     lane = lane_of((8, 128))
-    tops = get(near, far, 9, even)[1]
+    tops = beyond[9].astype(F32)
     for comp in range(3):
         speed = [speeds[18 * comp + n] for n in range(18)]
         for b in range(3):
-            both = get(near, far, 3 * comp + b, even)[1]
+            both = beyond[3 * comp + b].astype(F32)
             speed += [both, pltpu.roll(both, OWN, 0)]
             speed.append(third_along_z(both, tops, lane, SPEED_LANE + 3 * comp + b))
         for n in range(27):
@@ -483,7 +482,7 @@
     return total
 
 
-def product_kernel(zeroth, first, far_speed, near_speed, products):
+def product_kernel(zeroth, first, beyond, products):
     for k, (one, other) in enumerate([(zeroth, zeroth), (zeroth, first), (first, first)]):
         total = jnp.zeros((8, 128), F32)
         for comp in range(3):
@@ -661,13 +660,14 @@
         dtypes=[F32, F32, F32, BF16, BF16],
     )
     near, far = swap(near, far)
-    speeds, near_speed, far_speed = call(
+    speeds, plane = call(
         speed_kernel,
-        [(54,) + full, (10,) + full, (10,) + full],
+        [(54,) + full, (10,) + full],
         far_rim, near_rim, spread,
-        dtypes=[F32, BF16, BF16],
-    )
-    near_speed, far_speed = swap(near_speed, far_speed)
+        dtypes=[F32, BF16],
+    )
+    count = lax.axis_size("slab")
+    beyond = lax.ppermute(plane, "slab", [(i, (i - 1) % count) for i in range(count)])
     first, image, near, far = call(
         second_kernel,
         [(54,) + full, (54,) + full, (8,) + full, (8,) + full],
@@ -676,9 +676,9 @@
     )
     near, far = swap(near, far)
     (energy_half,) = call(
-        work_kernel, [(4,) + full], geometry, pressure, energy, energy_mass, speeds, far_speed, near_speed
-    )
-    (products,) = call(product_kernel, [(3,) + full], zeroth, first, far_speed, near_speed)
+        work_kernel, [(4,) + full], geometry, pressure, energy, energy_mass, speeds, beyond
+    )
+    (products,) = call(product_kernel, [(3,) + full], zeroth, first, beyond)
     second, moments = call(
         moment_kernel, [(54,) + full, (devices, 128)], image, far, near, weight, first, products
     )

time: 36.7 us -> 36.7 us (level)
  starting transfers between devices: 14.4 us -> 14 us
  waiting for transfers between devices: 14.4 us -> 14.8 us
    ppermute x5 -> x4, starting transfers between devices: 10.7 us -> 8.68 us  [swap(): lax.ppermute(far, axis, [(i, (i + (1 if i % 2 else -1)) % count) for i in...]
    ppermute x0 -> x1, starting transfers between devices: none -> 1.97 us  [local(): lax.ppermute(plane, 'slab', [(i, (i - 1) % count) for i in range(count)])]
    ppermute x5 -> x4, waiting for transfers between devices: 6.94 us -> 7.33 us  [swap(): lax.ppermute(far, axis, [(i, (i + (1 if i % 2 else -1)) % count) for i in...]
    ppermute x5 -> x4, starting transfers between devices: 0.8 us -> 0.43 us  [swap(): lax.ppermute(near, axis, [(i, i + (-1 if i % 2 else 1)) for i in range(co...]
    ppermute x5 -> x4, waiting for transfers between devices: 2 us -> 2 us  [swap(): lax.ppermute(near, axis, [(i, i + (-1 if i % 2 else 1)) for i in range(co...]
  transfers between devices with their start and end apart: 11 -> 10, of which waited for: 7 -> 6; matrix products, arithmetic and copies ran while one was open for 0% -> 0% of each run, Pallas kernels for 9% -> 9%
where the time goes in v10:
time: 36.7 us; the launch traced here: 36.4 us
  waiting for transfers between devices  14.8 us (40%)
  starting transfers between devices  14 us (38%)
  Pallas kernels  6.85 us (19%)
  between operations  0.74 us (2%)
    ppermute x4, starting transfers between devices, swap(): lax.ppermute(far, axis, [(i, (i + (1 if i % 2 else -1)) % count) for i in...  8.68 us
    ppermute x4, waiting for transfers between devices, swap(): lax.ppermute(far, axis, [(i, (i + (1 if i % 2 else -1)) % count) for i in...  7.33 us
    pallas_call x11, Pallas kernels, call(): pl.pallas_call(kernel, out_shape=shapes, in_specs=[HBM] * in_hbm + [VMEM]...  6.85 us
    all_to_all x1, waiting for transfers between devices, local(): moments = lax.all_to_all(moments, ('slab', 'brick'), 0, 0, tiled=True)  5.46 us
    all_to_all x1, starting transfers between devices, local(): moments = lax.all_to_all(moments, ('slab', 'brick'), 0, 0, tiled=True)  2.93 us
    ppermute x4, waiting for transfers between devices, swap(): lax.ppermute(near, axis, [(i, i + (-1 if i % 2 else 1)) for i in range(co...  2 us
    ppermute x1, starting transfers between devices, local(): lax.ppermute(plane, 'slab', [(i, (i - 1) % count) for i in range(count)])  1.97 us
  transfers between devices with their start and end apart: 10, of which 6 were waited for; matrix products, arithmetic and copies ran while one was open for 0% of the time, Pallas kernels for 9%

profile of v10, /device:TPU:0, one launch (start us, length us, event | category | flops | bytes accessed | tf_op | source)
XLA Modules:
  0.0 36.4 jit_solution(10869449392433481360)
XLA Ops:
  0.7 1.3 %force_kernel.1 = (f32[54,8,128]{2,1,0:T(8,128)S(1)}, bf16[27,4,128]{2,1,0:T(4,128)(2,1)S(1)}, bf16[27,4,128]{2,1,0:T(4,128)(2,1)S(1)}, f32[4,8,128]{2,1,0:T(8,128)S(1)}, f32[9,8,128]{2,1,0:T(8,128)S(1)}) custom-call(bf16[324,8,128]{2,1,0:T(8,128)(2,1)} %bitcast.13, f32[4,8,128]{2,1,0:T(8,128)} %bitcast.24, f32[4,8,128]{2,1,0:T(8,128)} %bitcast.19, ...), custom_call_target="tpu_custom_call" | custom-call | flops 100000 | bytes 1138688 | tf_op jit(solution)/shard_map/force_kernel/pallas_call | solution.py:590
  2.0 3.4 %collective-permute-start = (bf16[27,4,128]{2,1,0:T(4,128)(2,1)S(1)}, bf16[27,4,128]{2,1,0:T(4,128)(2,1)S(1)}, u32[]{:S(2)}, u32[]{:S(2)}) collective-permute-start(bf16[27,4,128]{2,1,0:T(4,128)(2,1)S(1)} %get-tuple-element.28), channel_id=1, source_target_pairs={{0,28},{4,8},{8,4},{12,16},{16,12},{20,24},{24,20},{28,0},{1,29},{... | collective-permute-start | bytes 82952 | tf_op jit(solution)/shard_map/ppermute | solution.py:604
  5.4 0.0 collective-permute-start.1
  5.4 1.3 %spread_kernel.1 = (f32[36,8,128]{2,1,0:T(8,128)S(1)}, f32[56,8,128]{2,1,0:T(8,128)S(1)}, bf16[79,2,128]{2,1,0:T(2,128)(2,1)S(1)}, bf16[79,2,128]{2,1,0:T(2,128)(2,1)S(1)}) custom-call(bf16[324,8,128]{2,1,0:T(8,128)(2,1)} %bitcast.14, f32[3,2,8,257]{3,2,1,0:T(8,128)S(1)} %copy-done.2, f32[4,8,128]{2,1,0:T(8,128)S(1)} %get-tuple-element.30.pressure_in, ...), custom_call_target="tpu_custom_call" | custom-call | flops 100000 | bytes 1360064 | tf_op jit(solution)/shard_map/spread_kernel/pallas_call | solution.py:590
  6.7 0.2 collective-permute-done.far
  6.9 0.0 collective-permute-done.1.near
  6.9 0.1 rim_kernel.1
  7.1 4.6 %collective-permute-start.2 = (bf16[79,2,128]{2,1,0:T(2,128)(2,1)S(1)}, bf16[79,2,128]{2,1,0:T(2,128)(2,1)S(1)}, u32[]{:S(2)}, u32[]{:S(2)}) collective-permute-start(bf16[79,2,128]{2,1,0:T(2,128)(2,1)S(1)} %get-tuple-element.36), channel_id=1, source_target_pairs={{0,3},{1,2},{2,1},{3,0},{4,7},{5,6},{6,5},{7,4},{8,11},{9,10},{10,... | collective-permute-start | bytes 121352 | tf_op jit(solution)/shard_map/ppermute | solution.py:604
  11.7 0.0 collective-permute-start.3
  11.7 2.0 %collective-permute-done.2.far_in = bf16[79,2,128]{2,1,0:T(2,128)(2,1)S(1)} collective-permute-done((bf16[79,2,128]{2,1,0:T(2,128)(2,1)S(1)}, bf16[79,2,128]{2,1,0:T(2,128)(2,1)S(1)}, u32[]{:S(2)}, u32[]{:S(2)}) %collective-permute-start.2) | collective-permute-done | bytes 40480 | tf_op jit(solution)/shard_map/ppermute | solution.py:604
  13.7 2.0 %collective-permute-done.3.near_in = bf16[79,2,128]{2,1,0:T(2,128)(2,1)S(1)} collective-permute-done((bf16[79,2,128]{2,1,0:T(2,128)(2,1)S(1)}, bf16[79,2,128]{2,1,0:T(2,128)(2,1)S(1)}, u32[]{:S(2)}, u32[]{:S(2)}) %collective-permute-start.3) | collective-permute-done | bytes 40480 | tf_op jit(solution)/shard_map/ppermute | solution.py:605
  15.7 0.4 %first_kernel.1 = (f32[54,8,128]{2,1,0:T(8,128)S(1)}, f32[27,8,128]{2,1,0:T(8,128)S(1)}, f32[54,8,128]{2,1,0:T(8,128)S(1)}, bf16[13,8,128]{2,1,0:T(8,128)(2,1)S(1)}, bf16[13,8,128]{2,1,0:T(8,128)(2,1)S(1)}) custom-call(f32[55,8,128]{2,1,0:T(8,128)S(1)} %get-tuple-element.35.own, bf16[79,2,128]{2,1,0:T(2,128)(2,1)S(1)} %collective-permute-done.2.far_in, ...), custom_call_target="tpu_custom_call" | custom-call | flops 100000 | bytes 1020928 | tf_op jit(solution)/shard_map/first_kernel/pallas_call | solution.py:590
  16.1 0.3 collective-permute-start.4
  16.4 0.4 %collective-permute-start.5 = (bf16[13,8,128]{2,1,0:T(8,128)(2,1)S(1)}, bf16[13,8,128]{2,1,0:T(8,128)(2,1)S(1)}, u32[]{:S(2)}, u32[]{:S(2)}) collective-permute-start(bf16[13,8,128]{2,1,0:T(8,128)(2,1)S(1)} %get-tuple-element.40), channel_id=1, source_target_pairs={{0,4},{4,0},{8,12},{12,8},{16,20},{20,16},{24,28},{28,24},{1,5},{5... | collective-permute-start | bytes 79880 | tf_op jit(solution)/shard_map/ppermute | solution.py:605
  16.8 0.2 speed_kernel.1
  17.0 2.0 %collective-permute-start.8 = (bf16[10,8,128]{2,1,0:T(8,128)(2,1)S(1)}, bf16[10,8,128]{2,1,0:T(8,128)(2,1)S(1)}, u32[]{:S(2)}, u32[]{:S(2)}) collective-permute-start(bf16[10,8,128]{2,1,0:T(8,128)(2,1)S(1)} %get-tuple-element.49), channel_id=1, source_target_pairs={{0,28},{4,0},{8,4},{12,8},{16,12},{20,16},{24,20},{28,24},{1,29},{... | collective-permute-start | bytes 61448 | tf_op jit(solution)/shard_map/ppermute | solution.py:670
  18.9 1.4 %collective-permute-done.4.far_in = bf16[13,8,128]{2,1,0:T(8,128)(2,1)S(1)} collective-permute-done((bf16[13,8,128]{2,1,0:T(8,128)(2,1)S(1)}, bf16[13,8,128]{2,1,0:T(8,128)(2,1)S(1)}, u32[]{:S(2)}, u32[]{:S(2)}) %collective-permute-start.4) | collective-permute-done | bytes 26656 | tf_op jit(solution)/shard_map/ppermute | solution.py:604
  20.3 0.0 collective-permute-done.5.near_in
  20.3 0.3 second_kernel.1
  20.6 0.0 copy-start
  20.6 0.3 collective-permute-start.6
  20.9 0.0 collective-permute-start.7
  20.9 0.0 collective-permute-done.8.beyond
  20.9 0.1 product_kernel.1.products
  21.0 3.7 %collective-permute-done.6.far = bf16[8,8,128]{2,1,0:T(8,128)(2,1)S(1)} collective-permute-done((bf16[8,8,128]{2,1,0:T(8,128)(2,1)S(1)}, bf16[8,8,128]{2,1,0:T(8,128)(2,1)S(1)}, u32[]{:S(2)}, u32[]{:S(2)}) %collective-permute-start.6) | collective-permute-done | bytes 16416 | tf_op jit(solution)/shard_map/ppermute | solution.py:604
  24.7 0.0 collective-permute-done.7.near
  24.7 0.9 %moment_kernel.1 = (f32[54,8,128]{2,1,0:T(8,128)S(1)}, f32[32,128]{1,0:T(8,128)}) custom-call(f32[54,8,128]{2,1,0:T(8,128)S(1)} %get-tuple-element.44.image, bf16[8,8,128]{2,1,0:T(8,128)(2,1)S(1)} %collective-permute-done.6.far, bf16[8,8,128]{2,1,0:T(8,128)(2,1)S(1)} %collective-permute-done.7.near, f32[27,8,128]{2,1,0:T(8,128)S(1)} %get-tuple-element.41.weight, ...), custom_call_target="tpu_custom_call" | custom-call | flops 100000 | bytes 835584 | tf_op jit(solution)/shard_map/moment_kernel/pallas_call | solution.py:590
  25.6 2.9 %all-to-all-start = ((f32[32,1,128]{2,1,0:T(1,128)}), f32[32,1,128]{2,1,0:T(1,128)S(1)}, u32[]{:S(2)}, u32[]{:S(2)}) async-start(f32[32,1,128]{2,1,0:T(1,128)} %bitcast.6), calls=%async_computation | async-start | bytes 32768 | tf_op jit(solution)/shard_map/all_to_all | solution.py:685
  28.6 0.8 %work_kernel.1 = f32[4,8,128]{2,1,0:T(8,128)} custom-call(bf16[324,8,128]{2,1,0:T(8,128)(2,1)S(1)} %bitcast.15, f32[4,8,128]{2,1,0:T(8,128)S(1)} %get-tuple-element.30.pressure_in, f32[4,8,128]{2,1,0:T(8,128)S(1)} %bitcast.20, f32[4,8,128]{2,1,0:T(8,128)S(1)} %bitcast.22, f32[54,8,128]{2,1,0:T(8,128)S(1)} %get-tuple-element.43.speeds, ...), custom_call_target="tpu_custom_call" | custom-call | flops 100000 | bytes 970752 | tf_op jit(solution)/shard_map/work_kernel/pallas_call | solution.py:590
  29.4 0.8 %nodal_kernel.1.nodal = f32[3,48,384]{2,1,0:T(8,128)S(1)} custom-call(f32[54,8,128]{2,1,0:T(8,128)S(1)} %get-tuple-element.48.zeroth, f32[54,8,128]{2,1,0:T(8,128)S(1)} %get-tuple-element.47.first, f32[54,8,128]{2,1,0:T(8,128)S(1)} %get-tuple-element.51.second), custom_call_target="tpu_custom_call" | custom-call | flops 100000 | bytes 884736 | tf_op jit(solution)/shard_map/nodal_kernel/pallas_call | solution.py:590
  30.2 5.5 %all-to-all-done = f32[32,1,128]{2,1,0:T(1,128)S(1)} async-done(((f32[32,1,128]{2,1,0:T(1,128)}), f32[32,1,128]{2,1,0:T(1,128)S(1)}, u32[]{:S(2)}, u32[]{:S(2)}) %all-to-all-start) | async-done | bytes 16416 | tf_op jit(solution)/shard_map/all_to_all | solution.py:685
  35.6 0.8 %last_kernel.1 = f32[3,2,8,257]{3,2,1,0:T(8,128)} custom-call(f32[32,128]{1,0:T(8,128)S(1)} %bitcast.21, f32[3,48,384]{2,1,0:T(8,128)S(1)} %nodal_kernel.1.nodal, f32[3,2,8,257]{3,2,1,0:T(8,128)S(1)} %copy-done.2), custom_call_target="tpu_custom_call" | custom-call | flops 100000 | bytes 336256 | tf_op jit(solution)/shard_map/last_kernel/pallas_call | solution.py:590
  (9 shorter events, 0.0 us)
Async XLA Ops:
  0.6 4.7 %copy-start.1 = (f32[27,1,4,128]{3,2,1,0:T(4,128)S(1)}, f32[27,1,4,128]{3,2,1,0:T(4,128)}, u32[]{:S(2)}) copy-start(f32[27,1,4,128]{3,2,1,0:T(4,128)} %param.12) | copy-start | bytes 165892
  0.6 4.7 %copy-start.2 = (f32[3,2,8,257]{3,2,1,0:T(8,128)S(1)}, f32[3,2,8,257]{3,2,1,0:T(8,128)}, u32[]{:S(2)}) copy-start(f32[3,2,8,257]{3,2,1,0:T(8,128)} %velocity.3) | copy-start | bytes 148036
  2.0 4.9 %collective-permute-start = (bf16[27,4,128]{2,1,0:T(4,128)(2,1)S(1)}, bf16[27,4,128]{2,1,0:T(4,128)(2,1)S(1)}, u32[]{:S(2)}, u32[]{:S(2)}) collective-permute-start(bf16[27,4,128]{2,1,0:T(4,128)(2,1)S(1)} %get-tuple-element.28), channel_id=1, source_target_pairs={{0,28},{4,8},{8,4},{12,16},{16,12},{20,24},{24,20},{28,0},{1,29},{... | collective-permute-start | bytes 82952 | tf_op jit(solution)/shard_map/ppermute | solution.py:604
  5.4 1.6 %collective-permute-start.1 = (bf16[27,4,128]{2,1,0:T(4,128)(2,1)S(1)}, bf16[27,4,128]{2,1,0:T(4,128)(2,1)S(1)}, u32[]{:S(2)}, u32[]{:S(2)}) collective-permute-start(bf16[27,4,128]{2,1,0:T(4,128)(2,1)S(1)} %get-tuple-element.29), channel_id=1, source_target_pairs={{0,4},{4,0},{8,12},{12,8},{16,20},{20,16},{24,28},{28,24},{1,5},{5... | collective-permute-start | bytes 82952 | tf_op jit(solution)/shard_map/ppermute | solution.py:605
  7.1 6.6 %collective-permute-start.2 = (bf16[79,2,128]{2,1,0:T(2,128)(2,1)S(1)}, bf16[79,2,128]{2,1,0:T(2,128)(2,1)S(1)}, u32[]{:S(2)}, u32[]{:S(2)}) collective-permute-start(bf16[79,2,128]{2,1,0:T(2,128)(2,1)S(1)} %get-tuple-element.36), channel_id=1, source_target_pairs={{0,3},{1,2},{2,1},{3,0},{4,7},{5,6},{6,5},{7,4},{8,11},{9,10},{10,... | collective-permute-start | bytes 121352 | tf_op jit(solution)/shard_map/ppermute | solution.py:604
  11.7 4.0 %collective-permute-start.3 = (bf16[79,2,128]{2,1,0:T(2,128)(2,1)S(1)}, bf16[79,2,128]{2,1,0:T(2,128)(2,1)S(1)}, u32[]{:S(2)}, u32[]{:S(2)}) collective-permute-start(bf16[79,2,128]{2,1,0:T(2,128)(2,1)S(1)} %get-tuple-element.37), channel_id=1, source_target_pairs={{0,1},{1,0},{2,3},{3,2},{4,5},{5,4},{6,7},{7,6},{8,9},{9,8},{10,11... | collective-permute-start | bytes 121352 | tf_op jit(solution)/shard_map/ppermute | solution.py:605
  16.1 4.2 %collective-permute-start.4 = (bf16[13,8,128]{2,1,0:T(8,128)(2,1)S(1)}, bf16[13,8,128]{2,1,0:T(8,128)(2,1)S(1)}, u32[]{:S(2)}, u32[]{:S(2)}) collective-permute-start(bf16[13,8,128]{2,1,0:T(8,128)(2,1)S(1)} %get-tuple-element.39), channel_id=1, source_target_pairs={{0,28},{4,8},{8,4},{12,16},{16,12},{20,24},{24,20},{28,0},{1,29},{... | collective-permute-start | bytes 79880 | tf_op jit(solution)/shard_map/ppermute | solution.py:604
  16.4 3.9 %collective-permute-start.5 = (bf16[13,8,128]{2,1,0:T(8,128)(2,1)S(1)}, bf16[13,8,128]{2,1,0:T(8,128)(2,1)S(1)}, u32[]{:S(2)}, u32[]{:S(2)}) collective-permute-start(bf16[13,8,128]{2,1,0:T(8,128)(2,1)S(1)} %get-tuple-element.40), channel_id=1, source_target_pairs={{0,4},{4,0},{8,12},{12,8},{16,20},{20,16},{24,28},{28,24},{1,5},{5... | collective-permute-start | bytes 79880 | tf_op jit(solution)/shard_map/ppermute | solution.py:605
  17.0 4.0 %collective-permute-start.8 = (bf16[10,8,128]{2,1,0:T(8,128)(2,1)S(1)}, bf16[10,8,128]{2,1,0:T(8,128)(2,1)S(1)}, u32[]{:S(2)}, u32[]{:S(2)}) collective-permute-start(bf16[10,8,128]{2,1,0:T(8,128)(2,1)S(1)} %get-tuple-element.49), channel_id=1, source_target_pairs={{0,28},{4,0},{8,4},{12,8},{16,12},{20,16},{24,20},{28,24},{1,29},{... | collective-permute-start | bytes 61448 | tf_op jit(solution)/shard_map/ppermute | solution.py:670
  20.6 8.0 %copy-start = (bf16[81,8,1,4,128]{4,3,2,1,0:T(4,128)(2,1)S(1)}, bf16[81,8,1,4,128]{4,3,2,1,0:T(4,128)(2,1)}, u32[]{:S(2)}) copy-start(bf16[81,8,1,4,128]{4,3,2,1,0:T(4,128)(2,1)} %param.11) | copy-start | bytes 1990660
  20.6 4.1 %collective-permute-start.6 = (bf16[8,8,128]{2,1,0:T(8,128)(2,1)S(1)}, bf16[8,8,128]{2,1,0:T(8,128)(2,1)S(1)}, u32[]{:S(2)}, u32[]{:S(2)}) collective-permute-start(bf16[8,8,128]{2,1,0:T(8,128)(2,1)S(1)} %get-tuple-element.45), channel_id=1, source_target_pairs={{0,28},{4,8},{8,4},{12,16},{16,12},{20,24},{24,20},{28,0},{1,29},{... | collective-permute-start | bytes 49160 | tf_op jit(solution)/shard_map/ppermute | solution.py:604
  20.9 3.8 %collective-permute-start.7 = (bf16[8,8,128]{2,1,0:T(8,128)(2,1)S(1)}, bf16[8,8,128]{2,1,0:T(8,128)(2,1)S(1)}, u32[]{:S(2)}, u32[]{:S(2)}) collective-permute-start(bf16[8,8,128]{2,1,0:T(8,128)(2,1)S(1)} %get-tuple-element.46), channel_id=1, source_target_pairs={{0,4},{4,0},{8,12},{12,8},{16,20},{20,16},{24,28},{28,24},{1,5},{5... | collective-permute-start | bytes 49160 | tf_op jit(solution)/shard_map/ppermute | solution.py:605
  25.6 3.0 %copy-start.3 = (f32[8,1,4,128]{3,2,1,0:T(4,128)S(1)}, f32[8,1,4,128]{3,2,1,0:T(4,128)}, u32[]{:S(2)}) copy-start(f32[8,1,4,128]{3,2,1,0:T(4,128)} %param.8) | copy-start | bytes 49156
  25.6 3.0 %copy-start.4 = (f32[8,1,4,128]{3,2,1,0:T(4,128)S(1)}, f32[8,1,4,128]{3,2,1,0:T(4,128)}, u32[]{:S(2)}) copy-start(f32[8,1,4,128]{3,2,1,0:T(4,128)} %param.13) | copy-start | bytes 49156
  25.6 10.0 %all-to-all-start = ((f32[32,1,128]{2,1,0:T(1,128)}), f32[32,1,128]{2,1,0:T(1,128)S(1)}, u32[]{:S(2)}, u32[]{:S(2)}) async-start(f32[32,1,128]{2,1,0:T(1,128)} %bitcast.6), calls=%async_computation | async-start | bytes 32768 | tf_op jit(solution)/shard_map/all_to_all | solution.py:685
